TPU v7x, 32 devices: a whole 2x2x4 slice. The times are simulated.
32 devices in a mesh: site: 4 (over z), bond: 8 (over y, x, core).
Axes of the slice: x: 2, y: 2, z: 4, core: 2. Of those that a mesh axis runs over, the one named last changes fastest.
Arguments:
- left_env: float32 [4, 512, 16, 512], P('site', 'bond'), may hold values from -6 to 6
- right_env: float32 [4, 512, 16, 512], P('site', 'bond'), may hold values from -6 to 6
- left_site: float32 [4, 512, 4, 512], P('site'), may hold values from -0.125 to 0.125
- right_site: float32 [4, 512, 4, 512], P('site'), may hold values from -0.125 to 0.125
- left_mpo: float32 [4, 16, 16, 4, 4], P('site'), may hold values from -1.5 to 1.5
- right_mpo: float32 [4, 16, 16, 4, 4], P('site'), may hold values from -1.5 to 1.5
Outputs:
- new_left: float32 [4, 512, 16, 512], P('site', 'bond')
- new_right: float32 [4, 512, 16, 512], P('site', 'bond')
All inputs are finite; a program needn't handle non-finite values.
Results may differ from a plain program's by a relative error of at most 0.0001.
Values sent between devices are 32-bit elements; how exact they have to be, the bound alone decides.
No kernel may reach another device: no remote copies, remote signals or barrier semaphores. Data moves between devices by JAX's collectives and lax.ppermute only.
A program may use at most 128 MiB of HBM per device.

v0:
```python
import jax
import jax.numpy as jnp
from jax import lax
from jax.sharding import PartitionSpec as P


def passed_along(block, axis, distance):
    devices = range(lax.axis_size(axis))
    route = [(i - distance, i) for i in devices if i - distance in devices]
    return lax.ppermute(block, axis, route)


def finish_env(first_part, tensor, operator, rows_dev):
    depth = tensor.shape[0]
    states = tensor.shape[1]
    width = operator.shape[0]
    shaped = first_part.reshape(width, depth, states, rows_dev)
    second_part = jnp.einsum("wcsb,wvst->bvct", shaped, operator, precision=lax.Precision.HIGHEST)
    result = jnp.dot(
        second_part.reshape(rows_dev * width, depth * states),
        tensor.reshape(depth * states, depth),
        precision=lax.Precision.HIGHEST,
    )
    return result.reshape(rows_dev, width, depth)


def grow_rows(environ, tensor, position):
    rows_dev = environ.shape[0]
    width = environ.shape[1]
    depth = environ.shape[2]
    states = tensor.shape[1]
    columns = lax.dynamic_slice_in_dim(tensor, position * rows_dev, rows_dev, 2).reshape(
        depth, states * rows_dev
    )

    def add_piece(carry, piece, start):
        count = piece.shape[0]
        return lax.dot_general(
            piece.reshape(count, width * depth),
            columns,
            (((0,), (0,)), ((), ())),
            precision=lax.Precision.HIGHEST,
        )

    return (add_piece, jnp.zeros((width * depth, states * rows_dev), jnp.float32))


def local(left_env, right_env, left_site, right_site, left_mpo, right_mpo):
    position = lax.axis_index("bond")
    left_environ = left_env[0]
    right_environ = right_env[0]
    left_tensor = left_site[0]
    right_tensor = right_site[0]
    left_operator = left_mpo[0]
    right_operator = jnp.transpose(right_mpo[0], (1, 0, 2, 3))
    rows_dev = left_environ.shape[0]
    add_left, zero_left = grow_rows(left_environ, left_tensor, position)
    left_first = add_left(
        zero_left, lax.all_gather(left_environ, "bond", axis=0, tiled=True), jnp.int32(0)
    )
    grown_left = finish_env(left_first, left_tensor, left_operator, rows_dev)
    add_right, zero_right = grow_rows(right_environ, right_tensor, position)
    right_first = add_right(
        zero_right, lax.all_gather(right_environ, "bond", axis=0, tiled=True), jnp.int32(0)
    )
    grown_right = finish_env(right_first, right_tensor, right_operator, rows_dev)
    segment = lax.axis_index("site")
    last_segment = lax.axis_size("site") - 1
    from_left = passed_along(grown_left, "site", 1)
    from_right = passed_along(grown_right, "site", -1)
    new_left = jnp.where(segment == 0, left_environ, from_left)
    new_right = jnp.where(segment == last_segment, right_environ, from_right)
    return (new_left[None], new_right[None])


def solution(mesh):
    return jax.shard_map(
        local,
        mesh=mesh,
        in_specs=(
            P("site", "bond", None, None),
            P("site", "bond", None, None),
            P("site", None, None, None),
            P("site", None, None, None),
            P("site", None, None, None, None),
            P("site", None, None, None, None),
        ),
        out_specs=(P("site", "bond", None, None), P("site", "bond", None, None)),
        check_vma=False,
    )
```

profile of v0, /device:TPU:0, one launch (start us, length us, event | category | flops | bytes accessed | tf_op | source)
XLA Modules:
  0.0 369.2 jit_solution(5574550125530846266)
XLA Ops:
  7.9 0.7 all-gather.7.cloned.1.call-update
  8.7 5.3 %reshape.47 = f32[2048,512,1]{1,0,2:T(8,128)} reshape(f32[1,512,4,512]{3,2,1,0:T(4,128)} %param.8) | data formatting | bytes 8388608 | tf_op jit(solution)/shard_map/reshape;squeeze | solution.py:21
  14.0 5.3 %reshape.51 = f32[2048,512,1]{1,0,2:T(8,128)} reshape(f32[1,512,4,512]{3,2,1,0:T(4,128)} %param.9) | data formatting | bytes 8388608 | tf_op jit(solution)/shard_map/reshape;squeeze | solution.py:21
  19.3 3.1 constant_dynamic-slice_fusion
  23.2 79.3 %all-gather.5.cloned.1.call-done = f32[1,512,16,512]{3,2,0,1:T(8,128)} async-done(((f32[1,64,16,512]{3,2,0,1:T(8,128)}), f32[1,512,16,512]{3,2,0,1:T(8,128)}) %all-gather.5.cloned.1.call-update) | async-done | bytes 16777232 | tf_op jit(solution)/shard_map/all_gather | solution.py:59
  102.5 18.7 %copy.44 = f32[64,8,16,512]{3,1,2,0:T(8,128)S(1)} copy(f32[64,8,16,512]{3,2,1,0:T(8,128)} %bitcast.79) | data formatting | bytes 33554432
  121.2 16.1 %fusion.15 = f32[256,8192]{1,0:T(8,128)S(1)} fusion(f32[512,256]{0,1:T(8,128)S(1)} %bitcast.83, f32[512,8192]{1,0:T(8,128)S(1)} %bitcast.72), kind=kOutput, calls=%fused_computation.15 | convolution fusion | flops 12884901888 | bytes 25690112 | tf_op jit(solution)/shard_map/dot_general | solution.py:38
  137.3 7.6 %copy.45 = f32[32,8,16,512]{3,2,1,0:T(8,128)S(1)} copy(f32[32,8,16,512]{3,1,2,0:T(8,128)S(1)} %bitcast.76) | data formatting | bytes 16777216
  144.9 10.5 %fusion.4 = f32[64,16,512,4]{2,1,3,0:T(8,128)} fusion(f32[16,512,4,64,1]{1,0,3,2,4:T(8,128)S(1)} %bitcast.74, f32[16,16,4,4]{0,1,2,3:T(8,128)S(1)} %copy.25), kind=kOutput, calls=%fused_computation.4 | convolution fusion | flops 1610612736 | bytes 16793600 | tf_op jit(solution)/shard_map/wcsb,wvst->bvct/dot_general | solution.py:18
  155.4 16.5 %copy.26 = f32[64,16,512,4]{0,1,3,2:T(8,128)} copy(f32[64,16,512,4]{2,1,3,0:T(8,128)} %fusion.4) | data formatting | bytes 16777216 | tf_op jit(solution)/shard_map/wcsb,wvst->bvct/transpose | solution.py:18
  171.9 13.9 %copy.27 = f32[64,16,2048]{2,1,0:T(8,128)} copy(f32[64,16,2048]{0,1,2:T(8,128)} %bitcast.70) | data formatting | bytes 16777216 | tf_op jit(solution)/shard_map/dot_general | solution.py:19
  185.8 17.0 %fusion.16 = f32[64,16,512]{2,1,0:T(8,128)} fusion(f32[64,16,2048]{2,1,0:T(8,128)} %copy.27, f32[2048,512,1]{1,0,2:T(8,128)} %reshape.47), kind=kOutput, calls=%fused_computation.16 | convolution fusion | flops 12884901888 | bytes 14680064 | tf_op jit(solution)/shard_map/dot_general | solution.py:19
  202.8 4.8 %collective-permute-start = (f32[64,16,512]{2,1,0:T(8,128)}, f32[64,16,512]{2,1,0:T(8,128)}, u32[]{:S(2)}, u32[]{:S(2)}) collective-permute-start(f32[64,16,512]{2,1,0:T(8,128)} %fusion.16), channel_id=1, source_target_pairs={{0,8},{8,16},{16,24},{1,9},{9,17},{17,25},{2,10},{10,18},{18,26},{... | collective-permute-start | bytes 6291464 | tf_op jit(solution)/shard_map/ppermute | solution.py:10
  207.5 18.7 %copy.46 = f32[64,8,16,512]{3,1,2,0:T(8,128)S(1)} copy(f32[64,8,16,512]{3,2,1,0:T(8,128)} %bitcast.78) | data formatting | bytes 33554432
  226.3 16.1 %fusion.17 = f32[256,8192]{1,0:T(8,128)S(1)} fusion(f32[512,256]{0,1:T(8,128)S(1)} %bitcast.82, f32[512,8192]{1,0:T(8,128)S(1)} %bitcast.73), kind=kOutput, calls=%fused_computation.17 | convolution fusion | flops 12884901888 | bytes 25690112 | tf_op jit(solution)/shard_map/dot_general | solution.py:38
  242.4 7.6 %copy.47 = f32[32,8,16,512]{3,2,1,0:T(8,128)S(1)} copy(f32[32,8,16,512]{3,1,2,0:T(8,128)S(1)} %bitcast.77) | data formatting | bytes 16777216
  250.0 10.4 %fusion.7 = f32[64,16,512,4]{2,1,3,0:T(8,128)} fusion(f32[16,512,4,64,1]{1,0,3,2,4:T(8,128)S(1)} %bitcast.75, f32[16,16,4,4]{0,3,2,1:T(4,128)S(1)} %bitcast.84), kind=kOutput, calls=%fused_computation.5 | convolution fusion | flops 1610612736 | bytes 16793600 | tf_op jit(solution)/shard_map/wcsb,wvst->bvct/dot_general | solution.py:18
  260.4 16.5 %copy.32 = f32[64,16,512,4]{0,1,3,2:T(8,128)} copy(f32[64,16,512,4]{2,1,3,0:T(8,128)} %fusion.7) | data formatting | bytes 16777216 | tf_op jit(solution)/shard_map/wcsb,wvst->bvct/transpose | solution.py:18
  276.9 13.8 %copy.33 = f32[64,16,2048]{2,1,0:T(8,128)} copy(f32[64,16,2048]{0,1,2:T(8,128)} %bitcast.71) | data formatting | bytes 16777216 | tf_op jit(solution)/shard_map/dot_general | solution.py:19
  290.7 17.1 %fusion.18 = f32[64,16,512]{2,1,0:T(8,128)} fusion(f32[64,16,2048]{2,1,0:T(8,128)} %copy.33, f32[2048,512,1]{1,0,2:T(8,128)} %reshape.51), kind=kOutput, calls=%fused_computation.18 | convolution fusion | flops 12884901888 | bytes 14680064 | tf_op jit(solution)/shard_map/dot_general | solution.py:19
  307.8 1.3 collective-permute-start.1
  309.2 1.8 fusion.11
  311.0 46.7 %collective-permute-done.1 = f32[64,16,512]{2,1,0:T(8,128)} collective-permute-done((f32[64,16,512]{2,1,0:T(8,128)}, f32[64,16,512]{2,1,0:T(8,128)}, u32[]{:S(2)}, u32[]{:S(2)}) %collective-permute-start.1) | collective-permute-done | bytes 2097184 | tf_op jit(solution)/shard_map/ppermute | solution.py:10
  357.7 4.2 %fusion.10 = f32[1,64,16,512]{3,2,1,0:T(8,128)} fusion(f32[64,16,512]{2,1,0:T(8,128)} %collective-permute-done.1, f32[1,64,16,512]{3,2,1,0:T(8,128)} %param.7, pred[]{:T(512)S(6)} %eq.7), kind=kLoop, calls=%fused_computation.7 | loop fusion | flops 524288 | bytes 6291457 | tf_op jit(solution)/shard_map/broadcast_in_dim | solution.py:73
  (14 shorter events, 1.6 us)
Async XLA Ops:
  7.2 95.3 %all-gather.5.cloned.1.call-start = ((), (), s32[]{:S(2)}) async-start(), calls=%async_computation | async-start | bytes 18874368 | tf_op jit(solution)/shard_map/all_gather | solution.py:59
  7.9 199.7 %all-gather.7.cloned.1.call-start = ((), (), s32[]{:S(2)}) async-start(), calls=%async_computation.1 | async-start | bytes 18874368 | tf_op jit(solution)/shard_map/all_gather | solution.py:64
  13.9 8.8 %copy-start.2 = (f32[1,16,16,4,4]{2,4,3,1,0:T(4,128)S(1)}, f32[1,16,16,4,4]{2,4,3,1,0:T(4,128)}, u32[]{:S(2)}) copy-start(f32[1,16,16,4,4]{2,4,3,1,0:T(4,128)} %param.10) | copy-start | bytes 49156
  202.8 106.4 %collective-permute-start = (f32[64,16,512]{2,1,0:T(8,128)}, f32[64,16,512]{2,1,0:T(8,128)}, u32[]{:S(2)}, u32[]{:S(2)}) collective-permute-start(f32[64,16,512]{2,1,0:T(8,128)} %fusion.16), channel_id=1, source_target_pairs={{0,8},{8,16},{16,24},{1,9},{9,17},{17,25},{2,10},{10,18},{18,26},{... | collective-permute-start | bytes 6291464 | tf_op jit(solution)/shard_map/ppermute | solution.py:10
  242.4 7.6 %copy-start.1 = (f32[1,16,16,4,4]{2,4,3,1,0:T(4,128)S(1)}, f32[1,16,16,4,4]{2,4,3,1,0:T(4,128)}, u32[]{:S(2)}) copy-start(f32[1,16,16,4,4]{2,4,3,1,0:T(4,128)} %param.11) | copy-start | bytes 49156
  290.7 18.4 %copy-start = (f32[1,64,16,512]{3,2,1,0:T(8,128)S(1)}, f32[1,64,16,512]{3,2,1,0:T(8,128)}, u32[]{:S(2)}) copy-start(f32[1,64,16,512]{3,2,1,0:T(8,128)} %param.6) | copy-start | bytes 6291460
  307.8 49.8 %collective-permute-start.1 = (f32[64,16,512]{2,1,0:T(8,128)}, f32[64,16,512]{2,1,0:T(8,128)}, u32[]{:S(2)}, u32[]{:S(2)}) collective-permute-start(f32[64,16,512]{2,1,0:T(8,128)} %fusion.18), channel_id=1, source_target_pairs={{8,0},{16,8},{24,16},{9,1},{17,9},{25,17},{10,2},{18,10},{26,18},{... | collective-permute-start | bytes 6291464 | tf_op jit(solution)/shard_map/ppermute | solution.py:10
Sparse Core Ops, SparseCore 0:
  9.9 92.5 all-gather.4
  104.4 89.8 all-gather.6
where the time goes:
time: 376 us; the launch traced here: 369 us
  local copies, waits for them, and re-layouts  128 us (34%)
  waiting for transfers between devices  127 us (34%)
  matrix products  87.4 us (23%)
  between operations  14.6 us (4%)
  starting transfers between devices  6.12 us (2%)
  other arithmetic  6.03 us (2%)
    all_gather x1, waiting for transfers between devices, local(): lax.all_gather(left_environ, 'bond', axis=0, tiled=True)  79.3 us
    unnamed x12, local copies, waits for them, and re-layouts  53.2 us
    ppermute x2, waiting for transfers between devices, passed_along(): return lax.ppermute(block, axis, route)  46.7 us
    dot_general x2, matrix products, finish_env(): jnp.dot(second_part.reshape(rows_dev * width, depth * states), tensor.res...  34.1 us
    transpose x2, local copies, waits for them, and re-layouts, finish_env(): jnp.einsum('wcsb,wvst->bvct', shaped, operator, precision=lax.Precision.H...  33 us
    dot_general x2, matrix products, add_piece(): lax.dot_general(piece.reshape(count, width * depth), columns, (((0,), (0,...  32.3 us
    dot_general x2, local copies, waits for them, and re-layouts, finish_env(): jnp.dot(second_part.reshape(rows_dev * width, depth * states), tensor.res...  27.7 us
    dot_general x2, matrix products, finish_env(): jnp.einsum('wcsb,wvst->bvct', shaped, operator, precision=lax.Precision.H...  21 us
  transfers between devices with their start and end apart: 4, of which 2 were waited for; matrix products, arithmetic and copies ran while one was open for 59% of the time, Pallas kernels for 0%

commit v1 on v0

v1 whole, which is shorter than its diff:
```python
import functools

import jax
import jax.numpy as jnp
from jax import lax
from jax.experimental import pallas as pl
from jax.experimental.pallas import tpu as pltpu
from jax.sharding import PartitionSpec as P

F32 = jnp.float32
BF16 = jnp.bfloat16
VMEM_BYTES = 40 << 20


def factors(n):
    pair = 2 if n % 2 == 0 else 1
    rest = n // pair
    inner = max(d for d in range(1, rest + 1) if rest % d == 0 and d * d <= rest)
    return rest // inner, inner, pair


def shares(total, weights, unit):
    cuts, done, seen = [], 0, 0
    for weight in weights:
        seen += weight
        upto = (total * seen // sum(weights)) // unit * unit
        cuts.append(upto - done)
        done = upto
    cuts[-1] += total - done
    return [c for c in cuts if c]


def parts(x):
    high = x.astype(BF16)
    return high, (x - high.astype(F32)).astype(BF16)


def parts_outside(x):
    high = lax.reduce_precision(x, 8, 7)
    return high.astype(BF16), (x - high).astype(BF16)


def stacked_parts(x, span):
    rows, columns = x.shape
    high = x.astype(BF16).astype(F32)
    both = [y.reshape(rows // span, span, columns) for y in (high, x - high)]
    return jnp.concatenate(both, 1).reshape(2 * rows, columns).astype(BF16)


def dot(a, b):
    return jnp.dot(a, b, preferred_element_type=F32)


def dot_parts(ah, al, bh, bl):
    return dot(ah, bh) + (dot(ah, bl) + dot(al, bh))


def nothing(*_):
    pass


class Turns:
    def __init__(self):
        self.token = None

    def call(self, body, name, grid, ins, outs, operands, scalars=None, scratch=(), aliases=None, flops=1000, after=()):
        lead = 0 if scalars is None else 1
        waits = [] if self.token is None else [self.token]
        tokens = len(waits)
        waits += after
        token = like((8, 128), F32)
        skip = lead + len(waits)
        count = len(operands) + len(outs)

        def inner(*refs):
            refs[skip + count][...] = jnp.zeros((8, 128), F32)
            body(*refs[:lead], *refs[skip : skip + count], *refs[skip + count + 1 :])

        *results, self.token = pl.pallas_call(
            inner,
            name=name,
            grid_spec=pltpu.PrefetchScalarGridSpec(
                num_scalar_prefetch=lead,
                grid=grid,
                in_specs=[whole(x) for x in waits[:tokens]] + [pl.BlockSpec(memory_space=pl.ANY)] * len(after) + list(ins),
                out_specs=[x for x, _ in outs] + [whole(token)],
                scratch_shapes=list(scratch),
            ),
            out_shape=[x for _, x in outs] + [token],
            input_output_aliases={skip + i: o for i, o in (aliases or {}).items()},
            compiler_params=pltpu.CompilerParams(vmem_limit_bytes=VMEM_BYTES),
            cost_estimate=pl.CostEstimate(flops=flops, bytes_accessed=1000, transcendentals=0),
        )(*([] if scalars is None else [scalars]), *waits, *operands)
        return results


    def take(self, *arrays):
        spec = pl.BlockSpec(memory_space=pl.ANY)
        outs = [(spec, pltpu.HBM(x.shape, x.dtype)) for x in arrays]
        same = {i: i for i in range(len(arrays))}
        return self.call(nothing, "take", (1,), [spec] * len(arrays), outs, [in_hbm(x) for x in arrays], aliases=same)


def whole(x):
    zeros = (0,) * len(x.shape)
    return pl.BlockSpec(tuple(x.shape), lambda *_: zeros)


def like(shape, dtype):
    return jax.ShapeDtypeStruct(tuple(shape), dtype)


def in_hbm(x):
    return pltpu.with_memory_space_constraint(x, pltpu.HBM)


def ids(dims, axis):
    return lax.broadcasted_iota(jnp.int32, dims, axis)


def cut_kernel(*refs):
    half = len(refs) // 2
    for x, out in zip(refs[:half], refs[half:]):
        out[...] = x[...]


def cut_columns(turns, envs, start, wide):
    rows, width, _ = envs[0].shape
    spec = pl.BlockSpec((rows, width, wide), lambda i: (0, 0, start // wide))
    outs = [like((rows, width, wide), F32) for _ in envs]
    return turns.call(cut_kernel, "cut_columns", (1,), [spec] * len(envs), [(whole(o), o) for o in outs], envs)


def operator_kernel(dims, op, out):
    t, v, w, s, g = dims
    rows, columns = t * g * v, w * 2 * g * s
    row, at = ids((rows, t * v), 0), ids((rows, t * v), 1)
    spread = (row // (g * v) * v + row % v == at).astype(F32).astype(BF16)
    at, column = ids((w * s, columns), 0), ids((w * s, columns), 1)
    along = (column // (2 * g * s) * s + column % s == at).astype(F32).astype(BF16)
    row, column = ids((rows, columns), 0), ids((rows, columns), 1)
    same = row // v % g == column // s % g
    low_rows = column // (g * s) % 2 == 1
    high, low = (dot(dot(spread, part).astype(BF16), along) for part in parts(op[...]))
    out[:rows] = jnp.where(same, high, 0.0).astype(BF16)
    out[rows:] = jnp.where(same, jnp.where(low_rows, 0.0, low), 0.0).astype(BF16)


def block_operator(turns, op, dims):
    t, v, w, s, g = dims
    out = like((2 * t * g * v, 2 * w * g * s), BF16)
    return turns.call(
        functools.partial(operator_kernel, dims), "operator", (1,), [whole(op)], [(whole(out), out)], [op]
    )[0]


def bra_kernel(tensor, high, low):
    step, states, _ = tensor.shape
    span = min(step, 32)
    row, at = ids((span * states, span * states), 0), ids((span * states, span * states), 1)
    order = (row % span * states + row // span == at).astype(F32).astype(BF16)
    for start in range(0, step, span):
        x = tensor[start : start + span].reshape(span * states, -1)
        for part, out in zip(parts(x), (high, low)):
            y = dot(order, part).astype(BF16)
            for t in range(states):
                out[t, start : start + span] = y[t * span : (t + 1) * span]


def bra(turns, tensor, after):
    depth, states, wide = tensor.shape
    step = min(depth, 128)
    out = like((states, depth, wide), BF16)
    spec = pl.BlockSpec((states, step, wide), lambda i: (0, i, 0))
    return turns.call(
        bra_kernel,
        "bra",
        (depth // step,),
        [pl.BlockSpec((step, states, wide), lambda i: (i, 0, 0))],
        [(spec, out)] * 2,
        [in_hbm(tensor)],
        after=after,
    )


def ket_kernel(at, *refs):
    tensors, (high, low, turned, mixed) = refs[:-4], refs[-4:]
    rows, states, _ = tensors[0].shape
    start = pl.multiple_of(at[0] * rows, rows)
    for s in range(states):
        turned[...] = jnp.concatenate([tensor[:, s, :] for tensor in tensors], 0).T
        for j in range(mixed.shape[0]):
            mixed[j, pl.ds(s, rows, stride=states), :] = turned[pl.ds(start, rows), j * 128 : (j + 1) * 128]
    for j in range(mixed.shape[0]):
        to = slice(j * 128, (j + 1) * 128)
        high[:, to], low[:, to] = parts(mixed[j])


def ket(turns, tensor, rows, lanes, scalars, row_at, count, lane_at, blocks, after):
    states = tensor.shape[1]
    if lanes % 128 or rows % 8 or count * rows % 128:
        flat = [lax.dynamic_slice_in_dim(tensor, scalars[row_at + q] * rows, rows, 0) for q in range(count)]
        flat = jnp.concatenate(flat, 0)
        starts = [scalars[lane_at + j] * lanes + scalars[0] * rows for j in range(blocks)]
        flat = jnp.concatenate([lax.dynamic_slice_in_dim(flat, b, rows, 2) for b in starts], 2)
        return parts_outside(jnp.transpose(flat, (2, 1, 0)).reshape(-1, flat.shape[0]))

    def spec(q):
        return pl.BlockSpec((rows, states, lanes), lambda j, at: (at[row_at + q], 0, at[lane_at + j]))

    block = (rows * states, count * rows)
    out = (pl.BlockSpec(block, lambda j, _: (j, 0)), like((blocks * block[0], block[1]), BF16))
    return turns.call(
        ket_kernel,
        "ket",
        (blocks,),
        [spec(q) for q in range(count)],
        [out] * 2,
        [in_hbm(tensor)] * count,
        scalars,
        [pltpu.VMEM((lanes, count * rows), F32), pltpu.VMEM((count * rows // 128, rows * states, 128), F32)],
        after=after,
    )


def first_kernel(n, *refs):
    envs, (sh, sl, op, yh, yl, held) = refs[:n], refs[n:]
    width, rows, wide = held.shape
    states = yh.shape[0]
    span = op.shape[1] // width // 2
    at_once = max(1, 512 // wide)

    @pl.when(pl.program_id(0) == 0)
    def _():
        for start in range(0, width, at_once):
            ws = range(start, min(width, start + at_once))
            sides = [jnp.concatenate([env[:, w, :] for env in envs], 0) for w in ws]
            eh, el = parts(jnp.concatenate(sides, 1))
            both = stacked_parts(dot_parts(sh[...], sl[...], eh, el), span)
            for j, w in enumerate(ws):
                held[w] = both[:, j * wide : (j + 1) * wide]

    groups = yh.shape[1] * states // (op.shape[0] // 2)
    base = pl.program_id(0) * groups
    for start in range(0, groups, at_once):
        gs = range(start, min(groups, start + at_once))
        sides = []
        for g in gs:
            at = pl.ds(pl.multiple_of((base + g) * 2 * span, 2 * span), 2 * span)
            sides.append(jnp.concatenate([held[w, at, :] for w in range(width)], 0))
        out = dot(op[...], jnp.concatenate(sides, 1))
        half = out.shape[0] // 2
        h, l = parts(out[:half] + out[half:])
        size = half // states
        for j, g in enumerate(gs):
            for t in range(states):
                to = slice(g * size, (g + 1) * size)
                yh[t, to] = h[t * size : (t + 1) * size, j * wide : (j + 1) * wide]
                yl[t, to] = l[t * size : (t + 1) * size, j * wide : (j + 1) * wide]


def first_part(turns, near, far, start, wide, ket, op, states, b_at, b_count):
    rows, width, _ = near[0].shape
    made, depth = b_count * states, ket[0].shape[1]
    steps = 4
    out = pltpu.HBM((states, made // states * width, wide), BF16)
    spec = pl.BlockSpec((states, out.shape[1] // steps, wide), lambda i: (0, i, 0))
    near_spec = pl.BlockSpec((rows, width, wide), lambda i: (0, 0, start // wide))
    ket_spec = pl.BlockSpec((made, depth), lambda i: (b_at // b_count, 0))
    h, l = turns.call(
        functools.partial(first_kernel, len(near) + len(far)),
        "first_part",
        (steps,),
        [near_spec] * len(near) + [whole(x) for x in far] + [ket_spec] * 2 + [whole(op)],
        [(spec, out)] * 2,
        [*near, *far, *ket, op],
        scratch=[pltpu.VMEM((width, 2 * made, wide), BF16)],
    )
    return h, l, b_at


def second_kernel(n, *refs):
    yhs, yls, (sh, sl), more, out = refs[:n], refs[n : 2 * n], refs[2 * n : 2 * n + 2], refs[2 * n + 2 : -1], refs[-1]
    states, depth, columns = sh.shape
    row = lambda ys: jnp.concatenate([y[t] for t in range(states) for y in ys], 1)
    flat = lambda s: s[...].reshape(states * depth, columns)
    total = dot_parts(row(yhs), row(yls), flat(sh), flat(sl)).reshape(out.shape)
    for x in more:
        total += x[...]
    out[...] = total


def second_part(turns, pieces, bra, start, count, width, more):
    states, depth, columns = bra[0].shape
    pieces = [p for p in pieces if p[2] <= start < p[2] + p[0].shape[1] // width]
    yhs = [in_hbm(h) for h, _, _ in pieces]
    yls = [in_hbm(l) for _, l, _ in pieces]
    block = next(b for b in range(min(count, 16), 0, -1) if start % b == 0 and count % b == 0)

    def y_spec(y, base):
        return pl.BlockSpec((states, block * width, y.shape[2]), lambda i: (0, (start - base) // block + i, 0))

    spec = pl.BlockSpec((block, width, columns), lambda i: (i, 0, 0))
    return turns.call(
        functools.partial(second_kernel, len(pieces)),
        "second_part",
        (count // block,),
        [y_spec(y, base) for y, (_, _, base) in zip((*yhs, *yls), pieces * 2)] + [whole(x) for x in bra] + [spec] * len(more),
        [(spec, like((count, width, columns), F32))],
        [*yhs, *yls, *bra, *more],
    )[0]


def place_kernel(edge, start, old, at, piece, env, *refs):
    out, held, arrived = refs[old], refs[old + 1], refs[old + 2]
    rows = pl.ds(start, piece.shape[0])

    def through(source, target):
        copy = pltpu.make_async_copy(source, target, arrived)
        copy.start()
        copy.wait()

    @pl.when(at[1] == edge)
    def _():
        through(env.at[rows], held)

    @pl.when(at[1] != edge)
    def _():
        through(piece, held)

    through(held, out.at[rows])


def place(turns, piece, env, start, old, scalars, edge):
    spec = pl.BlockSpec(memory_space=pl.ANY)
    return turns.call(
        functools.partial(place_kernel, edge, start, len(old)),
        "place",
        (1,),
        [spec] * (2 + len(old)),
        [(spec, pltpu.HBM(env.shape, F32))],
        [piece, env, *map(in_hbm, old)],
        scalars,
        [pltpu.VMEM(piece.shape, F32), pltpu.SemaphoreType.DMA(())],
        aliases={2 + i: i for i in range(len(old))},
    )


def local(sizes, left_env, right_env, left_site, right_site, left_mpo, right_mpo):
    outer, inner, pair = sizes
    n = outer * inner * pair
    chain = lax.axis_size("site")
    index = lambda o, i, p: (o % outer * inner + i % inner) * pair + p % pair

    def moved(x, o=0, i=0, p=0):
        route = []
        for d in range(n):
            do, di, dp = d // (inner * pair), d // pair % inner, d % pair
            route.append((d, index(do + o, di + i, dp + p)))
        return lax.ppermute(x, "bond", route)

    def handed(x, distance):
        return lax.ppermute(x, "site", [(k, k + distance) for k in range(chain) if 0 <= k + distance < chain])

    table = []
    for k in range(chain):
        for d in range(n):
            o, i, p = d // (inner * pair), d // pair % inner, d % pair
            left_rows = [index(o, i - k, p - q) for k in range(inner) for q in range(pair)]
            left_lanes = [index(o + k, i, 0) // pair for k in (*range(1, outer), 0)]
            right_rows = [index(o - k, i, p - q) for k in range(outer) for q in range(pair)]
            right_lanes = [index(o, i + k, 0) // pair for k in (*range(1, inner), 0)]
            table.append([p, k, *left_rows, *left_lanes, *right_rows, *right_lanes])
    scalars = jnp.asarray(table, jnp.int32)[lax.axis_index(("site", "bond"))]

    rows, width, depth = left_env.shape[1:]
    states = left_site.shape[2]
    group = max(1, 128 // (states * width))
    dims = (states, width, width, states, group)
    lane = 128 if depth % 128 == 0 else depth
    cuts = shares(depth, (1, 1), lane)
    pieces = shares(rows, (1, 1), group)

    class Side:
        def __init__(self, env, tensor, op, gather, reduce, row_at, distance):
            self.env, self.tensor, self.op = in_hbm(env[0]), tensor[0], op
            self.gather, self.reduce, self.row_at, self.distance = gather, reduce, row_at, distance
            self.ranks = {"o": outer, "i": inner}[gather]
            self.others = {"o": outer, "i": inner}[reduce]
            self.done, self.sent, self.handed, self.out = [], [], [], []

        def gather_near(self):
            self.near = [self.env] + [moved(self.env, p=p) for p in range(1, pair)]

        def gather_far(self, x):
            return [moved(x, **{self.gather: k}) for k in range(1, self.ranks)]

        def share(self, far):
            return [y for x in far for y in [x] + [moved(x, p=p) for p in range(1, pair)]]

        def prepare(self, after):
            count = self.ranks * pair
            self.operator = block_operator(turns, self.op, dims)
            self.ket = ket(
                turns, self.tensor, rows, pair * rows, scalars, self.row_at, count, self.row_at + count, self.others, after
            )

        def prepare_bra(self, after):
            self.bra = bra(turns, self.tensor, after)

        def first(self, j, far, b_at, b_count):
            args = self.near, far, sum(cuts[:j]), cuts[j], self.ket, self.operator, states
            self.done.append(first_part(turns, *args, b_at, b_count))

        def send(self, j):
            got = []
            for k in range(1, self.others):
                start = (k - 1) * rows + sum(pieces[:j])
                x = second_part(turns, self.done, self.bra, start, pieces[j], width, [])
                got.append(moved(x, **{self.reduce: k}))
            self.sent.append(got)

        def keep(self, j):
            start = (self.others - 1) * rows + sum(pieces[:j])
            x = second_part(turns, self.done, self.bra, start, pieces[j], width, self.sent[j])
            self.handed.append(handed(x, self.distance))

        def place(self, j):
            edge = 0 if self.distance > 0 else chain - 1
            self.out = place(turns, self.handed[j], self.env, sum(pieces[:j]), self.out, scalars, edge)

    turns = Turns()
    left_op = jnp.transpose(left_mpo[0], (3, 1, 0, 2)).reshape(states * width, -1)
    right_op = jnp.transpose(right_mpo[0], (3, 0, 1, 2)).reshape(states * width, -1)
    left = Side(left_env, left_site, left_op, "i", "o", 2, 1)
    right = Side(right_env, right_site, right_op, "o", "i", 2 + inner * pair + outer, -1)
    both = (left, right)

    far = {}

    def gather(j):
        chunks = cut_columns(turns, [side.env for side in both], sum(cuts[:j]), cuts[j])
        for side, x in zip(both, chunks):
            far[side, j] = side.gather_far(x)

    def share(j):
        arrived = turns.take(*far[left, j], *far[right, j])
        count = len(far[left, j])
        far[left, j] = left.share(arrived[:count])
        far[right, j] = right.share(arrived[count:])

    def first(side, j):
        side.first(j, far[side, j], 0, side.others * rows)

    for side in both:
        side.gather_near()
    gather(0)
    left.prepare(left.near[1:] + right.near[1:])
    right.prepare([])
    last = len(cuts) - 1
    for j in range(1, last + 1):
        gather(j)
    for side in both:
        side.prepare_bra([])
    for j in range(last + 1):
        share(j)
        for side in both:
            first(side, j)
            if j == last:
                side.send(0)
    for j in range(1, len(pieces)):
        for side in both:
            side.send(j)
    for j in range(len(pieces)):
        for side in both:
            side.keep(j)
    for j in range(len(pieces)):
        for side in both:
            side.place(j)
    return (left.out[0][None], right.out[0][None])


def solution(mesh):
    return jax.shard_map(
        functools.partial(local, factors(mesh.shape["bond"])),
        mesh=mesh,
        in_specs=(
            P("site", "bond", None, None),
            P("site", "bond", None, None),
            P("site", None, None, None),
            P("site", None, None, None),
            P("site", None, None, None, None),
            P("site", None, None, None, None),
        ),
        out_specs=(P("site", "bond", None, None), P("site", "bond", None, None)),
        check_vma=False,
    )
```

time: 376 us -> 178 us (0.47); the launches traced: 369 us -> 178 us
  local copies, waits for them, and re-layouts: 128 us -> 6.53 us
  Pallas kernels: 0 us -> 111 us
  waiting for transfers between devices: 127 us -> 35.9 us
  matrix products: 87.4 us -> 0 us
  starting transfers between devices: 6.12 us -> 23.5 us
  between operations: 14.6 us -> 1.05 us
  other arithmetic: 6.03 us -> 0 us
    pallas_call x0 -> x26, Pallas kernels: none -> 111 us  [call(): pl.pallas_call(inner, name=name, grid_spec=pltpu.PrefetchScalarGridSpec(n...]
    dot_general x6 -> x0, matrix products: 87.4 us -> none  [the longest x2 34.1 us: finish_env(): jnp.dot(second_part.reshape(rows_dev * width, depth * states), tensor.res...]
    all_gather x2 -> x0, waiting for transfers between devices: 79.3 us -> none  [the longest x1 79.3 us: local(): lax.all_gather(left_environ, 'bond', axis=0, tiled=True)]
    unnamed x12 -> x18, local copies, waits for them, and re-layouts: 53.2 us -> 4.4 us
    transpose x2 -> x1, local copies, waits for them, and re-layouts: 33 us -> 1.04 us  [local(): jnp.transpose(right_mpo[0], (3, 0, 1, 2)).reshape(states * width, -1)]
    dot_general x2 -> x0, local copies, waits for them, and re-layouts: 27.7 us -> none  [finish_env(): jnp.dot(second_part.reshape(rows_dev * width, depth * states), tensor.res...]
    ppermute x2 -> x18, starting transfers between devices: 6.04 us -> 23.5 us  [the longest x14 12.7 us: moved(): return lax.ppermute(x, 'bond', route)]
    ppermute x2 -> x18, waiting for transfers between devices: 46.7 us -> 35.9 us  [the longest x14 18.4 us: moved(): return lax.ppermute(x, 'bond', route)]
  transfers between devices with their start and end apart: 4 -> 18, of which waited for: 2 -> 9; matrix products, arithmetic and copies ran while one was open for 59% -> 1% of each run, Pallas kernels for 0% -> 61%
where the time goes in v1:
time: 178 us
  Pallas kernels  111 us (62%)
  waiting for transfers between devices  35.9 us (20%)
  starting transfers between devices  23.5 us (13%)
  local copies, waits for them, and re-layouts  6.53 us (4%)
    pallas_call x26, Pallas kernels, call(): pl.pallas_call(inner, name=name, grid_spec=pltpu.PrefetchScalarGridSpec(n...  111 us
    ppermute x14, waiting for transfers between devices, moved(): return lax.ppermute(x, 'bond', route)  18.4 us
    ppermute x4, waiting for transfers between devices, handed(): lax.ppermute(x, 'site', [(k, k + distance) for k in range(chain) if 0 <=...  17.5 us
    ppermute x14, starting transfers between devices, moved(): return lax.ppermute(x, 'bond', route)  12.7 us
    ppermute x4, starting transfers between devices, handed(): lax.ppermute(x, 'site', [(k, k + distance) for k in range(chain) if 0 <=...  10.7 us
    unnamed x18, local copies, waits for them, and re-layouts  4.4 us
  transfers between devices with their start and end apart: 18, of which 9 were waited for; matrix products, arithmetic and copies ran while one was open for 1% of the time, Pallas kernels for 61%

profile of v1, /device:TPU:0, one launch (start us, length us, event | category | flops | bytes accessed | tf_op | source)
XLA Modules:
  0.0 177.6 jit_solution(1613915723654636776)
XLA Ops:
  3.8 2.9 %collective-permute-start.2 = (f32[64,16,256]{2,1,0:T(8,128)}, f32[64,16,256]{2,1,0:T(8,128)S(1)}, u32[]{:S(2)}, u32[]{:S(2)}) collective-permute-start(f32[64,16,256]{2,1,0:T(8,128)} %get-tuple-element.73), channel_id=1, source_target_pairs={{0,2},{1,3},{2,0},{3,1},{4,6},{5,7},{6,4},{7,5},{8,10},{9,11},{10,... | collective-permute-start | bytes 3145736 | tf_op jit(solution)/shard_map/ppermute | solution.py:360
  18.0 4.1 %bra.2 = (bf16[4,512,512]{2,1,0:T(8,128)(2,1)S(1)}, bf16[4,512,512]{2,1,0:T(8,128)(2,1)S(1)}, f32[8,128]{1,0:T(8,128)S(1)}) custom-call(f32[8,128]{1,0:T(8,128)S(1)} %get-tuple-element.70.refs_0_, f32[512,4,512]{2,1,0:T(4,128)} %bitcast.22), custom_call_target="tpu_custom_call" | custom-call | flops 1000 | bytes 1000 | tf_op jit(solution)/shard_map/bra/pallas_call | solution.py:79
  22.1 4.1 %bra.3 = (bf16[4,512,512]{2,1,0:T(8,128)(2,1)S(1)}, bf16[4,512,512]{2,1,0:T(8,128)(2,1)S(1)}, f32[8,128]{1,0:T(8,128)S(1)}) custom-call(f32[8,128]{1,0:T(8,128)S(1)} %get-tuple-element.71.refs_0_, f32[512,4,512]{2,1,0:T(4,128)} %bitcast.27), custom_call_target="tpu_custom_call" | custom-call | flops 1000 | bytes 1000 | tf_op jit(solution)/shard_map/bra/pallas_call | solution.py:79
  26.2 4.2 %collective-permute-done.2.refs_1_ = f32[64,16,256]{2,1,0:T(8,128)S(1)} collective-permute-done((f32[64,16,256]{2,1,0:T(8,128)}, f32[64,16,256]{2,1,0:T(8,128)S(1)}, u32[]{:S(2)}, u32[]{:S(2)}) %collective-permute-start.2) | collective-permute-done | bytes 1048608 | tf_op jit(solution)/shard_map/ppermute | solution.py:360
  36.7 10.5 %first_part.4 = (bf16[4,2048,256]{2,1,0:T(8,128)(2,1)}, bf16[4,2048,256]{2,1,0:T(8,128)(2,1)}, f32[8,128]{1,0:T(8,128)S(1)}) custom-call(f32[8,128]{1,0:T(8,128)S(1)} %get-tuple-element.75.refs_0_, f32[64,16,512]{2,1,0:T(8,128)} %bitcast.31, f32[64,16,512]{2,1,0:T(8,128)} %collective-permute-done.refs_2_, f32[64,16,256]{2,1,0:T(8,128)S(1)} %copy-done.1, ...), custom_call_target="tpu_custom_call" | custom-call | flops 1000 | bytes 1000 | tf_op jit(solution)/shard_map/first_part/pallas_call | solution.py:79
  47.2 10.5 %first_part.5 = (bf16[4,2048,256]{2,1,0:T(8,128)(2,1)}, bf16[4,2048,256]{2,1,0:T(8,128)(2,1)}, f32[8,128]{1,0:T(8,128)S(1)}) custom-call(f32[8,128]{1,0:T(8,128)S(1)} %get-tuple-element.80.refs_0_, f32[64,16,512]{2,1,0:T(8,128)} %bitcast.38, f32[64,16,512]{2,1,0:T(8,128)} %collective-permute-done.1.refs_3_.refs_2_, f32[64,16,256]{2,1,0:T(8,128)S(1)} %copy-done.3, ...), custom_call_target="tpu_custom_call" | custom-call | flops 1000 | bytes 1000 | tf_op jit(solution)/shard_map/first_part/pallas_call | solution.py:79
  63.8 10.4 %first_part.6 = (bf16[4,2048,256]{2,1,0:T(8,128)(2,1)}, bf16[4,2048,256]{2,1,0:T(8,128)(2,1)}, f32[8,128]{1,0:T(8,128)S(1)}) custom-call(f32[8,128]{1,0:T(8,128)S(1)} %get-tuple-element.88.refs_0_, f32[64,16,512]{2,1,0:T(8,128)} %bitcast.32, f32[64,16,512]{2,1,0:T(8,128)} %collective-permute-done.refs_2_, f32[64,16,256]{2,1,0:T(8,128)S(1)} %copy-done.5, ...), custom_call_target="tpu_custom_call" | custom-call | flops 1000 | bytes 1000 | tf_op jit(solution)/shard_map/first_part/pallas_call | solution.py:79
  74.2 5.2 %second_part.8 = (f32[32,16,512]{2,1,0:T(8,128)S(1)}, f32[8,128]{1,0:T(8,128)S(1)}) custom-call(f32[8,128]{1,0:T(8,128)S(1)} %get-tuple-element.90.refs_0_, bf16[4,2048,256]{2,1,0:T(8,128)(2,1)} %get-tuple-element.91.refs_1_, bf16[4,2048,256]{2,1,0:T(8,128)(2,1)} %get-tuple-element.92.refs_2_, bf16[4,2048,256]{2,1,0:T(8,128)(2,1)} %get-tuple-element.93.refs_3_, ...), custom_call_target="tpu_custom_call" | custom-call | flops 1000 | bytes 1000 | tf_op jit(solution)/shard_map/second_part/pallas_call | solution.py:79
  81.0 10.5 %first_part.7 = (bf16[4,2048,256]{2,1,0:T(8,128)(2,1)}, bf16[4,2048,256]{2,1,0:T(8,128)(2,1)}, f32[8,128]{1,0:T(8,128)S(1)}) custom-call(f32[8,128]{1,0:T(8,128)S(1)} %get-tuple-element.97.refs_0_, f32[64,16,512]{2,1,0:T(8,128)} %bitcast.39, f32[64,16,512]{2,1,0:T(8,128)} %collective-permute-done.1.refs_3_.refs_2_, f32[64,16,256]{2,1,0:T(8,128)S(1)} %copy-done.7, ...), custom_call_target="tpu_custom_call" | custom-call | flops 1000 | bytes 1000 | tf_op jit(solution)/shard_map/first_part/pallas_call | solution.py:79
  91.5 5.1 %second_part.9 = (f32[32,16,512]{2,1,0:T(8,128)S(1)}, f32[8,128]{1,0:T(8,128)S(1)}) custom-call(f32[8,128]{1,0:T(8,128)S(1)} %get-tuple-element.99.refs_0_, bf16[4,2048,256]{2,1,0:T(8,128)(2,1)} %get-tuple-element.100.refs_1_, bf16[4,2048,256]{2,1,0:T(8,128)(2,1)} %get-tuple-element.101.refs_2_, bf16[4,2048,256]{2,1,0:T(8,128)(2,1)} %get-tuple-element.102.refs_3_, ...), custom_call_target="tpu_custom_call" | custom-call | flops 1000 | bytes 1000 | tf_op jit(solution)/shard_map/second_part/pallas_call | solution.py:79
  97.9 5.1 %second_part.10 = (f32[32,16,512]{2,1,0:T(8,128)S(1)}, f32[8,128]{1,0:T(8,128)S(1)}) custom-call(f32[8,128]{1,0:T(8,128)S(1)} %get-tuple-element.106.refs_0_, bf16[4,2048,256]{2,1,0:T(8,128)(2,1)} %get-tuple-element.91.refs_1_, bf16[4,2048,256]{2,1,0:T(8,128)(2,1)} %get-tuple-element.92.refs_2_, bf16[4,2048,256]{2,1,0:T(8,128)(2,1)} %get-tuple-element.93.refs_3_, ...), custom_call_target="tpu_custom_call" | custom-call | flops 1000 | bytes 1000 | tf_op jit(solution)/shard_map/second_part/pallas_call | solution.py:79
  103.6 5.1 %second_part.11 = (f32[32,16,512]{2,1,0:T(8,128)S(1)}, f32[8,128]{1,0:T(8,128)S(1)}) custom-call(f32[8,128]{1,0:T(8,128)S(1)} %get-tuple-element.107.refs_0_, bf16[4,2048,256]{2,1,0:T(8,128)(2,1)} %get-tuple-element.100.refs_1_, bf16[4,2048,256]{2,1,0:T(8,128)(2,1)} %get-tuple-element.101.refs_2_, bf16[4,2048,256]{2,1,0:T(8,128)(2,1)} %get-tuple-element.102.refs_3_, ...), custom_call_target="tpu_custom_call" | custom-call | flops 1000 | bytes 1000 | tf_op jit(solution)/shard_map/second_part/pallas_call | solution.py:79
  109.6 5.1 %second_part.12 = (f32[32,16,512]{2,1,0:T(8,128)S(1)}, f32[8,128]{1,0:T(8,128)S(1)}) custom-call(f32[8,128]{1,0:T(8,128)S(1)} %get-tuple-element.108.refs_0_, bf16[4,2048,256]{2,1,0:T(8,128)(2,1)} %get-tuple-element.91.refs_1_, bf16[4,2048,256]{2,1,0:T(8,128)(2,1)} %get-tuple-element.92.refs_2_, bf16[4,2048,256]{2,1,0:T(8,128)(2,1)} %get-tuple-element.93.refs_3_, ...), custom_call_target="tpu_custom_call" | custom-call | flops 1000 | bytes 1000 | tf_op jit(solution)/shard_map/second_part/pallas_call | solution.py:79
  114.8 3.5 %collective-permute-start.14 = (f32[32,16,512]{2,1,0:T(8,128)S(1)}, f32[32,16,512]{2,1,0:T(8,128)S(1)}, u32[]{:S(2)}, u32[]{:S(2)}) collective-permute-start(f32[32,16,512]{2,1,0:T(8,128)S(1)} %get-tuple-element.117), channel_id=1, source_target_pairs={{0,8},{8,16},{16,24},{1,9},{9,17},{17,25},{2,10},{10,18},{18,26},{... | collective-permute-start | bytes 3145736 | tf_op jit(solution)/shard_map/ppermute | solution.py:363
  118.3 4.4 %collective-permute-done.11.refs_7_ = f32[32,16,512]{2,1,0:T(8,128)S(1)} collective-permute-done((f32[32,16,512]{2,1,0:T(8,128)S(1)}, f32[32,16,512]{2,1,0:T(8,128)S(1)}, u32[]{:S(2)}, u32[]{:S(2)}) %collective-permute-start.11) | collective-permute-done | bytes 1048608 | tf_op jit(solution)/shard_map/ppermute | solution.py:360
  122.8 5.1 %second_part.13 = (f32[32,16,512]{2,1,0:T(8,128)S(1)}, f32[8,128]{1,0:T(8,128)S(1)}) custom-call(f32[8,128]{1,0:T(8,128)S(1)} %get-tuple-element.110.refs_0_, bf16[4,2048,256]{2,1,0:T(8,128)(2,1)} %get-tuple-element.100.refs_1_, bf16[4,2048,256]{2,1,0:T(8,128)(2,1)} %get-tuple-element.101.refs_2_, bf16[4,2048,256]{2,1,0:T(8,128)(2,1)} %get-tuple-element.102.refs_3_, ...), custom_call_target="tpu_custom_call" | custom-call | flops 1000 | bytes 1000 | tf_op jit(solution)/shard_map/second_part/pallas_call | solution.py:79
  129.2 5.1 %second_part.14 = (f32[32,16,512]{2,1,0:T(8,128)S(1)}, f32[8,128]{1,0:T(8,128)S(1)}) custom-call(f32[8,128]{1,0:T(8,128)S(1)} %get-tuple-element.112.refs_0_, bf16[4,2048,256]{2,1,0:T(8,128)(2,1)} %get-tuple-element.91.refs_1_, bf16[4,2048,256]{2,1,0:T(8,128)(2,1)} %get-tuple-element.92.refs_2_, bf16[4,2048,256]{2,1,0:T(8,128)(2,1)} %get-tuple-element.93.refs_3_, ...), custom_call_target="tpu_custom_call" | custom-call | flops 1000 | bytes 1000 | tf_op jit(solution)/shard_map/second_part/pallas_call | solution.py:79
  134.3 4.6 %collective-permute-start.16 = (f32[32,16,512]{2,1,0:T(8,128)S(1)}, f32[32,16,512]{2,1,0:T(8,128)S(1)}, u32[]{:S(2)}, u32[]{:S(2)}) collective-permute-start(f32[32,16,512]{2,1,0:T(8,128)S(1)} %get-tuple-element.121), channel_id=1, source_target_pairs={{0,8},{8,16},{16,24},{1,9},{9,17},{17,25},{2,10},{10,18},{18,26},{... | collective-permute-start | bytes 3145736 | tf_op jit(solution)/shard_map/ppermute | solution.py:363
  139.0 5.1 %collective-permute-done.13.refs_7_ = f32[32,16,512]{2,1,0:T(8,128)S(1)} collective-permute-done((f32[32,16,512]{2,1,0:T(8,128)S(1)}, f32[32,16,512]{2,1,0:T(8,128)S(1)}, u32[]{:S(2)}, u32[]{:S(2)}) %collective-permute-start.13) | collective-permute-done | bytes 1048608 | tf_op jit(solution)/shard_map/ppermute | solution.py:360
  144.1 5.1 %second_part.15 = (f32[32,16,512]{2,1,0:T(8,128)S(1)}, f32[8,128]{1,0:T(8,128)S(1)}) custom-call(f32[8,128]{1,0:T(8,128)S(1)} %get-tuple-element.114.refs_0_, bf16[4,2048,256]{2,1,0:T(8,128)(2,1)} %get-tuple-element.100.refs_1_, bf16[4,2048,256]{2,1,0:T(8,128)(2,1)} %get-tuple-element.101.refs_2_, bf16[4,2048,256]{2,1,0:T(8,128)(2,1)} %get-tuple-element.102.refs_3_, ...), custom_call_target="tpu_custom_call" | custom-call | flops 1000 | bytes 1000 | tf_op jit(solution)/shard_map/second_part/pallas_call | solution.py:79
  150.5 2.7 %place.4 = (f32[64,16,512]{2,1,0:T(8,128)}, f32[8,128]{1,0:T(8,128)S(1)}) custom-call(s32[14]{0:T(128)S(1)} %dynamic-slice_bitcast_fusion.refs_0_, f32[8,128]{1,0:T(8,128)S(1)} %get-tuple-element.116.refs_1_, f32[32,16,512]{2,1,0:T(8,128)S(1)} %collective-permute-done.14.refs_2_, f32[64,16,512]{2,1,0:T(8,128)} %bitcast.33), custom_call_target="tpu_custom_call" | custom-call | flops 1000 | bytes 1000 | tf_op jit(solution)/shard_map/place/pallas_call | solution.py:79
  154.9 7.4 %collective-permute-done.16.refs_2_ = f32[32,16,512]{2,1,0:T(8,128)S(1)} collective-permute-done((f32[32,16,512]{2,1,0:T(8,128)S(1)}, f32[32,16,512]{2,1,0:T(8,128)S(1)}, u32[]{:S(2)}, u32[]{:S(2)}) %collective-permute-start.16) | collective-permute-done | bytes 1048608 | tf_op jit(solution)/shard_map/ppermute | solution.py:363
  162.3 2.7 %place.6 = (f32[64,16,512]{2,1,0:T(8,128)}, f32[8,128]{1,0:T(8,128)S(1)}) custom-call(s32[14]{0:T(128)S(1)} %dynamic-slice_bitcast_fusion.refs_0_, f32[8,128]{1,0:T(8,128)S(1)} %get-tuple-element.120.refs_1_, f32[32,16,512]{2,1,0:T(8,128)S(1)} %collective-permute-done.16.refs_2_, f32[64,16,512]{2,1,0:T(8,128)} %bitcast.34, ...), custom_call_target="tpu_custom_call", output_to_operand_aliasing={{0}: (4, {})} | custom-call | flops 1000 | bytes 1000 | tf_op jit(solution)/shard_map/place/pallas_call | solution.py:79
  165.1 10.1 %collective-permute-done.17.refs_2_ = f32[32,16,512]{2,1,0:T(8,128)S(1)} collective-permute-done((f32[32,16,512]{2,1,0:T(8,128)S(1)}, f32[32,16,512]{2,1,0:T(8,128)S(1)}, u32[]{:S(2)}, u32[]{:S(2)}) %collective-permute-start.17) | collective-permute-done | bytes 1048608 | tf_op jit(solution)/shard_map/ppermute | solution.py:363
  (62 shorter events, 37.5 us)
Async XLA Ops:
  0.6 10.1 %collective-permute-start = (f32[64,16,512]{2,1,0:T(8,128)}, f32[64,16,512]{2,1,0:T(8,128)}, u32[]{:S(2)}, u32[]{:S(2)}) collective-permute-start(f32[64,16,512]{2,1,0:T(8,128)} %bitcast.28), channel_id=1, source_target_pairs={{0,1},{1,0},{2,3},{3,2},{4,5},{5,4},{6,7},{7,6},{8,9},{9,8},{10,11... | collective-permute-start | bytes 6291464 | tf_op jit(solution)/shard_map/ppermute | solution.py:360
  1.1 7.1 %copy-start.8 = (f32[1,16,16,4,4]{2,4,3,1,0:T(4,128)S(1)}, f32[1,16,16,4,4]{2,4,3,1,0:T(4,128)}, u32[]{:S(2)}) copy-start(f32[1,16,16,4,4]{2,4,3,1,0:T(4,128)} %param.11) | copy-start | bytes 49156
  1.1 9.6 %collective-permute-start.1 = (f32[64,16,512]{2,1,0:T(8,128)}, f32[64,16,512]{2,1,0:T(8,128)}, u32[]{:S(2)}, u32[]{:S(2)}) collective-permute-start(f32[64,16,512]{2,1,0:T(8,128)} %bitcast.35), channel_id=1, source_target_pairs={{0,1},{1,0},{2,3},{3,2},{4,5},{5,4},{6,7},{7,6},{8,9},{9,8},{10,11... | collective-permute-start | bytes 6291464 | tf_op jit(solution)/shard_map/ppermute | solution.py:360
  3.8 26.5 %collective-permute-start.2 = (f32[64,16,256]{2,1,0:T(8,128)}, f32[64,16,256]{2,1,0:T(8,128)S(1)}, u32[]{:S(2)}, u32[]{:S(2)}) collective-permute-start(f32[64,16,256]{2,1,0:T(8,128)} %get-tuple-element.73), channel_id=1, source_target_pairs={{0,2},{1,3},{2,0},{3,1},{4,6},{5,7},{6,4},{7,5},{8,10},{9,11},{10,... | collective-permute-start | bytes 3145736 | tf_op jit(solution)/shard_map/ppermute | solution.py:360
  6.7 24.9 %collective-permute-start.3 = (f32[64,16,256]{2,1,0:T(8,128)S(1)}, f32[64,16,256]{2,1,0:T(8,128)S(1)}, u32[]{:S(2)}, u32[]{:S(2)}) collective-permute-start(f32[64,16,256]{2,1,0:T(8,128)S(1)} %get-tuple-element.74), channel_id=1, source_target_pairs={{0,4},{1,5},{2,6},{3,7},{4,0},{5,1},{6,2},{7,3},{8,12},{9,13},{10,... | collective-permute-start | bytes 3145736 | tf_op jit(solution)/shard_map/ppermute | solution.py:360
  30.3 1.3 copy-start
  32.6 2.9 %collective-permute-start.4 = (f32[64,16,256]{2,1,0:T(8,128)}, f32[64,16,256]{2,1,0:T(8,128)S(1)}, u32[]{:S(2)}, u32[]{:S(2)}) collective-permute-start(f32[64,16,256]{2,1,0:T(8,128)} %get-tuple-element.76.refs_3_), channel_id=1, source_target_pairs={{0,1},{1,0},{2,3},{3,2},{4,5},{5,4},{6,7},{7,6},{8,9},{9,8},{10,11... | collective-permute-start | bytes 3145736 | tf_op jit(solution)/shard_map/ppermute | solution.py:360
  32.6 14.6 %collective-permute-start.5 = (f32[64,16,256]{2,1,0:T(8,128)}, f32[64,16,256]{2,1,0:T(8,128)S(1)}, u32[]{:S(2)}, u32[]{:S(2)}) collective-permute-start(f32[64,16,256]{2,1,0:T(8,128)} %get-tuple-element.81.refs_3_), channel_id=1, source_target_pairs={{0,1},{1,0},{2,3},{3,2},{4,5},{5,4},{6,7},{7,6},{8,9},{9,8},{10,11... | collective-permute-start | bytes 3145736 | tf_op jit(solution)/shard_map/ppermute | solution.py:360
  33.1 25.1 %collective-permute-start.6 = (f32[64,16,256]{2,1,0:T(8,128)S(1)}, f32[64,16,256]{2,1,0:T(8,128)S(1)}, u32[]{:S(2)}, u32[]{:S(2)}) collective-permute-start(f32[64,16,256]{2,1,0:T(8,128)S(1)} %get-tuple-element.86), channel_id=1, source_target_pairs={{0,2},{1,3},{2,0},{3,1},{4,6},{5,7},{6,4},{7,5},{8,10},{9,11},{10,... | collective-permute-start | bytes 3145736 | tf_op jit(solution)/shard_map/ppermute | solution.py:360
  33.9 24.8 %collective-permute-start.7 = (f32[64,16,256]{2,1,0:T(8,128)S(1)}, f32[64,16,256]{2,1,0:T(8,128)S(1)}, u32[]{:S(2)}, u32[]{:S(2)}) collective-permute-start(f32[64,16,256]{2,1,0:T(8,128)S(1)} %get-tuple-element.87), channel_id=1, source_target_pairs={{0,4},{1,5},{2,6},{3,7},{4,0},{5,1},{6,2},{7,3},{8,12},{9,13},{10,... | collective-permute-start | bytes 3145736 | tf_op jit(solution)/shard_map/ppermute | solution.py:360
  35.4 1.2 copy-start.1
  36.7 10.5 %copy-start.3 = (f32[64,16,256]{2,1,0:T(8,128)S(1)}, f32[64,16,256]{2,1,0:T(8,128)}, u32[]{:S(2)}) copy-start(f32[64,16,256]{2,1,0:T(8,128)} %get-tuple-element.81.refs_3_) | copy-start | bytes 3145732
  59.7 2.9 %collective-permute-start.8 = (f32[64,16,256]{2,1,0:T(8,128)}, f32[64,16,256]{2,1,0:T(8,128)S(1)}, u32[]{:S(2)}, u32[]{:S(2)}) collective-permute-start(f32[64,16,256]{2,1,0:T(8,128)} %get-tuple-element.89.refs_3_), channel_id=1, source_target_pairs={{0,1},{1,0},{2,3},{3,2},{4,5},{5,4},{6,7},{7,6},{8,9},{9,8},{10,11... | collective-permute-start | bytes 3145736 | tf_op jit(solution)/shard_map/ppermute | solution.py:360
  59.7 21.3 %collective-permute-start.9 = (f32[64,16,256]{2,1,0:T(8,128)}, f32[64,16,256]{2,1,0:T(8,128)S(1)}, u32[]{:S(2)}, u32[]{:S(2)}) collective-permute-start(f32[64,16,256]{2,1,0:T(8,128)} %get-tuple-element.98.refs_3_), channel_id=1, source_target_pairs={{0,1},{1,0},{2,3},{3,2},{4,5},{5,4},{6,7},{7,6},{8,9},{9,8},{10,11... | collective-permute-start | bytes 3145736 | tf_op jit(solution)/shard_map/ppermute | solution.py:360
  62.6 1.2 copy-start.5
  74.2 6.8 %copy-start.7 = (f32[64,16,256]{2,1,0:T(8,128)S(1)}, f32[64,16,256]{2,1,0:T(8,128)}, u32[]{:S(2)}) copy-start(f32[64,16,256]{2,1,0:T(8,128)} %get-tuple-element.98.refs_3_) | copy-start | bytes 3145732
  79.4 30.2 %collective-permute-start.10 = (f32[32,16,512]{2,1,0:T(8,128)S(1)}, f32[32,16,512]{2,1,0:T(8,128)S(1)}, u32[]{:S(2)}, u32[]{:S(2)}) collective-permute-start(f32[32,16,512]{2,1,0:T(8,128)S(1)} %get-tuple-element.109), channel_id=1, source_target_pairs={{0,4},{1,5},{2,6},{3,7},{4,0},{5,1},{6,2},{7,3},{8,12},{9,13},{10,... | collective-permute-start | bytes 3145736 | tf_op jit(solution)/shard_map/ppermute | solution.py:360
  96.6 26.1 %collective-permute-start.11 = (f32[32,16,512]{2,1,0:T(8,128)S(1)}, f32[32,16,512]{2,1,0:T(8,128)S(1)}, u32[]{:S(2)}, u32[]{:S(2)}) collective-permute-start(f32[32,16,512]{2,1,0:T(8,128)S(1)} %get-tuple-element.111), channel_id=1, source_target_pairs={{0,2},{1,3},{2,0},{3,1},{4,6},{5,7},{6,4},{7,5},{8,10},{9,11},{10,... | collective-permute-start | bytes 3145736 | tf_op jit(solution)/shard_map/ppermute | solution.py:360
  103.0 26.2 %collective-permute-start.12 = (f32[32,16,512]{2,1,0:T(8,128)S(1)}, f32[32,16,512]{2,1,0:T(8,128)S(1)}, u32[]{:S(2)}, u32[]{:S(2)}) collective-permute-start(f32[32,16,512]{2,1,0:T(8,128)S(1)} %get-tuple-element.113), channel_id=1, source_target_pairs={{0,4},{1,5},{2,6},{3,7},{4,0},{5,1},{6,2},{7,3},{8,12},{9,13},{10,... | collective-permute-start | bytes 3145736 | tf_op jit(solution)/shard_map/ppermute | solution.py:360
  108.7 35.4 %collective-permute-start.13 = (f32[32,16,512]{2,1,0:T(8,128)S(1)}, f32[32,16,512]{2,1,0:T(8,128)S(1)}, u32[]{:S(2)}, u32[]{:S(2)}) collective-permute-start(f32[32,16,512]{2,1,0:T(8,128)S(1)} %get-tuple-element.115), channel_id=1, source_target_pairs={{0,2},{1,3},{2,0},{3,1},{4,6},{5,7},{6,4},{7,5},{8,10},{9,11},{10,... | collective-permute-start | bytes 3145736 | tf_op jit(solution)/shard_map/ppermute | solution.py:360
  114.8 35.8 %collective-permute-start.14 = (f32[32,16,512]{2,1,0:T(8,128)S(1)}, f32[32,16,512]{2,1,0:T(8,128)S(1)}, u32[]{:S(2)}, u32[]{:S(2)}) collective-permute-start(f32[32,16,512]{2,1,0:T(8,128)S(1)} %get-tuple-element.117), channel_id=1, source_target_pairs={{0,8},{8,16},{16,24},{1,9},{9,17},{17,25},{2,10},{10,18},{18,26},{... | collective-permute-start | bytes 3145736 | tf_op jit(solution)/shard_map/ppermute | solution.py:363
  127.9 25.4 %collective-permute-start.15 = (f32[32,16,512]{2,1,0:T(8,128)S(1)}, f32[32,16,512]{2,1,0:T(8,128)S(1)}, u32[]{:S(2)}, u32[]{:S(2)}) collective-permute-start(f32[32,16,512]{2,1,0:T(8,128)S(1)} %get-tuple-element.119), channel_id=1, source_target_pairs={{8,0},{16,8},{24,16},{9,1},{17,9},{25,17},{10,2},{18,10},{26,18},{... | collective-permute-start | bytes 3145736 | tf_op jit(solution)/shard_map/ppermute | solution.py:363
  134.3 28.0 %collective-permute-start.16 = (f32[32,16,512]{2,1,0:T(8,128)S(1)}, f32[32,16,512]{2,1,0:T(8,128)S(1)}, u32[]{:S(2)}, u32[]{:S(2)}) collective-permute-start(f32[32,16,512]{2,1,0:T(8,128)S(1)} %get-tuple-element.121), channel_id=1, source_target_pairs={{0,8},{8,16},{16,24},{1,9},{9,17},{17,25},{2,10},{10,18},{18,26},{... | collective-permute-start | bytes 3145736 | tf_op jit(solution)/shard_map/ppermute | solution.py:363
  149.2 25.9 %collective-permute-start.17 = (f32[32,16,512]{2,1,0:T(8,128)S(1)}, f32[32,16,512]{2,1,0:T(8,128)S(1)}, u32[]{:S(2)}, u32[]{:S(2)}) collective-permute-start(f32[32,16,512]{2,1,0:T(8,128)S(1)} %get-tuple-element.125), channel_id=1, source_target_pairs={{8,0},{16,8},{24,16},{9,1},{17,9},{25,17},{10,2},{18,10},{26,18},{... | collective-permute-start | bytes 3145736 | tf_op jit(solution)/shard_map/ppermute | solution.py:363
  (3 other events, 2.9 us)

commit v2 on v1

--- a/solution.py
+++ b/solution.py
@@ -9,7 +9,8 @@
 
 F32 = jnp.float32
 BF16 = jnp.bfloat16
-VMEM_BYTES = 40 << 20
+VMEM_BYTES = 27 << 20
+FLOPS_A_US = 10**11
 
 
 def factors(n):
@@ -63,7 +64,7 @@
     def __init__(self):
         self.token = None
 
-    def call(self, body, name, grid, ins, outs, operands, scalars=None, scratch=(), aliases=None, flops=1000, after=()):
+    def call(self, body, name, grid, ins, outs, operands, scalars=None, scratch=(), aliases=None, about_us=0.3, after=()):
         lead = 0 if scalars is None else 1
         waits = [] if self.token is None else [self.token]
         tokens = len(waits)
@@ -89,7 +90,7 @@
             out_shape=[x for _, x in outs] + [token],
             input_output_aliases={skip + i: o for i, o in (aliases or {}).items()},
             compiler_params=pltpu.CompilerParams(vmem_limit_bytes=VMEM_BYTES),
-            cost_estimate=pl.CostEstimate(flops=flops, bytes_accessed=1000, transcendentals=0),
+            cost_estimate=pl.CostEstimate(flops=int(about_us * FLOPS_A_US), bytes_accessed=1000, transcendentals=0),
         )(*([] if scalars is None else [scalars]), *waits, *operands)
         return results
 
@@ -121,14 +122,15 @@
 def cut_kernel(*refs):
     half = len(refs) // 2
     for x, out in zip(refs[:half], refs[half:]):
-        out[...] = x[...]
+        for w in range(out.shape[0]):
+            out[w] = x[:, w, :]
 
 
 def cut_columns(turns, envs, start, wide):
     rows, width, _ = envs[0].shape
     spec = pl.BlockSpec((rows, width, wide), lambda i: (0, 0, start // wide))
-    outs = [like((rows, width, wide), F32) for _ in envs]
-    return turns.call(cut_kernel, "cut_columns", (1,), [spec] * len(envs), [(whole(o), o) for o in outs], envs)
+    out = like((width, rows, wide), F32)
+    return turns.call(cut_kernel, "cut_columns", (1,), [spec] * len(envs), [(whole(out), out)] * len(envs), envs)
 
 
 def operator_kernel(dims, op, out):
@@ -180,6 +182,7 @@
         [(spec, out)] * 2,
         [in_hbm(tensor)],
         after=after,
+        about_us=4,
     )
 
 
@@ -220,70 +223,83 @@
         scalars,
         [pltpu.VMEM((lanes, count * rows), F32), pltpu.VMEM((count * rows // 128, rows * states, 128), F32)],
         after=after,
+        about_us=2.7,
     )
 
 
-def first_kernel(n, *refs):
+def first_kernel(raw, *refs):
+    n = len(raw)
     envs, (sh, sl, op, yh, yl, held) = refs[:n], refs[n:]
-    width, rows, wide = held.shape
+    width, _, wide = held.shape
     states = yh.shape[0]
     span = op.shape[1] // width // 2
     at_once = max(1, 512 // wide)
 
-    @pl.when(pl.program_id(0) == 0)
+    here = envs[0].shape[0]
+    halves = width // here
+    step = pl.program_id(0)
+
+    @pl.when(step < halves)
     def _():
-        for start in range(0, width, at_once):
-            ws = range(start, min(width, start + at_once))
-            sides = [jnp.concatenate([env[:, w, :] for env in envs], 0) for w in ws]
+        for start in range(0, here, at_once):
+            ws = range(start, min(here, start + at_once))
+            pick = lambda w: [env[:, w, :] if r else env[w] for r, env in zip(raw, envs)]
+            sides = [jnp.concatenate(pick(w), 0) for w in ws]
             eh, el = parts(jnp.concatenate(sides, 1))
             both = stacked_parts(dot_parts(sh[...], sl[...], eh, el), span)
             for j, w in enumerate(ws):
-                held[w] = both[:, j * wide : (j + 1) * wide]
-
-    groups = yh.shape[1] * states // (op.shape[0] // 2)
-    base = pl.program_id(0) * groups
-    for start in range(0, groups, at_once):
-        gs = range(start, min(groups, start + at_once))
-        sides = []
-        for g in gs:
-            at = pl.ds(pl.multiple_of((base + g) * 2 * span, 2 * span), 2 * span)
-            sides.append(jnp.concatenate([held[w, at, :] for w in range(width)], 0))
-        out = dot(op[...], jnp.concatenate(sides, 1))
-        half = out.shape[0] // 2
-        h, l = parts(out[:half] + out[half:])
-        size = half // states
-        for j, g in enumerate(gs):
-            for t in range(states):
-                to = slice(g * size, (g + 1) * size)
-                yh[t, to] = h[t * size : (t + 1) * size, j * wide : (j + 1) * wide]
-                yl[t, to] = l[t * size : (t + 1) * size, j * wide : (j + 1) * wide]
-
-
-def first_part(turns, near, far, start, wide, ket, op, states, b_at, b_count):
-    rows, width, _ = near[0].shape
+                held[step * here + w] = both[:, j * wide : (j + 1) * wide]
+
+    @pl.when(step >= halves)
+    def _():
+        groups = yh.shape[1] * states // (op.shape[0] // 2)
+        base = (step - halves) * groups
+        for start in range(0, groups, at_once):
+            gs = range(start, min(groups, start + at_once))
+            sides = []
+            for g in gs:
+                at = pl.ds(pl.multiple_of((base + g) * 2 * span, 2 * span), 2 * span)
+                sides.append(jnp.concatenate([held[w, at, :] for w in range(width)], 0))
+            out = dot(op[...], jnp.concatenate(sides, 1))
+            half = out.shape[0] // 2
+            h, l = parts(out[:half] + out[half:])
+            size = half // states
+            for j, g in enumerate(gs):
+                for t in range(states):
+                    to = slice(g * size, (g + 1) * size)
+                    yh[t, to] = h[t * size : (t + 1) * size, j * wide : (j + 1) * wide]
+                    yl[t, to] = l[t * size : (t + 1) * size, j * wide : (j + 1) * wide]
+
+
+def first_part(turns, own, near, far, start, ket, op, states, b_at, b_count):
+    width, rows, wide = own.shape
     made, depth = b_count * states, ket[0].shape[1]
     steps = 4
-    out = pltpu.HBM((states, made // states * width, wide), BF16)
-    spec = pl.BlockSpec((states, out.shape[1] // steps, wide), lambda i: (0, i, 0))
-    near_spec = pl.BlockSpec((rows, width, wide), lambda i: (0, 0, start // wide))
+    shape = (states, made // states * width, wide)
+    out = like(shape, BF16) if start else pltpu.HBM(shape, BF16)
+    halves = 2 if width % 16 == 0 else 1
+    here = width // halves
+    spec = pl.BlockSpec((states, out.shape[1] // steps, wide), lambda i: (0, jnp.maximum(i - halves, 0), 0))
+    near_spec = pl.BlockSpec((rows, here, wide), lambda i: (0, jnp.minimum(i, halves - 1), start // wide))
+    far_spec = pl.BlockSpec((here, rows, wide), lambda i: (jnp.minimum(i, halves - 1), 0, 0))
     ket_spec = pl.BlockSpec((made, depth), lambda i: (b_at // b_count, 0))
     h, l = turns.call(
-        functools.partial(first_kernel, len(near) + len(far)),
+        functools.partial(first_kernel, (False, *(True for _ in near), *(False for _ in far))),
         "first_part",
-        (steps,),
-        [near_spec] * len(near) + [whole(x) for x in far] + [ket_spec] * 2 + [whole(op)],
+        (halves + steps,),
+        [far_spec] + [near_spec] * len(near) + [far_spec] * len(far) + [ket_spec] * 2 + [whole(op)],
         [(spec, out)] * 2,
-        [*near, *far, *ket, op],
+        [own, *near, *far, *ket, op],
         scratch=[pltpu.VMEM((width, 2 * made, wide), BF16)],
+        about_us=3 + 0.03 * wide,
     )
-    return h, l, b_at
+    return (h, l, b_at) if start else (in_hbm(h), in_hbm(l), b_at)
 
 
 def second_kernel(n, *refs):
     yhs, yls, (sh, sl), more, out = refs[:n], refs[n : 2 * n], refs[2 * n : 2 * n + 2], refs[2 * n + 2 : -1], refs[-1]
-    states, depth, columns = sh.shape
-    row = lambda ys: jnp.concatenate([y[t] for t in range(states) for y in ys], 1)
-    flat = lambda s: s[...].reshape(states * depth, columns)
+    row = lambda ys: jnp.concatenate([y[t] for t in range(ys[0].shape[0]) for y in ys], 1)
+    flat = lambda s: s[...].reshape(-1, s.shape[2])
     total = dot_parts(row(yhs), row(yls), flat(sh), flat(sl)).reshape(out.shape)
     for x in more:
         total += x[...]
@@ -293,9 +309,9 @@
 def second_part(turns, pieces, bra, start, count, width, more):
     states, depth, columns = bra[0].shape
     pieces = [p for p in pieces if p[2] <= start < p[2] + p[0].shape[1] // width]
-    yhs = [in_hbm(h) for h, _, _ in pieces]
-    yls = [in_hbm(l) for _, l, _ in pieces]
-    block = next(b for b in range(min(count, 16), 0, -1) if start % b == 0 and count % b == 0)
+    yhs = [h for h, _, _ in pieces]
+    yls = [l for _, l, _ in pieces]
+    block = next(b for b in range(min(count, 24), 0, -1) if start % b == 0 and count % b == 0)
 
     def y_spec(y, base):
         return pl.BlockSpec((states, block * width, y.shape[2]), lambda i: (0, (start - base) // block + i, 0))
@@ -308,6 +324,7 @@
         [y_spec(y, base) for y, (_, _, base) in zip((*yhs, *yls), pieces * 2)] + [whole(x) for x in bra] + [spec] * len(more),
         [(spec, like((count, width, columns), F32))],
         [*yhs, *yls, *bra, *more],
+        about_us=3e-2,
     )[0]
 
 
@@ -343,6 +360,7 @@
         scalars,
         [pltpu.VMEM(piece.shape, F32), pltpu.SemaphoreType.DMA(())],
         aliases={2 + i: i for i in range(len(old))},
+        about_us=1e-1,
     )
 
 
@@ -379,7 +397,6 @@
     dims = (states, width, width, states, group)
     lane = 128 if depth % 128 == 0 else depth
     cuts = shares(depth, (1, 1), lane)
-    pieces = shares(rows, (1, 1), group)
 
     class Side:
         def __init__(self, env, tensor, op, gather, reduce, row_at, distance):
@@ -387,10 +404,11 @@
             self.gather, self.reduce, self.row_at, self.distance = gather, reduce, row_at, distance
             self.ranks = {"o": outer, "i": inner}[gather]
             self.others = {"o": outer, "i": inner}[reduce]
-            self.done, self.sent, self.handed, self.out = [], [], [], []
+            self.pieces = shares(rows, (1, 1) if distance > 0 else (2, 3, 3), group)
+            self.own, self.done, self.sent, self.handed, self.out = [], [], [], [], []
 
         def gather_near(self):
-            self.near = [self.env] + [moved(self.env, p=p) for p in range(1, pair)]
+            self.near = [moved(self.env, p=p) for p in range(1, pair)]
 
         def gather_far(self, x):
             return [moved(x, **{self.gather: k}) for k in range(1, self.ranks)]
@@ -409,25 +427,25 @@
             self.bra = bra(turns, self.tensor, after)
 
         def first(self, j, far, b_at, b_count):
-            args = self.near, far, sum(cuts[:j]), cuts[j], self.ket, self.operator, states
+            args = self.own[j], self.near, far, sum(cuts[:j]), self.ket, self.operator, states
             self.done.append(first_part(turns, *args, b_at, b_count))
 
         def send(self, j):
             got = []
             for k in range(1, self.others):
-                start = (k - 1) * rows + sum(pieces[:j])
-                x = second_part(turns, self.done, self.bra, start, pieces[j], width, [])
+                start = (k - 1) * rows + sum(self.pieces[:j])
+                x = second_part(turns, self.done, self.bra, start, self.pieces[j], width, [])
                 got.append(moved(x, **{self.reduce: k}))
             self.sent.append(got)
 
         def keep(self, j):
-            start = (self.others - 1) * rows + sum(pieces[:j])
-            x = second_part(turns, self.done, self.bra, start, pieces[j], width, self.sent[j])
+            start = (self.others - 1) * rows + sum(self.pieces[:j])
+            x = second_part(turns, self.done, self.bra, start, self.pieces[j], width, self.sent[j])
             self.handed.append(handed(x, self.distance))
 
         def place(self, j):
             edge = 0 if self.distance > 0 else chain - 1
-            self.out = place(turns, self.handed[j], self.env, sum(pieces[:j]), self.out, scalars, edge)
+            self.out = place(turns, self.handed[j], self.env, sum(self.pieces[:j]), self.out, scalars, edge)
 
     turns = Turns()
     left_op = jnp.transpose(left_mpo[0], (3, 1, 0, 2)).reshape(states * width, -1)
@@ -441,10 +459,12 @@
     def gather(j):
         chunks = cut_columns(turns, [side.env for side in both], sum(cuts[:j]), cuts[j])
         for side, x in zip(both, chunks):
+            side.own.append(x)
             far[side, j] = side.gather_far(x)
 
     def share(j):
-        arrived = turns.take(*far[left, j], *far[right, j])
+        arrived = [*far[left, j], *far[right, j]]
+        arrived = turns.take(*arrived)
         count = len(far[left, j])
         far[left, j] = left.share(arrived[:count])
         far[right, j] = right.share(arrived[count:])
@@ -455,28 +475,32 @@
     for side in both:
         side.gather_near()
     gather(0)
-    left.prepare(left.near[1:] + right.near[1:])
+    left.prepare(left.near + right.near)
     right.prepare([])
-    last = len(cuts) - 1
-    for j in range(1, last + 1):
-        gather(j)
+    gather(1)
     for side in both:
         side.prepare_bra([])
-    for j in range(last + 1):
-        share(j)
-        for side in both:
-            first(side, j)
-            if j == last:
-                side.send(0)
-    for j in range(1, len(pieces)):
-        for side in both:
-            side.send(j)
-    for j in range(len(pieces)):
-        for side in both:
-            side.keep(j)
-    for j in range(len(pieces)):
-        for side in both:
-            side.place(j)
+    share(0)
+    first(left, 0)
+    first(right, 0)
+    share(1)
+    first(left, 1)
+    left.send(0)
+    first(right, 1)
+    right.send(0)
+    left.send(1)
+    right.send(1)
+    left.keep(0)
+    right.keep(0)
+    right.send(2)
+    right.keep(1)
+    left.keep(1)
+    left.place(0)
+    right.place(0)
+    right.keep(2)
+    right.place(1)
+    left.place(1)
+    right.place(2)
     return (left.out[0][None], right.out[0][None])
 
 

time: 178 us -> 169 us (0.949)
  waiting for transfers between devices: 35.9 us -> 24.3 us
  local copies, waits for them, and re-layouts: 6.53 us -> 2.85 us
  Pallas kernels: 111 us -> 114 us
    ppermute x14 -> x15, waiting for transfers between devices: 18.4 us -> 9.93 us  [moved(): return lax.ppermute(x, 'bond', route)]
    pallas_call x26 -> x29, Pallas kernels: 111 us -> 114 us  [call(): pl.pallas_call(inner, name=name, grid_spec=pltpu.PrefetchScalarGridSpec(n...]
    ppermute x4 -> x5, waiting for transfers between devices: 17.5 us -> 14.4 us  [handed(): lax.ppermute(x, 'site', [(k, k + distance) for k in range(chain) if 0 <=...]
    unnamed x18 -> x34, local copies, waits for them, and re-layouts: 4.4 us -> 1.62 us
    ppermute x14 -> x15, starting transfers between devices: 12.7 us -> 13.6 us  [moved(): return lax.ppermute(x, 'bond', route)]
    ppermute x4 -> x5, starting transfers between devices: 10.7 us -> 11.6 us  [handed(): lax.ppermute(x, 'site', [(k, k + distance) for k in range(chain) if 0 <=...]
  transfers between devices with their start and end apart: 18 -> 20, of which waited for: 9 -> 10; matrix products, arithmetic and copies ran while one was open for 1% -> 1% of each run, Pallas kernels for 61% -> 67%
where the time goes in v2:
time: 169 us; the launch traced here: 168 us
  Pallas kernels  114 us (67%)
  starting transfers between devices  25.2 us (15%)
  waiting for transfers between devices  24.3 us (14%)
  local copies, waits for them, and re-layouts  2.85 us (2%)
    pallas_call x29, Pallas kernels, call(): pl.pallas_call(inner, name=name, grid_spec=pltpu.PrefetchScalarGridSpec(n...  114 us
    ppermute x5, waiting for transfers between devices, handed(): lax.ppermute(x, 'site', [(k, k + distance) for k in range(chain) if 0 <=...  14.4 us
    ppermute x15, starting transfers between devices, moved(): return lax.ppermute(x, 'bond', route)  13.6 us
    ppermute x5, starting transfers between devices, handed(): lax.ppermute(x, 'site', [(k, k + distance) for k in range(chain) if 0 <=...  11.6 us
    ppermute x15, waiting for transfers between devices, moved(): return lax.ppermute(x, 'bond', route)  9.93 us
  transfers between devices with their start and end apart: 20, of which 10 were waited for; matrix products, arithmetic and copies ran while one was open for 1% of the time, Pallas kernels for 67%

profile of v2, /device:TPU:0, one launch (start us, length us, event | category | flops | bytes accessed | tf_op | source)
XLA Modules:
  0.0 168.0 jit_solution(14339109939523296602)
XLA Ops:
  1.2 3.3 %cut_columns.2 = (f32[16,64,256]{2,1,0:T(8,128)}, f32[16,64,256]{2,1,0:T(8,128)}, f32[8,128]{1,0:T(8,128)S(1)}) custom-call(f32[64,16,512]{2,1,0:T(8,128)} %bitcast.31, f32[64,16,512]{2,1,0:T(8,128)} %bitcast.36), custom_call_target="tpu_custom_call" | custom-call | flops 30000001024 | bytes 1000 | tf_op jit(solution)/shard_map/cut_columns/pallas_call | solution.py:80
  4.6 2.9 %collective-permute-start.2 = (f32[16,64,256]{2,1,0:T(8,128)}, f32[16,64,256]{2,1,0:T(8,128)}, u32[]{:S(2)}, u32[]{:S(2)}) collective-permute-start(f32[16,64,256]{2,1,0:T(8,128)} %get-tuple-element.79.refs_1_), channel_id=1, source_target_pairs={{0,2},{1,3},{2,0},{3,1},{4,6},{5,7},{6,4},{7,5},{8,10},{9,11},{10,... | collective-permute-start | bytes 3145736 | tf_op jit(solution)/shard_map/ppermute | solution.py:378
  17.5 3.3 %cut_columns.3 = (f32[16,64,256]{2,1,0:T(8,128)}, f32[16,64,256]{2,1,0:T(8,128)}, f32[8,128]{1,0:T(8,128)S(1)}) custom-call(f32[8,128]{1,0:T(8,128)S(1)} %get-tuple-element.75.refs_0_, f32[64,16,512]{2,1,0:T(8,128)} %bitcast.32, f32[64,16,512]{2,1,0:T(8,128)} %bitcast.37), custom_call_target="tpu_custom_call" | custom-call | flops 30000001024 | bytes 1000 | tf_op jit(solution)/shard_map/cut_columns/pallas_call | solution.py:80
  20.8 4.1 %bra.2 = (bf16[4,512,512]{2,1,0:T(8,128)(2,1)S(1)}, bf16[4,512,512]{2,1,0:T(8,128)(2,1)S(1)}, f32[8,128]{1,0:T(8,128)S(1)}) custom-call(f32[8,128]{1,0:T(8,128)S(1)} %get-tuple-element.76.refs_0_, f32[512,4,512]{2,1,0:T(4,128)} %bitcast.24), custom_call_target="tpu_custom_call" | custom-call | flops 399999991808 | bytes 1000 | tf_op jit(solution)/shard_map/bra/pallas_call | solution.py:80
  24.9 5.4 %bra.3 = (bf16[4,512,512]{2,1,0:T(8,128)(2,1)S(1)}, bf16[4,512,512]{2,1,0:T(8,128)(2,1)S(1)}, f32[8,128]{1,0:T(8,128)S(1)}) custom-call(f32[8,128]{1,0:T(8,128)S(1)} %get-tuple-element.77.refs_0_, f32[512,4,512]{2,1,0:T(4,128)} %bitcast.29), custom_call_target="tpu_custom_call" | custom-call | flops 399999991808 | bytes 1000 | tf_op jit(solution)/shard_map/bra/pallas_call | solution.py:80
  35.5 10.1 %first_part.4 = (bf16[4,2048,256]{2,1,0:T(8,128)(2,1)}, bf16[4,2048,256]{2,1,0:T(8,128)(2,1)}, f32[8,128]{1,0:T(8,128)S(1)}) custom-call(f32[8,128]{1,0:T(8,128)S(1)} %get-tuple-element.81.refs_0_, f32[16,64,256]{2,1,0:T(8,128)} %get-tuple-element.79.refs_1_, f32[64,16,512]{2,1,0:T(8,128)} %collective-permute-done.refs_2_, ...), custom_call_target="tpu_custom_call" | custom-call | flops 1068000018432 | bytes 1000 | tf_op jit(solution)/shard_map/first_part/pallas_call | solution.py:80
  45.7 10.4 %first_part.5 = (bf16[4,2048,256]{2,1,0:T(8,128)(2,1)}, bf16[4,2048,256]{2,1,0:T(8,128)(2,1)}, f32[8,128]{1,0:T(8,128)S(1)}) custom-call(f32[8,128]{1,0:T(8,128)S(1)} %get-tuple-element.86.refs_0_, f32[16,64,256]{2,1,0:T(8,128)} %get-tuple-element.80.refs_1_, f32[64,16,512]{2,1,0:T(8,128)} %copy-done.16, f32[16,64,256]{2,1,0:T(8,128)} %get-tuple-element.87.refs_3_, ...), custom_call_target="tpu_custom_call" | custom-call | flops 1068000018432 | bytes 1000 | tf_op jit(solution)/shard_map/first_part/pallas_call | solution.py:80
  59.2 3.1 %collective-permute-done.8.refs_4_ = f32[16,64,256]{2,1,0:T(8,128)S(1)} collective-permute-done((f32[16,64,256]{2,1,0:T(8,128)}, f32[16,64,256]{2,1,0:T(8,128)S(1)}, u32[]{:S(2)}, u32[]{:S(2)}) %collective-permute-start.8) | collective-permute-done | bytes 1048608 | tf_op jit(solution)/shard_map/ppermute | solution.py:378
  62.2 8.9 %first_part.6 = (bf16[4,2048,256]{2,1,0:T(8,128)(2,1)S(1)}, bf16[4,2048,256]{2,1,0:T(8,128)(2,1)S(1)}, f32[8,128]{1,0:T(8,128)S(1)}) custom-call(f32[8,128]{1,0:T(8,128)S(1)} %get-tuple-element.94.refs_0_, f32[16,64,256]{2,1,0:T(8,128)} %get-tuple-element.92.refs_1_, f32[64,16,512]{2,1,0:T(8,128)} %collective-permute-done.refs_2_, ...), custom_call_target="tpu_custom_call" | custom-call | flops 1068000018432 | bytes 1000 | tf_op jit(solution)/shard_map/first_part/pallas_call | solution.py:80
  71.2 6.4 %second_part.10 = (f32[32,16,512]{2,1,0:T(8,128)}, f32[8,128]{1,0:T(8,128)S(1)}) custom-call(f32[8,128]{1,0:T(8,128)S(1)} %get-tuple-element.96.refs_0_, bf16[4,2048,256]{2,1,0:T(8,128)(2,1)} %get-tuple-element.97.refs_1_, bf16[4,2048,256]{2,1,0:T(8,128)(2,1)S(1)} %get-tuple-element.98.refs_2_, bf16[4,2048,256]{2,1,0:T(8,128)(2,1)} %get-tuple-element.99.refs_3_, ...), custom_call_target="tpu_custom_call" | custom-call | flops 3000000000 | bytes 1000 | tf_op jit(solution)/shard_map/second_part/pallas_call | solution.py:80
  79.4 9.1 %first_part.7 = (bf16[4,2048,256]{2,1,0:T(8,128)(2,1)S(1)}, bf16[4,2048,256]{2,1,0:T(8,128)(2,1)S(1)}, f32[8,128]{1,0:T(8,128)S(1)}) custom-call(f32[8,128]{1,0:T(8,128)S(1)} %get-tuple-element.103.refs_0_, f32[16,64,256]{2,1,0:T(8,128)} %get-tuple-element.93.refs_1_, f32[64,16,512]{2,1,0:T(8,128)} %copy-done.16, f32[16,64,256]{2,1,0:T(8,128)} %get-tuple-element.104.refs_3_, ...), custom_call_target="tpu_custom_call" | custom-call | flops 1068000018432 | bytes 1000 | tf_op jit(solution)/shard_map/first_part/pallas_call | solution.py:80
  88.5 3.1 %second_part.11 = (f32[16,16,512]{2,1,0:T(8,128)S(1)}, f32[8,128]{1,0:T(8,128)S(1)}) custom-call(f32[8,128]{1,0:T(8,128)S(1)} %get-tuple-element.105.refs_0_, bf16[4,2048,256]{2,1,0:T(8,128)(2,1)} %get-tuple-element.106.refs_1_, bf16[4,2048,256]{2,1,0:T(8,128)(2,1)S(1)} %get-tuple-element.107.refs_2_, bf16[4,2048,256]{2,1,0:T(8,128)(2,1)} %get-tuple-element.108.refs_3_, ...), custom_call_target="tpu_custom_call" | custom-call | flops 3000000000 | bytes 1000 | tf_op jit(solution)/shard_map/second_part/pallas_call | solution.py:80
  93.5 4.8 %second_part.12 = (f32[32,16,512]{2,1,0:T(8,128)S(1)}, f32[8,128]{1,0:T(8,128)S(1)}) custom-call(f32[8,128]{1,0:T(8,128)S(1)} %get-tuple-element.112.refs_0_, bf16[4,2048,256]{2,1,0:T(8,128)(2,1)} %get-tuple-element.97.refs_1_, bf16[4,2048,256]{2,1,0:T(8,128)(2,1)S(1)} %copy-done.1, bf16[4,2048,256]{2,1,0:T(8,128)(2,1)} %get-tuple-element.99.refs_3_, ...), custom_call_target="tpu_custom_call" | custom-call | flops 3000000000 | bytes 1000 | tf_op jit(solution)/shard_map/second_part/pallas_call | solution.py:80
  98.3 4.1 %second_part.13 = (f32[24,16,512]{2,1,0:T(8,128)S(1)}, f32[8,128]{1,0:T(8,128)S(1)}) custom-call(f32[8,128]{1,0:T(8,128)S(1)} %get-tuple-element.113.refs_0_, bf16[4,2048,256]{2,1,0:T(8,128)(2,1)} %get-tuple-element.106.refs_1_, bf16[4,2048,256]{2,1,0:T(8,128)(2,1)S(1)} %get-tuple-element.107.refs_2_, bf16[4,2048,256]{2,1,0:T(8,128)(2,1)} %get-tuple-element.108.refs_3_, ...), custom_call_target="tpu_custom_call" | custom-call | flops 3000000000 | bytes 1000 | tf_op jit(solution)/shard_map/second_part/pallas_call | solution.py:80
  104.4 5.0 %second_part.14 = (f32[32,16,512]{2,1,0:T(8,128)S(1)}, f32[8,128]{1,0:T(8,128)S(1)}) custom-call(f32[8,128]{1,0:T(8,128)S(1)} %get-tuple-element.114.refs_0_, bf16[4,2048,256]{2,1,0:T(8,128)(2,1)} %get-tuple-element.97.refs_1_, bf16[4,2048,256]{2,1,0:T(8,128)(2,1)S(1)} %copy-done.1, bf16[4,2048,256]{2,1,0:T(8,128)(2,1)} %get-tuple-element.99.refs_3_, ...), custom_call_target="tpu_custom_call" | custom-call | flops 3000000000 | bytes 1000 | tf_op jit(solution)/shard_map/second_part/pallas_call | solution.py:80
  109.5 3.6 %collective-permute-start.14 = (f32[32,16,512]{2,1,0:T(8,128)S(1)}, f32[32,16,512]{2,1,0:T(8,128)S(1)}, u32[]{:S(2)}, u32[]{:S(2)}) collective-permute-start(f32[32,16,512]{2,1,0:T(8,128)S(1)} %get-tuple-element.124), channel_id=1, source_target_pairs={{0,8},{8,16},{16,24},{1,9},{9,17},{17,25},{2,10},{10,18},{18,26},{... | collective-permute-start | bytes 3145736 | tf_op jit(solution)/shard_map/ppermute | solution.py:381
  113.0 3.0 %second_part.15 = (f32[16,16,512]{2,1,0:T(8,128)S(1)}, f32[8,128]{1,0:T(8,128)S(1)}) custom-call(f32[8,128]{1,0:T(8,128)S(1)} %get-tuple-element.116.refs_0_, bf16[4,2048,256]{2,1,0:T(8,128)(2,1)} %get-tuple-element.106.refs_1_, bf16[4,2048,256]{2,1,0:T(8,128)(2,1)S(1)} %get-tuple-element.107.refs_2_, bf16[4,2048,256]{2,1,0:T(8,128)(2,1)} %get-tuple-element.108.refs_3_, ...), custom_call_target="tpu_custom_call" | custom-call | flops 3000000000 | bytes 1000 | tf_op jit(solution)/shard_map/second_part/pallas_call | solution.py:80
  117.3 4.1 %second_part.16 = (f32[24,16,512]{2,1,0:T(8,128)S(1)}, f32[8,128]{1,0:T(8,128)S(1)}) custom-call(f32[8,128]{1,0:T(8,128)S(1)} %get-tuple-element.118.refs_0_, bf16[4,2048,256]{2,1,0:T(8,128)(2,1)} %get-tuple-element.106.refs_1_, bf16[4,2048,256]{2,1,0:T(8,128)(2,1)S(1)} %get-tuple-element.107.refs_2_, bf16[4,2048,256]{2,1,0:T(8,128)(2,1)} %get-tuple-element.108.refs_3_, ...), custom_call_target="tpu_custom_call" | custom-call | flops 3000000000 | bytes 1000 | tf_op jit(solution)/shard_map/second_part/pallas_call | solution.py:80
  122.3 4.1 %second_part.17 = (f32[24,16,512]{2,1,0:T(8,128)S(1)}, f32[8,128]{1,0:T(8,128)S(1)}) custom-call(f32[8,128]{1,0:T(8,128)S(1)} %get-tuple-element.119.refs_0_, bf16[4,2048,256]{2,1,0:T(8,128)(2,1)} %get-tuple-element.106.refs_1_, bf16[4,2048,256]{2,1,0:T(8,128)(2,1)S(1)} %get-tuple-element.107.refs_2_, bf16[4,2048,256]{2,1,0:T(8,128)(2,1)} %get-tuple-element.108.refs_3_, ...), custom_call_target="tpu_custom_call" | custom-call | flops 3000000000 | bytes 1000 | tf_op jit(solution)/shard_map/second_part/pallas_call | solution.py:80
  128.6 4.8 %second_part.18 = (f32[32,16,512]{2,1,0:T(8,128)S(1)}, f32[8,128]{1,0:T(8,128)S(1)}) custom-call(f32[8,128]{1,0:T(8,128)S(1)} %get-tuple-element.121.refs_0_, bf16[4,2048,256]{2,1,0:T(8,128)(2,1)} %get-tuple-element.97.refs_1_, bf16[4,2048,256]{2,1,0:T(8,128)(2,1)S(1)} %copy-done.1, bf16[4,2048,256]{2,1,0:T(8,128)(2,1)} %get-tuple-element.99.refs_3_, ...), custom_call_target="tpu_custom_call" | custom-call | flops 3000000000 | bytes 1000 | tf_op jit(solution)/shard_map/second_part/pallas_call | solution.py:80
  133.4 4.1 %collective-permute-start.18 = (f32[32,16,512]{2,1,0:T(8,128)S(1)}, f32[32,16,512]{2,1,0:T(8,128)S(1)}, u32[]{:S(2)}, u32[]{:S(2)}) collective-permute-start(f32[32,16,512]{2,1,0:T(8,128)S(1)} %get-tuple-element.133), channel_id=1, source_target_pairs={{0,8},{8,16},{16,24},{1,9},{9,17},{17,25},{2,10},{10,18},{18,26},{... | collective-permute-start | bytes 3145736 | tf_op jit(solution)/shard_map/ppermute | solution.py:381
  141.7 4.1 %second_part.19 = (f32[24,16,512]{2,1,0:T(8,128)S(1)}, f32[8,128]{1,0:T(8,128)S(1)}) custom-call(f32[8,128]{1,0:T(8,128)S(1)} %get-tuple-element.127.refs_0_, bf16[4,2048,256]{2,1,0:T(8,128)(2,1)} %get-tuple-element.106.refs_1_, bf16[4,2048,256]{2,1,0:T(8,128)(2,1)S(1)} %get-tuple-element.107.refs_2_, bf16[4,2048,256]{2,1,0:T(8,128)(2,1)} %get-tuple-element.108.refs_3_, ...), custom_call_target="tpu_custom_call" | custom-call | flops 3000000000 | bytes 1000 | tf_op jit(solution)/shard_map/second_part/pallas_call | solution.py:80
  149.1 9.7 %collective-permute-done.18.refs_2_ = f32[32,16,512]{2,1,0:T(8,128)S(1)} collective-permute-done((f32[32,16,512]{2,1,0:T(8,128)S(1)}, f32[32,16,512]{2,1,0:T(8,128)S(1)}, u32[]{:S(2)}, u32[]{:S(2)}) %collective-permute-start.18) | collective-permute-done | bytes 1048608 | tf_op jit(solution)/shard_map/ppermute | solution.py:381
  161.6 4.1 %collective-permute-done.19.refs_2_ = f32[24,16,512]{2,1,0:T(8,128)S(1)} collective-permute-done((f32[24,16,512]{2,1,0:T(8,128)S(1)}, f32[24,16,512]{2,1,0:T(8,128)S(1)}, u32[]{:S(2)}, u32[]{:S(2)}) %collective-permute-start.19) | collective-permute-done | bytes 786464 | tf_op jit(solution)/shard_map/ppermute | solution.py:381
  (85 shorter events, 41.2 us)
Async XLA Ops:
  0.6 9.9 %collective-permute-start = (f32[64,16,512]{2,1,0:T(8,128)}, f32[64,16,512]{2,1,0:T(8,128)}, u32[]{:S(2)}, u32[]{:S(2)}) collective-permute-start(f32[64,16,512]{2,1,0:T(8,128)} %bitcast.30), channel_id=1, source_target_pairs={{0,1},{1,0},{2,3},{3,2},{4,5},{5,4},{6,7},{7,6},{8,9},{9,8},{10,11... | collective-permute-start | bytes 6291464 | tf_op jit(solution)/shard_map/ppermute | solution.py:378
  1.2 9.4 %collective-permute-start.1 = (f32[64,16,512]{2,1,0:T(8,128)}, f32[64,16,512]{2,1,0:T(8,128)S(1)}, u32[]{:S(2)}, u32[]{:S(2)}) collective-permute-start(f32[64,16,512]{2,1,0:T(8,128)} %bitcast.35), channel_id=1, source_target_pairs={{0,1},{1,0},{2,3},{3,2},{4,5},{5,4},{6,7},{7,6},{8,9},{9,8},{10,11... | collective-permute-start | bytes 6291464 | tf_op jit(solution)/shard_map/ppermute | solution.py:378
  4.6 26.6 %collective-permute-start.2 = (f32[16,64,256]{2,1,0:T(8,128)}, f32[16,64,256]{2,1,0:T(8,128)}, u32[]{:S(2)}, u32[]{:S(2)}) collective-permute-start(f32[16,64,256]{2,1,0:T(8,128)} %get-tuple-element.79.refs_1_), channel_id=1, source_target_pairs={{0,2},{1,3},{2,0},{3,1},{4,6},{5,7},{6,4},{7,5},{8,10},{9,11},{10,... | collective-permute-start | bytes 3145736 | tf_op jit(solution)/shard_map/ppermute | solution.py:378
  7.4 25.2 %collective-permute-start.3 = (f32[16,64,256]{2,1,0:T(8,128)}, f32[16,64,256]{2,1,0:T(8,128)}, u32[]{:S(2)}, u32[]{:S(2)}) collective-permute-start(f32[16,64,256]{2,1,0:T(8,128)} %get-tuple-element.80.refs_1_), channel_id=1, source_target_pairs={{0,4},{1,5},{2,6},{3,7},{4,0},{5,1},{6,2},{7,3},{8,12},{9,13},{10,... | collective-permute-start | bytes 3145736 | tf_op jit(solution)/shard_map/ppermute | solution.py:378
  14.5 21.0 %copy-start.10 = (bf16[512,256]{1,0:T(8,128)(2,1)}, bf16[512,256]{1,0:T(8,128)(2,1)S(1)}, u32[]{:S(2)}) copy-start(bf16[512,256]{1,0:T(8,128)(2,1)S(1)} %get-tuple-element.83.refs_5_) | copy-start | bytes 786436
  14.5 21.0 %copy-start.12 = (bf16[512,256]{1,0:T(8,128)(2,1)}, bf16[512,256]{1,0:T(8,128)(2,1)S(1)}, u32[]{:S(2)}) copy-start(bf16[512,256]{1,0:T(8,128)(2,1)S(1)} %get-tuple-element.84.refs_6_) | copy-start | bytes 786436
  24.9 46.3 %copy-start.4 = (bf16[4,512,512]{2,1,0:T(8,128)(2,1)}, bf16[4,512,512]{2,1,0:T(8,128)(2,1)S(1)}, u32[]{:S(2)}) copy-start(bf16[4,512,512]{2,1,0:T(8,128)(2,1)S(1)} %get-tuple-element.101.refs_5_) | copy-start | bytes 6291460
  24.9 46.3 %copy-start.6 = (bf16[4,512,512]{2,1,0:T(8,128)(2,1)}, bf16[4,512,512]{2,1,0:T(8,128)(2,1)S(1)}, u32[]{:S(2)}) copy-start(bf16[4,512,512]{2,1,0:T(8,128)(2,1)S(1)} %get-tuple-element.102.refs_6_) | copy-start | bytes 6291460
  32.7 2.9 %collective-permute-start.4 = (f32[16,64,256]{2,1,0:T(8,128)}, f32[16,64,256]{2,1,0:T(8,128)S(1)}, u32[]{:S(2)}, u32[]{:S(2)}) collective-permute-start(f32[16,64,256]{2,1,0:T(8,128)} %get-tuple-element.82.refs_3_), channel_id=1, source_target_pairs={{0,1},{1,0},{2,3},{3,2},{4,5},{5,4},{6,7},{7,6},{8,9},{9,8},{10,11... | collective-permute-start | bytes 3145736 | tf_op jit(solution)/shard_map/ppermute | solution.py:378
  32.7 25.9 %collective-permute-start.6 = (f32[16,64,256]{2,1,0:T(8,128)}, f32[16,64,256]{2,1,0:T(8,128)}, u32[]{:S(2)}, u32[]{:S(2)}) collective-permute-start(f32[16,64,256]{2,1,0:T(8,128)} %get-tuple-element.92.refs_1_), channel_id=1, source_target_pairs={{0,2},{1,3},{2,0},{3,1},{4,6},{5,7},{6,4},{7,5},{8,10},{9,11},{10,... | collective-permute-start | bytes 3145736 | tf_op jit(solution)/shard_map/ppermute | solution.py:378
  33.0 25.6 %collective-permute-start.7 = (f32[16,64,256]{2,1,0:T(8,128)}, f32[16,64,256]{2,1,0:T(8,128)}, u32[]{:S(2)}, u32[]{:S(2)}) collective-permute-start(f32[16,64,256]{2,1,0:T(8,128)} %get-tuple-element.93.refs_1_), channel_id=1, source_target_pairs={{0,4},{1,5},{2,6},{3,7},{4,0},{5,1},{6,2},{7,3},{8,12},{9,13},{10,... | collective-permute-start | bytes 3145736 | tf_op jit(solution)/shard_map/ppermute | solution.py:378
  34.7 10.9 %collective-permute-start.5 = (f32[16,64,256]{2,1,0:T(8,128)}, f32[16,64,256]{2,1,0:T(8,128)}, u32[]{:S(2)}, u32[]{:S(2)}) collective-permute-start(f32[16,64,256]{2,1,0:T(8,128)} %get-tuple-element.87.refs_3_), channel_id=1, source_target_pairs={{0,1},{1,0},{2,3},{3,2},{4,5},{5,4},{6,7},{7,6},{8,9},{9,8},{10,11... | collective-permute-start | bytes 3145736 | tf_op jit(solution)/shard_map/ppermute | solution.py:378
  58.6 3.6 %collective-permute-start.8 = (f32[16,64,256]{2,1,0:T(8,128)}, f32[16,64,256]{2,1,0:T(8,128)S(1)}, u32[]{:S(2)}, u32[]{:S(2)}) collective-permute-start(f32[16,64,256]{2,1,0:T(8,128)} %get-tuple-element.95.refs_3_), channel_id=1, source_target_pairs={{0,1},{1,0},{2,3},{3,2},{4,5},{5,4},{6,7},{7,6},{8,9},{9,8},{10,11... | collective-permute-start | bytes 3145736 | tf_op jit(solution)/shard_map/ppermute | solution.py:378
  58.7 20.8 %collective-permute-start.9 = (f32[16,64,256]{2,1,0:T(8,128)}, f32[16,64,256]{2,1,0:T(8,128)}, u32[]{:S(2)}, u32[]{:S(2)}) collective-permute-start(f32[16,64,256]{2,1,0:T(8,128)} %get-tuple-element.104.refs_3_), channel_id=1, source_target_pairs={{0,1},{1,0},{2,3},{3,2},{4,5},{5,4},{6,7},{7,6},{8,9},{9,8},{10,11... | collective-permute-start | bytes 3145736 | tf_op jit(solution)/shard_map/ppermute | solution.py:378
  77.6 26.8 %collective-permute-start.10 = (f32[32,16,512]{2,1,0:T(8,128)}, f32[32,16,512]{2,1,0:T(8,128)}, u32[]{:S(2)}, u32[]{:S(2)}) collective-permute-start(f32[32,16,512]{2,1,0:T(8,128)} %get-tuple-element.115), channel_id=1, source_target_pairs={{0,4},{1,5},{2,6},{3,7},{4,0},{5,1},{6,2},{7,3},{8,12},{9,13},{10,... | collective-permute-start | bytes 3145736 | tf_op jit(solution)/shard_map/ppermute | solution.py:378
  91.7 21.3 %collective-permute-start.11 = (f32[16,16,512]{2,1,0:T(8,128)S(1)}, f32[16,16,512]{2,1,0:T(8,128)S(1)}, u32[]{:S(2)}, u32[]{:S(2)}) collective-permute-start(f32[16,16,512]{2,1,0:T(8,128)S(1)} %get-tuple-element.117), channel_id=1, source_target_pairs={{0,2},{1,3},{2,0},{3,1},{4,6},{5,7},{6,4},{7,5},{8,10},{9,11},{10,... | collective-permute-start | bytes 1572872 | tf_op jit(solution)/shard_map/ppermute | solution.py:378
  102.4 19.9 %collective-permute-start.12 = (f32[24,16,512]{2,1,0:T(8,128)S(1)}, f32[24,16,512]{2,1,0:T(8,128)S(1)}, u32[]{:S(2)}, u32[]{:S(2)}) collective-permute-start(f32[24,16,512]{2,1,0:T(8,128)S(1)} %get-tuple-element.120), channel_id=1, source_target_pairs={{0,2},{1,3},{2,0},{3,1},{4,6},{5,7},{6,4},{7,5},{8,10},{9,11},{10,... | collective-permute-start | bytes 2359304 | tf_op jit(solution)/shard_map/ppermute | solution.py:378
  104.0 24.6 %collective-permute-start.13 = (f32[32,16,512]{2,1,0:T(8,128)S(1)}, f32[32,16,512]{2,1,0:T(8,128)S(1)}, u32[]{:S(2)}, u32[]{:S(2)}) collective-permute-start(f32[32,16,512]{2,1,0:T(8,128)S(1)} %get-tuple-element.122), channel_id=1, source_target_pairs={{0,4},{1,5},{2,6},{3,7},{4,0},{5,1},{6,2},{7,3},{8,12},{9,13},{10,... | collective-permute-start | bytes 3145736 | tf_op jit(solution)/shard_map/ppermute | solution.py:378
  109.5 28.1 %collective-permute-start.14 = (f32[32,16,512]{2,1,0:T(8,128)S(1)}, f32[32,16,512]{2,1,0:T(8,128)S(1)}, u32[]{:S(2)}, u32[]{:S(2)}) collective-permute-start(f32[32,16,512]{2,1,0:T(8,128)S(1)} %get-tuple-element.124), channel_id=1, source_target_pairs={{0,8},{8,16},{16,24},{1,9},{9,17},{17,25},{2,10},{10,18},{18,26},{... | collective-permute-start | bytes 3145736 | tf_op jit(solution)/shard_map/ppermute | solution.py:381
  116.0 24.3 %collective-permute-start.15 = (f32[16,16,512]{2,1,0:T(8,128)S(1)}, f32[16,16,512]{2,1,0:T(8,128)S(1)}, u32[]{:S(2)}, u32[]{:S(2)}) collective-permute-start(f32[16,16,512]{2,1,0:T(8,128)S(1)} %get-tuple-element.126), channel_id=1, source_target_pairs={{8,0},{16,8},{24,16},{9,1},{17,9},{25,17},{10,2},{18,10},{26,18},{... | collective-permute-start | bytes 1572872 | tf_op jit(solution)/shard_map/ppermute | solution.py:381
  121.4 20.3 %collective-permute-start.16 = (f32[24,16,512]{2,1,0:T(8,128)S(1)}, f32[24,16,512]{2,1,0:T(8,128)S(1)}, u32[]{:S(2)}, u32[]{:S(2)}) collective-permute-start(f32[24,16,512]{2,1,0:T(8,128)S(1)} %get-tuple-element.128), channel_id=1, source_target_pairs={{0,2},{1,3},{2,0},{3,1},{4,6},{5,7},{6,4},{7,5},{8,10},{9,11},{10,... | collective-permute-start | bytes 2359304 | tf_op jit(solution)/shard_map/ppermute | solution.py:378
  126.4 21.3 %collective-permute-start.17 = (f32[24,16,512]{2,1,0:T(8,128)S(1)}, f32[24,16,512]{2,1,0:T(8,128)S(1)}, u32[]{:S(2)}, u32[]{:S(2)}) collective-permute-start(f32[24,16,512]{2,1,0:T(8,128)S(1)} %get-tuple-element.130), channel_id=1, source_target_pairs={{8,0},{16,8},{24,16},{9,1},{17,9},{25,17},{10,2},{18,10},{26,18},{... | collective-permute-start | bytes 2359304 | tf_op jit(solution)/shard_map/ppermute | solution.py:381
  133.4 25.5 %collective-permute-start.18 = (f32[32,16,512]{2,1,0:T(8,128)S(1)}, f32[32,16,512]{2,1,0:T(8,128)S(1)}, u32[]{:S(2)}, u32[]{:S(2)}) collective-permute-start(f32[32,16,512]{2,1,0:T(8,128)S(1)} %get-tuple-element.133), channel_id=1, source_target_pairs={{0,8},{8,16},{16,24},{1,9},{9,17},{17,25},{2,10},{10,18},{18,26},{... | collective-permute-start | bytes 3145736 | tf_op jit(solution)/shard_map/ppermute | solution.py:381
  145.8 19.9 %collective-permute-start.19 = (f32[24,16,512]{2,1,0:T(8,128)S(1)}, f32[24,16,512]{2,1,0:T(8,128)S(1)}, u32[]{:S(2)}, u32[]{:S(2)}) collective-permute-start(f32[24,16,512]{2,1,0:T(8,128)S(1)} %get-tuple-element.137), channel_id=1, source_target_pairs={{8,0},{16,8},{24,16},{9,1},{17,9},{25,17},{10,2},{18,10},{26,18},{... | collective-permute-start | bytes 2359304 | tf_op jit(solution)/shard_map/ppermute | solution.py:381
  (13 other events, 70.0 us)

commit v3 on v2

--- a/solution.py
+++ b/solution.py
@@ -9,7 +9,7 @@
 
 F32 = jnp.float32
 BF16 = jnp.bfloat16
-VMEM_BYTES = 27 << 20
+VMEM_BYTES = 22 << 20
 FLOPS_A_US = 10**11
 
 
@@ -180,7 +180,7 @@
         (depth // step,),
         [pl.BlockSpec((step, states, wide), lambda i: (i, 0, 0))],
         [(spec, out)] * 2,
-        [in_hbm(tensor)],
+        [tensor],
         after=after,
         about_us=4,
     )
@@ -271,12 +271,12 @@
                     yl[t, to] = l[t * size : (t + 1) * size, j * wide : (j + 1) * wide]
 
 
-def first_part(turns, own, near, far, start, ket, op, states, b_at, b_count):
+def first_part(turns, own, near, far, start, ket, op, states, b_at, b_count, stays):
     width, rows, wide = own.shape
     made, depth = b_count * states, ket[0].shape[1]
     steps = 4
     shape = (states, made // states * width, wide)
-    out = like(shape, BF16) if start else pltpu.HBM(shape, BF16)
+    out = like(shape, BF16) if stays else pltpu.HBM(shape, BF16)
     halves = 2 if width % 16 == 0 else 1
     here = width // halves
     spec = pl.BlockSpec((states, out.shape[1] // steps, wide), lambda i: (0, jnp.maximum(i - halves, 0), 0))
@@ -293,7 +293,7 @@
         scratch=[pltpu.VMEM((width, 2 * made, wide), BF16)],
         about_us=3 + 0.03 * wide,
     )
-    return (h, l, b_at) if start else (in_hbm(h), in_hbm(l), b_at)
+    return (h, l, b_at) if stays else (in_hbm(h), in_hbm(l), b_at)
 
 
 def second_kernel(n, *refs):
@@ -306,9 +306,13 @@
     out[...] = total
 
 
-def second_part(turns, pieces, bra, start, count, width, more):
+def second_part(turns, pieces, bra, start, count, width, more, only=None):
     states, depth, columns = bra[0].shape
     pieces = [p for p in pieces if p[2] <= start < p[2] + p[0].shape[1] // width]
+    if only is not None:
+        pieces = pieces[only : only + 1]
+        depth = pieces[0][0].shape[2]
+    bra_spec = pl.BlockSpec((states, depth, columns), lambda i: (0, only or 0, 0))
     yhs = [h for h, _, _ in pieces]
     yls = [l for _, l, _ in pieces]
     block = next(b for b in range(min(count, 24), 0, -1) if start % b == 0 and count % b == 0)
@@ -321,7 +325,7 @@
         functools.partial(second_kernel, len(pieces)),
         "second_part",
         (count // block,),
-        [y_spec(y, base) for y, (_, _, base) in zip((*yhs, *yls), pieces * 2)] + [whole(x) for x in bra] + [spec] * len(more),
+        [y_spec(y, base) for y, (_, _, base) in zip((*yhs, *yls), pieces * 2)] + [bra_spec] * 2 + [spec] * len(more),
         [(spec, like((count, width, columns), F32))],
         [*yhs, *yls, *bra, *more],
         about_us=3e-2,
@@ -428,13 +432,19 @@
 
         def first(self, j, far, b_at, b_count):
             args = self.own[j], self.near, far, sum(cuts[:j]), self.ket, self.operator, states
-            self.done.append(first_part(turns, *args, b_at, b_count))
+            self.done.append(first_part(turns, *args, b_at, b_count, j > 0 or self.distance < 0))
+
+        def begin(self):
+            starts = [(k - 1) * rows for k in range(1, self.others)]
+            args = self.done, self.bra
+            self.begun = [second_part(turns, *args, at, self.pieces[0], width, [], 0) for at in starts]
 
         def send(self, j):
             got = []
             for k in range(1, self.others):
                 start = (k - 1) * rows + sum(self.pieces[:j])
-                x = second_part(turns, self.done, self.bra, start, self.pieces[j], width, [])
+                more, only = ([], None) if j else ([self.begun[k - 1]], 1)
+                x = second_part(turns, self.done, self.bra, start, self.pieces[j], width, more, only)
                 got.append(moved(x, **{self.reduce: k}))
             self.sent.append(got)
 
@@ -462,12 +472,8 @@
             side.own.append(x)
             far[side, j] = side.gather_far(x)
 
-    def share(j):
-        arrived = [*far[left, j], *far[right, j]]
-        arrived = turns.take(*arrived)
-        count = len(far[left, j])
-        far[left, j] = left.share(arrived[:count])
-        far[right, j] = right.share(arrived[count:])
+    def share(j, side):
+        far[side, j] = side.share(turns.take(*far[side, j]))
 
     def first(side, j):
         side.first(j, far[side, j], 0, side.others * rows)
@@ -480,10 +486,14 @@
     gather(1)
     for side in both:
         side.prepare_bra([])
-    share(0)
+    share(0, left)
+    share(0, right)
     first(left, 0)
     first(right, 0)
-    share(1)
+    share(1, left)
+    left.begin()
+    share(1, right)
+    right.begin()
     first(left, 1)
     left.send(0)
     first(right, 1)

time: 169 us -> 162 us (0.959)
  Pallas kernels: 114 us -> 104 us
  local copies, waits for them, and re-layouts: 2.85 us -> 5.54 us
  starting transfers between devices: 25.2 us -> 27.5 us
  waiting for transfers between devices: 24.3 us -> 22.4 us
    pallas_call x29 -> x33, Pallas kernels: 114 us -> 104 us  [call(): pl.pallas_call(inner, name=name, grid_spec=pltpu.PrefetchScalarGridSpec(n...]
    unnamed x34 -> x70, local copies, waits for them, and re-layouts: 1.62 us -> 4.31 us
    ppermute x15, starting transfers between devices: 13.6 us -> 15.7 us  [moved(): return lax.ppermute(x, 'bond', route)]
  transfers between devices with their start and end apart: 20 -> 20, of which waited for: 10 -> 8; matrix products, arithmetic and copies ran while one was open for 1% -> 1% of each run, Pallas kernels for 67% -> 63%
where the time goes in v3:
time: 162 us; the launch traced here: 161 us
  Pallas kernels  104 us (64%)
  starting transfers between devices  27.5 us (17%)
  waiting for transfers between devices  22.4 us (14%)
  local copies, waits for them, and re-layouts  5.54 us (3%)
    pallas_call x33, Pallas kernels, call(): pl.pallas_call(inner, name=name, grid_spec=pltpu.PrefetchScalarGridSpec(n...  104 us
    ppermute x15, starting transfers between devices, moved(): return lax.ppermute(x, 'bond', route)  15.7 us
    ppermute x5, waiting for transfers between devices, handed(): lax.ppermute(x, 'site', [(k, k + distance) for k in range(chain) if 0 <=...  13.8 us
    ppermute x5, starting transfers between devices, handed(): lax.ppermute(x, 'site', [(k, k + distance) for k in range(chain) if 0 <=...  11.8 us
    ppermute x15, waiting for transfers between devices, moved(): return lax.ppermute(x, 'bond', route)  8.6 us
    unnamed x70, local copies, waits for them, and re-layouts  4.31 us
  transfers between devices with their start and end apart: 20, of which 8 were waited for; matrix products, arithmetic and copies ran while one was open for 1% of the time, Pallas kernels for 63%

profile of v3, /device:TPU:0, one launch (start us, length us, event | category | flops | bytes accessed | tf_op | source)
XLA Modules:
  0.0 161.2 jit_solution(2649553549886829874)
XLA Ops:
  1.2 3.3 %cut_columns.2 = (f32[16,64,256]{2,1,0:T(8,128)}, f32[16,64,256]{2,1,0:T(8,128)}, f32[8,128]{1,0:T(8,128)S(1)}) custom-call(f32[64,16,512]{2,1,0:T(8,128)} %bitcast.31, f32[64,16,512]{2,1,0:T(8,128)} %bitcast.36), custom_call_target="tpu_custom_call" | custom-call | flops 30000001024 | bytes 1000 | tf_op jit(solution)/shard_map/cut_columns/pallas_call | solution.py:80
  4.6 2.9 %collective-permute-start.2 = (f32[16,64,256]{2,1,0:T(8,128)}, f32[16,64,256]{2,1,0:T(8,128)}, u32[]{:S(2)}, u32[]{:S(2)}) collective-permute-start(f32[16,64,256]{2,1,0:T(8,128)} %get-tuple-element.85.refs_1_), channel_id=1, source_target_pairs={{0,2},{1,3},{2,0},{3,1},{4,6},{5,7},{6,4},{7,5},{8,10},{9,11},{10,... | collective-permute-start | bytes 3145736 | tf_op jit(solution)/shard_map/ppermute | solution.py:382
  14.9 2.6 %ket.3 = (bf16[512,256]{1,0:T(8,128)(2,1)S(1)}, bf16[512,256]{1,0:T(8,128)(2,1)S(1)}, f32[8,128]{1,0:T(8,128)S(1)}) custom-call(s32[14]{0:T(128)S(1)} %dynamic-slice_bitcast_fusion.refs_0_, f32[8,128]{1,0:T(8,128)S(1)} %get-tuple-element.80.refs_1_, f32[512,4,512]{2,1,0:T(4,128)} %bitcast.23, f32[512,4,512]{2,1,0:T(4,128)} %bitcast.24, ...), custom_call_target="tpu_custom_call" | custom-call | flops 269999996928 | bytes 1000 | tf_op jit(solution)/shard_map/ket/pallas_call | solution.py:80
  17.5 3.5 %cut_columns.3 = (f32[16,64,256]{2,1,0:T(8,128)}, f32[16,64,256]{2,1,0:T(8,128)}, f32[8,128]{1,0:T(8,128)S(1)}) custom-call(f32[8,128]{1,0:T(8,128)S(1)} %get-tuple-element.81.refs_0_, f32[64,16,512]{2,1,0:T(8,128)} %bitcast.32, f32[64,16,512]{2,1,0:T(8,128)} %bitcast.37), custom_call_target="tpu_custom_call" | custom-call | flops 30000001024 | bytes 1000 | tf_op jit(solution)/shard_map/cut_columns/pallas_call | solution.py:80
  27.3 4.4 %collective-permute-done.2.refs_1_ = f32[16,64,256]{2,1,0:T(8,128)} collective-permute-done((f32[16,64,256]{2,1,0:T(8,128)}, f32[16,64,256]{2,1,0:T(8,128)}, u32[]{:S(2)}, u32[]{:S(2)}) %collective-permute-start.2) | collective-permute-done | bytes 1048608 | tf_op jit(solution)/shard_map/ppermute | solution.py:382
  34.6 10.2 %first_part.4 = (bf16[4,2048,256]{2,1,0:T(8,128)(2,1)}, bf16[4,2048,256]{2,1,0:T(8,128)(2,1)}, f32[8,128]{1,0:T(8,128)S(1)}) custom-call(f32[8,128]{1,0:T(8,128)S(1)} %get-tuple-element.88.refs_0_, f32[16,64,256]{2,1,0:T(8,128)} %get-tuple-element.85.refs_1_, f32[64,16,512]{2,1,0:T(8,128)} %collective-permute-done.refs_2_, ...), custom_call_target="tpu_custom_call" | custom-call | flops 1068000018432 | bytes 1000 | tf_op jit(solution)/shard_map/first_part/pallas_call | solution.py:80
  44.8 9.1 %first_part.5 = (bf16[4,2048,256]{2,1,0:T(8,128)(2,1)S(1)}, bf16[4,2048,256]{2,1,0:T(8,128)(2,1)S(1)}, f32[8,128]{1,0:T(8,128)S(1)}) custom-call(f32[8,128]{1,0:T(8,128)S(1)} %get-tuple-element.93.refs_0_, f32[16,64,256]{2,1,0:T(8,128)} %get-tuple-element.87.refs_1_, f32[64,16,512]{2,1,0:T(8,128)} %copy-done.34, f32[16,64,256]{2,1,0:T(8,128)} %get-tuple-element.94.refs_3_, ...), custom_call_target="tpu_custom_call" | custom-call | flops 1068000018432 | bytes 1000 | tf_op jit(solution)/shard_map/first_part/pallas_call | solution.py:80
  54.2 4.1 %second_part.12 = (f32[32,16,512]{2,1,0:T(8,128)S(1)}, f32[8,128]{1,0:T(8,128)S(1)}) custom-call(f32[8,128]{1,0:T(8,128)S(1)} %get-tuple-element.100.refs_0_, bf16[4,2048,256]{2,1,0:T(8,128)(2,1)} %get-tuple-element.101.refs_1_, bf16[4,2048,256]{2,1,0:T(8,128)(2,1)} %get-tuple-element.102.refs_2_.refs_3_, ...), custom_call_target="tpu_custom_call" | custom-call | flops 3000000000 | bytes 1000 | tf_op jit(solution)/shard_map/second_part/pallas_call | solution.py:80
  59.8 9.0 %first_part.6 = (bf16[4,2048,256]{2,1,0:T(8,128)(2,1)S(1)}, bf16[4,2048,256]{2,1,0:T(8,128)(2,1)S(1)}, f32[8,128]{1,0:T(8,128)S(1)}) custom-call(f32[8,128]{1,0:T(8,128)S(1)} %get-tuple-element.112.refs_0_, f32[16,64,256]{2,1,0:T(8,128)} %get-tuple-element.99.refs_1_, f32[64,16,512]{2,1,0:T(8,128)} %collective-permute-done.refs_2_, ...), custom_call_target="tpu_custom_call" | custom-call | flops 1068000018432 | bytes 1000 | tf_op jit(solution)/shard_map/first_part/pallas_call | solution.py:80
  68.9 3.3 %second_part.14 = (f32[32,16,512]{2,1,0:T(8,128)}, f32[8,128]{1,0:T(8,128)S(1)}) custom-call(f32[8,128]{1,0:T(8,128)S(1)} %get-tuple-element.114.refs_0_, bf16[4,2048,256]{2,1,0:T(8,128)(2,1)S(1)} %get-tuple-element.115.refs_1_.refs_2_, bf16[4,2048,256]{2,1,0:T(8,128)(2,1)S(1)} %get-tuple-element.116.refs_2_.refs_4_, bf16[4,512,512]{2,1,0:T(8,128)(2,1)S(1)} %copy-done.9, ...), custom_call_target="tpu_custom_call" | custom-call | flops 3000000000 | bytes 1000 | tf_op jit(solution)/shard_map/second_part/pallas_call | solution.py:80
  74.3 9.2 %first_part.7 = (bf16[4,2048,256]{2,1,0:T(8,128)(2,1)S(1)}, bf16[4,2048,256]{2,1,0:T(8,128)(2,1)S(1)}, f32[8,128]{1,0:T(8,128)S(1)}) custom-call(f32[8,128]{1,0:T(8,128)S(1)} %get-tuple-element.118.refs_0_, f32[16,64,256]{2,1,0:T(8,128)} %get-tuple-element.106.refs_1_, f32[64,16,512]{2,1,0:T(8,128)} %copy-done.34, ...), custom_call_target="tpu_custom_call" | custom-call | flops 1068000018432 | bytes 1000 | tf_op jit(solution)/shard_map/first_part/pallas_call | solution.py:80
  86.9 4.9 %second_part.16 = (f32[32,16,512]{2,1,0:T(8,128)S(1)}, f32[8,128]{1,0:T(8,128)S(1)}) custom-call(f32[8,128]{1,0:T(8,128)S(1)} %get-tuple-element.124.refs_0_, bf16[4,2048,256]{2,1,0:T(8,128)(2,1)} %get-tuple-element.101.refs_1_, bf16[4,2048,256]{2,1,0:T(8,128)(2,1)S(1)} %copy-done.7, bf16[4,2048,256]{2,1,0:T(8,128)(2,1)} %get-tuple-element.102.refs_2_.refs_3_, ...), custom_call_target="tpu_custom_call" | custom-call | flops 3000000000 | bytes 1000 | tf_op jit(solution)/shard_map/second_part/pallas_call | solution.py:80
  91.9 3.2 %second_part.17 = (f32[24,16,512]{2,1,0:T(8,128)S(1)}, f32[8,128]{1,0:T(8,128)S(1)}) custom-call(f32[8,128]{1,0:T(8,128)S(1)} %get-tuple-element.125.refs_0_, bf16[4,2048,256]{2,1,0:T(8,128)(2,1)S(1)} %copy-done.1, bf16[4,2048,256]{2,1,0:T(8,128)(2,1)S(1)} %get-tuple-element.121.refs_1_.refs_2_, bf16[4,2048,256]{2,1,0:T(8,128)(2,1)S(1)} %copy-done.3, ...), custom_call_target="tpu_custom_call" | custom-call | flops 3000000000 | bytes 1000 | tf_op jit(solution)/shard_map/second_part/pallas_call | solution.py:80
  98.0 5.0 %second_part.18 = (f32[32,16,512]{2,1,0:T(8,128)S(1)}, f32[8,128]{1,0:T(8,128)S(1)}) custom-call(f32[8,128]{1,0:T(8,128)S(1)} %get-tuple-element.126.refs_0_, bf16[4,2048,256]{2,1,0:T(8,128)(2,1)} %get-tuple-element.101.refs_1_, bf16[4,2048,256]{2,1,0:T(8,128)(2,1)S(1)} %copy-done.7, bf16[4,2048,256]{2,1,0:T(8,128)(2,1)} %get-tuple-element.102.refs_2_.refs_3_, ...), custom_call_target="tpu_custom_call" | custom-call | flops 3000000000 | bytes 1000 | tf_op jit(solution)/shard_map/second_part/pallas_call | solution.py:80
  103.0 3.8 %collective-permute-start.14 = (f32[32,16,512]{2,1,0:T(8,128)S(1)}, f32[32,16,512]{2,1,0:T(8,128)S(1)}, u32[]{:S(2)}, u32[]{:S(2)}) collective-permute-start(f32[32,16,512]{2,1,0:T(8,128)S(1)} %get-tuple-element.136), channel_id=1, source_target_pairs={{0,8},{8,16},{16,24},{1,9},{9,17},{17,25},{2,10},{10,18},{18,26},{... | collective-permute-start | bytes 3145736 | tf_op jit(solution)/shard_map/ppermute | solution.py:385
  110.7 3.2 %second_part.20 = (f32[24,16,512]{2,1,0:T(8,128)S(1)}, f32[8,128]{1,0:T(8,128)S(1)}) custom-call(f32[8,128]{1,0:T(8,128)S(1)} %get-tuple-element.130.refs_0_, bf16[4,2048,256]{2,1,0:T(8,128)(2,1)S(1)} %copy-done.1, bf16[4,2048,256]{2,1,0:T(8,128)(2,1)S(1)} %get-tuple-element.121.refs_1_.refs_2_, bf16[4,2048,256]{2,1,0:T(8,128)(2,1)S(1)} %copy-done.3, ...), custom_call_target="tpu_custom_call" | custom-call | flops 3000000000 | bytes 1000 | tf_op jit(solution)/shard_map/second_part/pallas_call | solution.py:80
  115.7 3.2 %second_part.21 = (f32[24,16,512]{2,1,0:T(8,128)S(1)}, f32[8,128]{1,0:T(8,128)S(1)}) custom-call(f32[8,128]{1,0:T(8,128)S(1)} %get-tuple-element.131.refs_0_, bf16[4,2048,256]{2,1,0:T(8,128)(2,1)S(1)} %copy-done.1, bf16[4,2048,256]{2,1,0:T(8,128)(2,1)S(1)} %get-tuple-element.121.refs_1_.refs_2_, bf16[4,2048,256]{2,1,0:T(8,128)(2,1)S(1)} %copy-done.3, ...), custom_call_target="tpu_custom_call" | custom-call | flops 3000000000 | bytes 1000 | tf_op jit(solution)/shard_map/second_part/pallas_call | solution.py:80
  121.3 4.8 %second_part.22 = (f32[32,16,512]{2,1,0:T(8,128)S(1)}, f32[8,128]{1,0:T(8,128)S(1)}) custom-call(f32[8,128]{1,0:T(8,128)S(1)} %get-tuple-element.133.refs_0_, bf16[4,2048,256]{2,1,0:T(8,128)(2,1)} %get-tuple-element.101.refs_1_, bf16[4,2048,256]{2,1,0:T(8,128)(2,1)S(1)} %copy-done.7, bf16[4,2048,256]{2,1,0:T(8,128)(2,1)} %get-tuple-element.102.refs_2_.refs_3_, ...), custom_call_target="tpu_custom_call" | custom-call | flops 3000000000 | bytes 1000 | tf_op jit(solution)/shard_map/second_part/pallas_call | solution.py:80
  126.1 4.2 %collective-permute-start.18 = (f32[32,16,512]{2,1,0:T(8,128)S(1)}, f32[32,16,512]{2,1,0:T(8,128)S(1)}, u32[]{:S(2)}, u32[]{:S(2)}) collective-permute-start(f32[32,16,512]{2,1,0:T(8,128)S(1)} %get-tuple-element.145), channel_id=1, source_target_pairs={{0,8},{8,16},{16,24},{1,9},{9,17},{17,25},{2,10},{10,18},{18,26},{... | collective-permute-start | bytes 3145736 | tf_op jit(solution)/shard_map/ppermute | solution.py:385
  130.3 2.7 %place.5 = (f32[64,16,512]{2,1,0:T(8,128)}, f32[8,128]{1,0:T(8,128)S(1)}) custom-call(s32[14]{0:T(128)S(1)} %copy-done.19, f32[8,128]{1,0:T(8,128)S(1)} %get-tuple-element.135.refs_1_, f32[32,16,512]{2,1,0:T(8,128)S(1)} %collective-permute-done.14.refs_2_, f32[64,16,512]{2,1,0:T(8,128)} %bitcast.33), custom_call_target="tpu_custom_call" | custom-call | flops 10000000000 | bytes 1000 | tf_op jit(solution)/shard_map/place/pallas_call | solution.py:80
  136.3 3.2 %second_part.23 = (f32[24,16,512]{2,1,0:T(8,128)S(1)}, f32[8,128]{1,0:T(8,128)S(1)}) custom-call(f32[8,128]{1,0:T(8,128)S(1)} %get-tuple-element.139.refs_0_, bf16[4,2048,256]{2,1,0:T(8,128)(2,1)S(1)} %copy-done.1, bf16[4,2048,256]{2,1,0:T(8,128)(2,1)S(1)} %get-tuple-element.121.refs_1_.refs_2_, bf16[4,2048,256]{2,1,0:T(8,128)(2,1)S(1)} %copy-done.3, ...), custom_call_target="tpu_custom_call" | custom-call | flops 3000000000 | bytes 1000 | tf_op jit(solution)/shard_map/second_part/pallas_call | solution.py:80
  142.7 8.4 %collective-permute-done.18.refs_2_ = f32[32,16,512]{2,1,0:T(8,128)S(1)} collective-permute-done((f32[32,16,512]{2,1,0:T(8,128)S(1)}, f32[32,16,512]{2,1,0:T(8,128)S(1)}, u32[]{:S(2)}, u32[]{:S(2)}) %collective-permute-start.18) | collective-permute-done | bytes 1048608 | tf_op jit(solution)/shard_map/ppermute | solution.py:385
  151.1 2.7 %place.8 = (f32[64,16,512]{2,1,0:T(8,128)}, f32[8,128]{1,0:T(8,128)S(1)}) custom-call(s32[14]{0:T(128)S(1)} %copy-done.19, f32[8,128]{1,0:T(8,128)S(1)} %get-tuple-element.144.refs_1_, f32[32,16,512]{2,1,0:T(8,128)S(1)} %collective-permute-done.18.refs_2_, f32[64,16,512]{2,1,0:T(8,128)} %bitcast.34, ...), custom_call_target="tpu_custom_call", output_to_operand_aliasing={{0}: (4, {})} | custom-call | flops 10000000000 | bytes 1000 | tf_op jit(solution)/shard_map/place/pallas_call | solution.py:80
  153.8 5.1 %collective-permute-done.19.refs_2_ = f32[24,16,512]{2,1,0:T(8,128)S(1)} collective-permute-done((f32[24,16,512]{2,1,0:T(8,128)S(1)}, f32[24,16,512]{2,1,0:T(8,128)S(1)}, u32[]{:S(2)}, u32[]{:S(2)}) %collective-permute-start.19) | collective-permute-done | bytes 786464 | tf_op jit(solution)/shard_map/ppermute | solution.py:385
  (125 shorter events, 43.6 us)
Async XLA Ops:
  0.6 9.9 %collective-permute-start = (f32[64,16,512]{2,1,0:T(8,128)}, f32[64,16,512]{2,1,0:T(8,128)}, u32[]{:S(2)}, u32[]{:S(2)}) collective-permute-start(f32[64,16,512]{2,1,0:T(8,128)} %bitcast.30), channel_id=1, source_target_pairs={{0,1},{1,0},{2,3},{3,2},{4,5},{5,4},{6,7},{7,6},{8,9},{9,8},{10,11... | collective-permute-start | bytes 6291464 | tf_op jit(solution)/shard_map/ppermute | solution.py:382
  1.2 9.4 %collective-permute-start.1 = (f32[64,16,512]{2,1,0:T(8,128)}, f32[64,16,512]{2,1,0:T(8,128)S(1)}, u32[]{:S(2)}, u32[]{:S(2)}) collective-permute-start(f32[64,16,512]{2,1,0:T(8,128)} %bitcast.35), channel_id=1, source_target_pairs={{0,1},{1,0},{2,3},{3,2},{4,5},{5,4},{6,7},{7,6},{8,9},{9,8},{10,11... | collective-permute-start | bytes 6291464 | tf_op jit(solution)/shard_map/ppermute | solution.py:382
  4.6 27.1 %collective-permute-start.2 = (f32[16,64,256]{2,1,0:T(8,128)}, f32[16,64,256]{2,1,0:T(8,128)}, u32[]{:S(2)}, u32[]{:S(2)}) collective-permute-start(f32[16,64,256]{2,1,0:T(8,128)} %get-tuple-element.85.refs_1_), channel_id=1, source_target_pairs={{0,2},{1,3},{2,0},{3,1},{4,6},{5,7},{6,4},{7,5},{8,10},{9,11},{10,... | collective-permute-start | bytes 3145736 | tf_op jit(solution)/shard_map/ppermute | solution.py:382
  7.5 26.4 %collective-permute-start.3 = (f32[16,64,256]{2,1,0:T(8,128)}, f32[16,64,256]{2,1,0:T(8,128)}, u32[]{:S(2)}, u32[]{:S(2)}) collective-permute-start(f32[16,64,256]{2,1,0:T(8,128)} %get-tuple-element.87.refs_1_), channel_id=1, source_target_pairs={{0,4},{1,5},{2,6},{3,7},{4,0},{5,1},{6,2},{7,3},{8,12},{9,13},{10,... | collective-permute-start | bytes 3145736 | tf_op jit(solution)/shard_map/ppermute | solution.py:382
  14.8 30.0 %copy-start.20 = (bf16[256,256]{1,0:T(8,128)(2,1)}, bf16[256,256]{1,0:T(8,128)(2,1)S(1)}, u32[]{:S(2)}) copy-start(bf16[256,256]{1,0:T(8,128)(2,1)S(1)} %get-tuple-element.97.refs_7_) | copy-start | bytes 393220
  21.1 32.9 %collective-permute-start.6 = (f32[16,64,256]{2,1,0:T(8,128)}, f32[16,64,256]{2,1,0:T(8,128)}, u32[]{:S(2)}, u32[]{:S(2)}) collective-permute-start(f32[16,64,256]{2,1,0:T(8,128)} %get-tuple-element.99.refs_1_), channel_id=1, source_target_pairs={{0,2},{1,3},{2,0},{3,1},{4,6},{5,7},{6,4},{7,5},{8,10},{9,11},{10,... | collective-permute-start | bytes 3145736 | tf_op jit(solution)/shard_map/ppermute | solution.py:382
  21.6 36.6 %collective-permute-start.7 = (f32[16,64,256]{2,1,0:T(8,128)}, f32[16,64,256]{2,1,0:T(8,128)}, u32[]{:S(2)}, u32[]{:S(2)}) collective-permute-start(f32[16,64,256]{2,1,0:T(8,128)} %get-tuple-element.106.refs_1_), channel_id=1, source_target_pairs={{0,4},{1,5},{2,6},{3,7},{4,0},{5,1},{6,2},{7,3},{8,12},{9,13},{10,... | collective-permute-start | bytes 3145736 | tf_op jit(solution)/shard_map/ppermute | solution.py:382
  25.1 29.0 %copy-start.8 = (bf16[4,512,512]{2,1,0:T(8,128)(2,1)}, bf16[4,512,512]{2,1,0:T(8,128)(2,1)S(1)}, u32[]{:S(2)}) copy-start(bf16[4,512,512]{2,1,0:T(8,128)(2,1)S(1)} %get-tuple-element.103.refs_3_.refs_5_) | copy-start | bytes 6291460
  25.1 29.0 %copy-start.11 = (bf16[4,512,512]{2,1,0:T(8,128)(2,1)}, bf16[4,512,512]{2,1,0:T(8,128)(2,1)S(1)}, u32[]{:S(2)}) copy-start(bf16[4,512,512]{2,1,0:T(8,128)(2,1)S(1)} %get-tuple-element.104.refs_4_.refs_6_) | copy-start | bytes 6291460
  27.3 31.4 %copy-start.4 = (bf16[4,512,512]{2,1,0:T(8,128)(2,1)}, bf16[4,512,512]{2,1,0:T(8,128)(2,1)S(1)}, u32[]{:S(2)}) copy-start(bf16[4,512,512]{2,1,0:T(8,128)(2,1)S(1)} %get-tuple-element.110.refs_3_.refs_5_) | copy-start | bytes 6291460
  31.7 2.9 %collective-permute-start.4 = (f32[16,64,256]{2,1,0:T(8,128)}, f32[16,64,256]{2,1,0:T(8,128)S(1)}, u32[]{:S(2)}, u32[]{:S(2)}) collective-permute-start(f32[16,64,256]{2,1,0:T(8,128)} %get-tuple-element.89.refs_3_), channel_id=1, source_target_pairs={{0,1},{1,0},{2,3},{3,2},{4,5},{5,4},{6,7},{7,6},{8,9},{9,8},{10,11... | collective-permute-start | bytes 3145736 | tf_op jit(solution)/shard_map/ppermute | solution.py:382
  33.8 11.0 %collective-permute-start.5 = (f32[16,64,256]{2,1,0:T(8,128)}, f32[16,64,256]{2,1,0:T(8,128)}, u32[]{:S(2)}, u32[]{:S(2)}) collective-permute-start(f32[16,64,256]{2,1,0:T(8,128)} %get-tuple-element.94.refs_3_), channel_id=1, source_target_pairs={{0,1},{1,0},{2,3},{3,2},{4,5},{5,4},{6,7},{7,6},{8,9},{9,8},{10,11... | collective-permute-start | bytes 3145736 | tf_op jit(solution)/shard_map/ppermute | solution.py:382
  54.0 5.7 %collective-permute-start.8 = (f32[16,64,256]{2,1,0:T(8,128)}, f32[16,64,256]{2,1,0:T(8,128)S(1)}, u32[]{:S(2)}, u32[]{:S(2)}) collective-permute-start(f32[16,64,256]{2,1,0:T(8,128)} %get-tuple-element.113.refs_3_), channel_id=1, source_target_pairs={{0,1},{1,0},{2,3},{3,2},{4,5},{5,4},{6,7},{7,6},{8,9},{9,8},{10,11... | collective-permute-start | bytes 3145736 | tf_op jit(solution)/shard_map/ppermute | solution.py:382
  58.3 16.0 %collective-permute-start.9 = (f32[16,64,256]{2,1,0:T(8,128)}, f32[16,64,256]{2,1,0:T(8,128)}, u32[]{:S(2)}, u32[]{:S(2)}) collective-permute-start(f32[16,64,256]{2,1,0:T(8,128)} %get-tuple-element.119.refs_3_), channel_id=1, source_target_pairs={{0,1},{1,0},{2,3},{3,2},{4,5},{5,4},{6,7},{7,6},{8,9},{9,8},{10,11... | collective-permute-start | bytes 3145736 | tf_op jit(solution)/shard_map/ppermute | solution.py:382
  72.2 25.9 %collective-permute-start.10 = (f32[32,16,512]{2,1,0:T(8,128)}, f32[32,16,512]{2,1,0:T(8,128)}, u32[]{:S(2)}, u32[]{:S(2)}) collective-permute-start(f32[32,16,512]{2,1,0:T(8,128)} %get-tuple-element.127), channel_id=1, source_target_pairs={{0,4},{1,5},{2,6},{3,7},{4,0},{5,1},{6,2},{7,3},{8,12},{9,13},{10,... | collective-permute-start | bytes 3145736 | tf_op jit(solution)/shard_map/ppermute | solution.py:382
  84.5 22.4 %collective-permute-start.11 = (f32[16,16,512]{2,1,0:T(8,128)S(1)}, f32[16,16,512]{2,1,0:T(8,128)S(1)}, u32[]{:S(2)}, u32[]{:S(2)}) collective-permute-start(f32[16,16,512]{2,1,0:T(8,128)S(1)} %get-tuple-element.129), channel_id=1, source_target_pairs={{0,2},{1,3},{2,0},{3,1},{4,6},{5,7},{6,4},{7,5},{8,10},{9,11},{10,... | collective-permute-start | bytes 1572872 | tf_op jit(solution)/shard_map/ppermute | solution.py:382
  95.1 20.5 %collective-permute-start.12 = (f32[24,16,512]{2,1,0:T(8,128)S(1)}, f32[24,16,512]{2,1,0:T(8,128)S(1)}, u32[]{:S(2)}, u32[]{:S(2)}) collective-permute-start(f32[24,16,512]{2,1,0:T(8,128)S(1)} %get-tuple-element.132), channel_id=1, source_target_pairs={{0,2},{1,3},{2,0},{3,1},{4,6},{5,7},{6,4},{7,5},{8,10},{9,11},{10,... | collective-permute-start | bytes 2359304 | tf_op jit(solution)/shard_map/ppermute | solution.py:382
  96.7 24.6 %collective-permute-start.13 = (f32[32,16,512]{2,1,0:T(8,128)S(1)}, f32[32,16,512]{2,1,0:T(8,128)S(1)}, u32[]{:S(2)}, u32[]{:S(2)}) collective-permute-start(f32[32,16,512]{2,1,0:T(8,128)S(1)} %get-tuple-element.134), channel_id=1, source_target_pairs={{0,4},{1,5},{2,6},{3,7},{4,0},{5,1},{6,2},{7,3},{8,12},{9,13},{10,... | collective-permute-start | bytes 3145736 | tf_op jit(solution)/shard_map/ppermute | solution.py:382
  103.0 27.3 %collective-permute-start.14 = (f32[32,16,512]{2,1,0:T(8,128)S(1)}, f32[32,16,512]{2,1,0:T(8,128)S(1)}, u32[]{:S(2)}, u32[]{:S(2)}) collective-permute-start(f32[32,16,512]{2,1,0:T(8,128)S(1)} %get-tuple-element.136), channel_id=1, source_target_pairs={{0,8},{8,16},{16,24},{1,9},{9,17},{17,25},{2,10},{10,18},{18,26},{... | collective-permute-start | bytes 3145736 | tf_op jit(solution)/shard_map/ppermute | solution.py:385
  109.4 23.7 %collective-permute-start.15 = (f32[16,16,512]{2,1,0:T(8,128)}, f32[16,16,512]{2,1,0:T(8,128)S(1)}, u32[]{:S(2)}, u32[]{:S(2)}) collective-permute-start(f32[16,16,512]{2,1,0:T(8,128)} %get-tuple-element.138), channel_id=1, source_target_pairs={{8,0},{16,8},{24,16},{9,1},{17,9},{25,17},{10,2},{18,10},{26,18},{... | collective-permute-start | bytes 1572872 | tf_op jit(solution)/shard_map/ppermute | solution.py:385
  113.9 22.4 %collective-permute-start.16 = (f32[24,16,512]{2,1,0:T(8,128)S(1)}, f32[24,16,512]{2,1,0:T(8,128)S(1)}, u32[]{:S(2)}, u32[]{:S(2)}) collective-permute-start(f32[24,16,512]{2,1,0:T(8,128)S(1)} %get-tuple-element.140), channel_id=1, source_target_pairs={{0,2},{1,3},{2,0},{3,1},{4,6},{5,7},{6,4},{7,5},{8,10},{9,11},{10,... | collective-permute-start | bytes 2359304 | tf_op jit(solution)/shard_map/ppermute | solution.py:382
  118.9 22.3 %collective-permute-start.17 = (f32[24,16,512]{2,1,0:T(8,128)S(1)}, f32[24,16,512]{2,1,0:T(8,128)S(1)}, u32[]{:S(2)}, u32[]{:S(2)}) collective-permute-start(f32[24,16,512]{2,1,0:T(8,128)S(1)} %get-tuple-element.142), channel_id=1, source_target_pairs={{8,0},{16,8},{24,16},{9,1},{17,9},{25,17},{10,2},{18,10},{26,18},{... | collective-permute-start | bytes 2359304 | tf_op jit(solution)/shard_map/ppermute | solution.py:385
  126.1 24.9 %collective-permute-start.18 = (f32[32,16,512]{2,1,0:T(8,128)S(1)}, f32[32,16,512]{2,1,0:T(8,128)S(1)}, u32[]{:S(2)}, u32[]{:S(2)}) collective-permute-start(f32[32,16,512]{2,1,0:T(8,128)S(1)} %get-tuple-element.145), channel_id=1, source_target_pairs={{0,8},{8,16},{16,24},{1,9},{9,17},{17,25},{2,10},{10,18},{18,26},{... | collective-permute-start | bytes 3145736 | tf_op jit(solution)/shard_map/ppermute | solution.py:385
  139.6 19.4 %collective-permute-start.19 = (f32[24,16,512]{2,1,0:T(8,128)S(1)}, f32[24,16,512]{2,1,0:T(8,128)S(1)}, u32[]{:S(2)}, u32[]{:S(2)}) collective-permute-start(f32[24,16,512]{2,1,0:T(8,128)S(1)} %get-tuple-element.149), channel_id=1, source_target_pairs={{8,0},{16,8},{24,16},{9,1},{17,9},{25,17},{10,2},{18,10},{26,18},{... | collective-permute-start | bytes 2359304 | tf_op jit(solution)/shard_map/ppermute | solution.py:385
  (31 other events, 237.4 us)

commit v4 on v3

--- a/solution.py
+++ b/solution.py
@@ -9,7 +9,7 @@
 
 F32 = jnp.float32
 BF16 = jnp.bfloat16
-VMEM_BYTES = 22 << 20
+VMEM_BYTES = 20 << 20
 FLOPS_A_US = 10**11
 
 

time: 162 us -> 160 us (0.988)
  local copies, waits for them, and re-layouts: 5.54 us -> 3.72 us
    unnamed x70 -> x66, local copies, waits for them, and re-layouts: 4.31 us -> 2.49 us
  transfers between devices with their start and end apart: 20 -> 20, of which waited for: 8 -> 9; matrix products, arithmetic and copies ran while one was open for 1% -> 1% of each run, Pallas kernels for 63% -> 64%
where the time goes in v4:
time: 160 us; the launch traced here: 159 us
  Pallas kernels  103 us (64%)
  starting transfers between devices  26.8 us (17%)
  waiting for transfers between devices  23.8 us (15%)
  local copies, waits for them, and re-layouts  3.72 us (2%)
    pallas_call x33, Pallas kernels, call(): pl.pallas_call(inner, name=name, grid_spec=pltpu.PrefetchScalarGridSpec(n...  103 us
    ppermute x15, starting transfers between devices, moved(): return lax.ppermute(x, 'bond', route)  15.6 us
    ppermute x5, waiting for transfers between devices, handed(): lax.ppermute(x, 'site', [(k, k + distance) for k in range(chain) if 0 <=...  14.3 us
    ppermute x5, starting transfers between devices, handed(): lax.ppermute(x, 'site', [(k, k + distance) for k in range(chain) if 0 <=...  11.2 us
    ppermute x15, waiting for transfers between devices, moved(): return lax.ppermute(x, 'bond', route)  9.47 us
  transfers between devices with their start and end apart: 20, of which 9 were waited for; matrix products, arithmetic and copies ran while one was open for 1% of the time, Pallas kernels for 64%

profile of v4, /device:TPU:0, one launch (start us, length us, event | category | flops | bytes accessed | tf_op | source)
XLA Modules:
  0.0 159.2 jit_solution(10554663269172589093)
XLA Ops:
  1.2 3.3 %cut_columns.2 = (f32[16,64,256]{2,1,0:T(8,128)}, f32[16,64,256]{2,1,0:T(8,128)}, f32[8,128]{1,0:T(8,128)S(1)}) custom-call(f32[64,16,512]{2,1,0:T(8,128)} %bitcast.31, f32[64,16,512]{2,1,0:T(8,128)} %bitcast.36), custom_call_target="tpu_custom_call" | custom-call | flops 30000001024 | bytes 1000 | tf_op jit(solution)/shard_map/cut_columns/pallas_call | solution.py:80
  4.6 2.9 %collective-permute-start.2 = (f32[16,64,256]{2,1,0:T(8,128)}, f32[16,64,256]{2,1,0:T(8,128)}, u32[]{:S(2)}, u32[]{:S(2)}) collective-permute-start(f32[16,64,256]{2,1,0:T(8,128)} %get-tuple-element.85.refs_1_), channel_id=1, source_target_pairs={{0,2},{1,3},{2,0},{3,1},{4,6},{5,7},{6,4},{7,5},{8,10},{9,11},{10,... | collective-permute-start | bytes 3145736 | tf_op jit(solution)/shard_map/ppermute | solution.py:382
  14.9 2.6 %ket.3 = (bf16[512,256]{1,0:T(8,128)(2,1)S(1)}, bf16[512,256]{1,0:T(8,128)(2,1)S(1)}, f32[8,128]{1,0:T(8,128)S(1)}) custom-call(s32[14]{0:T(128)S(1)} %dynamic-slice_bitcast_fusion.refs_0_, f32[8,128]{1,0:T(8,128)S(1)} %get-tuple-element.80.refs_1_, f32[512,4,512]{2,1,0:T(4,128)} %bitcast.23, f32[512,4,512]{2,1,0:T(4,128)} %bitcast.24, ...), custom_call_target="tpu_custom_call" | custom-call | flops 269999996928 | bytes 1000 | tf_op jit(solution)/shard_map/ket/pallas_call | solution.py:80
  17.5 3.5 %cut_columns.3 = (f32[16,64,256]{2,1,0:T(8,128)}, f32[16,64,256]{2,1,0:T(8,128)}, f32[8,128]{1,0:T(8,128)S(1)}) custom-call(f32[8,128]{1,0:T(8,128)S(1)} %get-tuple-element.81.refs_0_, f32[64,16,512]{2,1,0:T(8,128)} %bitcast.32, f32[64,16,512]{2,1,0:T(8,128)} %bitcast.37), custom_call_target="tpu_custom_call" | custom-call | flops 30000001024 | bytes 1000 | tf_op jit(solution)/shard_map/cut_columns/pallas_call | solution.py:80
  27.3 4.4 %collective-permute-done.2.refs_1_ = f32[16,64,256]{2,1,0:T(8,128)} collective-permute-done((f32[16,64,256]{2,1,0:T(8,128)}, f32[16,64,256]{2,1,0:T(8,128)}, u32[]{:S(2)}, u32[]{:S(2)}) %collective-permute-start.2) | collective-permute-done | bytes 1048608 | tf_op jit(solution)/shard_map/ppermute | solution.py:382
  34.6 10.2 %first_part.4 = (bf16[4,2048,256]{2,1,0:T(8,128)(2,1)}, bf16[4,2048,256]{2,1,0:T(8,128)(2,1)}, f32[8,128]{1,0:T(8,128)S(1)}) custom-call(f32[8,128]{1,0:T(8,128)S(1)} %get-tuple-element.88.refs_0_, f32[16,64,256]{2,1,0:T(8,128)} %get-tuple-element.85.refs_1_, f32[64,16,512]{2,1,0:T(8,128)} %collective-permute-done.refs_2_, ...), custom_call_target="tpu_custom_call" | custom-call | flops 1068000018432 | bytes 1000 | tf_op jit(solution)/shard_map/first_part/pallas_call | solution.py:80
  44.8 9.1 %first_part.5 = (bf16[4,2048,256]{2,1,0:T(8,128)(2,1)S(1)}, bf16[4,2048,256]{2,1,0:T(8,128)(2,1)S(1)}, f32[8,128]{1,0:T(8,128)S(1)}) custom-call(f32[8,128]{1,0:T(8,128)S(1)} %get-tuple-element.93.refs_0_, f32[16,64,256]{2,1,0:T(8,128)} %get-tuple-element.87.refs_1_, f32[64,16,512]{2,1,0:T(8,128)} %copy-done.32, f32[16,64,256]{2,1,0:T(8,128)} %get-tuple-element.94.refs_3_, ...), custom_call_target="tpu_custom_call" | custom-call | flops 1068000018432 | bytes 1000 | tf_op jit(solution)/shard_map/first_part/pallas_call | solution.py:80
  54.1 4.1 %second_part.12 = (f32[32,16,512]{2,1,0:T(8,128)S(1)}, f32[8,128]{1,0:T(8,128)S(1)}) custom-call(f32[8,128]{1,0:T(8,128)S(1)} %get-tuple-element.100.refs_0_, bf16[4,2048,256]{2,1,0:T(8,128)(2,1)} %get-tuple-element.101.refs_1_, bf16[4,2048,256]{2,1,0:T(8,128)(2,1)} %get-tuple-element.102.refs_2_.refs_3_, ...), custom_call_target="tpu_custom_call" | custom-call | flops 3000000000 | bytes 1000 | tf_op jit(solution)/shard_map/second_part/pallas_call | solution.py:80
  59.8 9.0 %first_part.6 = (bf16[4,2048,256]{2,1,0:T(8,128)(2,1)S(1)}, bf16[4,2048,256]{2,1,0:T(8,128)(2,1)S(1)}, f32[8,128]{1,0:T(8,128)S(1)}) custom-call(f32[8,128]{1,0:T(8,128)S(1)} %get-tuple-element.112.refs_0_, f32[16,64,256]{2,1,0:T(8,128)} %get-tuple-element.99.refs_1_, f32[64,16,512]{2,1,0:T(8,128)} %collective-permute-done.refs_2_, ...), custom_call_target="tpu_custom_call" | custom-call | flops 1068000018432 | bytes 1000 | tf_op jit(solution)/shard_map/first_part/pallas_call | solution.py:80
  68.8 3.3 %second_part.14 = (f32[32,16,512]{2,1,0:T(8,128)}, f32[8,128]{1,0:T(8,128)S(1)}) custom-call(f32[8,128]{1,0:T(8,128)S(1)} %get-tuple-element.114.refs_0_, bf16[4,2048,256]{2,1,0:T(8,128)(2,1)S(1)} %get-tuple-element.115.refs_1_.refs_2_, bf16[4,2048,256]{2,1,0:T(8,128)(2,1)S(1)} %get-tuple-element.116.refs_2_.refs_4_, bf16[4,512,512]{2,1,0:T(8,128)(2,1)S(1)} %copy-done.9, ...), custom_call_target="tpu_custom_call" | custom-call | flops 3000000000 | bytes 1000 | tf_op jit(solution)/shard_map/second_part/pallas_call | solution.py:80
  74.2 9.1 %first_part.7 = (bf16[4,2048,256]{2,1,0:T(8,128)(2,1)S(1)}, bf16[4,2048,256]{2,1,0:T(8,128)(2,1)S(1)}, f32[8,128]{1,0:T(8,128)S(1)}) custom-call(f32[8,128]{1,0:T(8,128)S(1)} %get-tuple-element.118.refs_0_, f32[16,64,256]{2,1,0:T(8,128)} %get-tuple-element.106.refs_1_, f32[64,16,512]{2,1,0:T(8,128)} %copy-done.32, ...), custom_call_target="tpu_custom_call" | custom-call | flops 1068000018432 | bytes 1000 | tf_op jit(solution)/shard_map/first_part/pallas_call | solution.py:80
  86.9 4.9 %second_part.16 = (f32[32,16,512]{2,1,0:T(8,128)S(1)}, f32[8,128]{1,0:T(8,128)S(1)}) custom-call(f32[8,128]{1,0:T(8,128)S(1)} %get-tuple-element.124.refs_0_, bf16[4,2048,256]{2,1,0:T(8,128)(2,1)} %get-tuple-element.101.refs_1_, bf16[4,2048,256]{2,1,0:T(8,128)(2,1)S(1)} %copy-done.7, bf16[4,2048,256]{2,1,0:T(8,128)(2,1)} %get-tuple-element.102.refs_2_.refs_3_, ...), custom_call_target="tpu_custom_call" | custom-call | flops 3000000000 | bytes 1000 | tf_op jit(solution)/shard_map/second_part/pallas_call | solution.py:80
  91.9 3.2 %second_part.17 = (f32[24,16,512]{2,1,0:T(8,128)S(1)}, f32[8,128]{1,0:T(8,128)S(1)}) custom-call(f32[8,128]{1,0:T(8,128)S(1)} %get-tuple-element.125.refs_0_, bf16[4,2048,256]{2,1,0:T(8,128)(2,1)S(1)} %copy-done.1, bf16[4,2048,256]{2,1,0:T(8,128)(2,1)S(1)} %get-tuple-element.121.refs_1_.refs_2_, bf16[4,2048,256]{2,1,0:T(8,128)(2,1)S(1)} %copy-done.3, ...), custom_call_target="tpu_custom_call" | custom-call | flops 3000000000 | bytes 1000 | tf_op jit(solution)/shard_map/second_part/pallas_call | solution.py:80
  98.0 5.0 %second_part.18 = (f32[32,16,512]{2,1,0:T(8,128)S(1)}, f32[8,128]{1,0:T(8,128)S(1)}) custom-call(f32[8,128]{1,0:T(8,128)S(1)} %get-tuple-element.126.refs_0_, bf16[4,2048,256]{2,1,0:T(8,128)(2,1)} %get-tuple-element.101.refs_1_, bf16[4,2048,256]{2,1,0:T(8,128)(2,1)S(1)} %copy-done.7, bf16[4,2048,256]{2,1,0:T(8,128)(2,1)} %get-tuple-element.102.refs_2_.refs_3_, ...), custom_call_target="tpu_custom_call" | custom-call | flops 3000000000 | bytes 1000 | tf_op jit(solution)/shard_map/second_part/pallas_call | solution.py:80
  103.0 3.8 %collective-permute-start.14 = (f32[32,16,512]{2,1,0:T(8,128)S(1)}, f32[32,16,512]{2,1,0:T(8,128)S(1)}, u32[]{:S(2)}, u32[]{:S(2)}) collective-permute-start(f32[32,16,512]{2,1,0:T(8,128)S(1)} %get-tuple-element.136), channel_id=1, source_target_pairs={{0,8},{8,16},{16,24},{1,9},{9,17},{17,25},{2,10},{10,18},{18,26},{... | collective-permute-start | bytes 3145736 | tf_op jit(solution)/shard_map/ppermute | solution.py:385
  109.8 3.2 %second_part.20 = (f32[24,16,512]{2,1,0:T(8,128)S(1)}, f32[8,128]{1,0:T(8,128)S(1)}) custom-call(f32[8,128]{1,0:T(8,128)S(1)} %get-tuple-element.130.refs_0_, bf16[4,2048,256]{2,1,0:T(8,128)(2,1)S(1)} %copy-done.1, bf16[4,2048,256]{2,1,0:T(8,128)(2,1)S(1)} %get-tuple-element.121.refs_1_.refs_2_, bf16[4,2048,256]{2,1,0:T(8,128)(2,1)S(1)} %copy-done.3, ...), custom_call_target="tpu_custom_call" | custom-call | flops 3000000000 | bytes 1000 | tf_op jit(solution)/shard_map/second_part/pallas_call | solution.py:80
  115.3 3.2 %second_part.21 = (f32[24,16,512]{2,1,0:T(8,128)S(1)}, f32[8,128]{1,0:T(8,128)S(1)}) custom-call(f32[8,128]{1,0:T(8,128)S(1)} %get-tuple-element.131.refs_0_, bf16[4,2048,256]{2,1,0:T(8,128)(2,1)S(1)} %copy-done.1, bf16[4,2048,256]{2,1,0:T(8,128)(2,1)S(1)} %get-tuple-element.121.refs_1_.refs_2_, bf16[4,2048,256]{2,1,0:T(8,128)(2,1)S(1)} %copy-done.3, ...), custom_call_target="tpu_custom_call" | custom-call | flops 3000000000 | bytes 1000 | tf_op jit(solution)/shard_map/second_part/pallas_call | solution.py:80
  121.3 4.8 %second_part.22 = (f32[32,16,512]{2,1,0:T(8,128)S(1)}, f32[8,128]{1,0:T(8,128)S(1)}) custom-call(f32[8,128]{1,0:T(8,128)S(1)} %get-tuple-element.133.refs_0_, bf16[4,2048,256]{2,1,0:T(8,128)(2,1)} %get-tuple-element.101.refs_1_, bf16[4,2048,256]{2,1,0:T(8,128)(2,1)S(1)} %copy-done.7, bf16[4,2048,256]{2,1,0:T(8,128)(2,1)} %get-tuple-element.102.refs_2_.refs_3_, ...), custom_call_target="tpu_custom_call" | custom-call | flops 3000000000 | bytes 1000 | tf_op jit(solution)/shard_map/second_part/pallas_call | solution.py:80
  126.1 3.5 %collective-permute-start.18 = (f32[32,16,512]{2,1,0:T(8,128)S(1)}, f32[32,16,512]{2,1,0:T(8,128)S(1)}, u32[]{:S(2)}, u32[]{:S(2)}) collective-permute-start(f32[32,16,512]{2,1,0:T(8,128)S(1)} %get-tuple-element.145), channel_id=1, source_target_pairs={{0,8},{8,16},{16,24},{1,9},{9,17},{17,25},{2,10},{10,18},{18,26},{... | collective-permute-start | bytes 3145736 | tf_op jit(solution)/shard_map/ppermute | solution.py:385
  129.7 2.7 %place.5 = (f32[64,16,512]{2,1,0:T(8,128)}, f32[8,128]{1,0:T(8,128)S(1)}) custom-call(s32[14]{0:T(128)S(1)} %copy-done.17, f32[8,128]{1,0:T(8,128)S(1)} %get-tuple-element.135.refs_1_, f32[32,16,512]{2,1,0:T(8,128)S(1)} %collective-permute-done.14.refs_2_, f32[64,16,512]{2,1,0:T(8,128)} %bitcast.33), custom_call_target="tpu_custom_call" | custom-call | flops 10000000000 | bytes 1000 | tf_op jit(solution)/shard_map/place/pallas_call | solution.py:80
  133.8 3.2 %second_part.23 = (f32[24,16,512]{2,1,0:T(8,128)S(1)}, f32[8,128]{1,0:T(8,128)S(1)}) custom-call(f32[8,128]{1,0:T(8,128)S(1)} %get-tuple-element.139.refs_0_, bf16[4,2048,256]{2,1,0:T(8,128)(2,1)S(1)} %copy-done.1, bf16[4,2048,256]{2,1,0:T(8,128)(2,1)S(1)} %get-tuple-element.121.refs_1_.refs_2_, bf16[4,2048,256]{2,1,0:T(8,128)(2,1)S(1)} %copy-done.3, ...), custom_call_target="tpu_custom_call" | custom-call | flops 3000000000 | bytes 1000 | tf_op jit(solution)/shard_map/second_part/pallas_call | solution.py:80
  141.7 9.3 %collective-permute-done.18.refs_2_ = f32[32,16,512]{2,1,0:T(8,128)S(1)} collective-permute-done((f32[32,16,512]{2,1,0:T(8,128)S(1)}, f32[32,16,512]{2,1,0:T(8,128)S(1)}, u32[]{:S(2)}, u32[]{:S(2)}) %collective-permute-start.18) | collective-permute-done | bytes 1048608 | tf_op jit(solution)/shard_map/ppermute | solution.py:385
  151.0 2.7 %place.8 = (f32[64,16,512]{2,1,0:T(8,128)}, f32[8,128]{1,0:T(8,128)S(1)}) custom-call(s32[14]{0:T(128)S(1)} %copy-done.17, f32[8,128]{1,0:T(8,128)S(1)} %get-tuple-element.144.refs_1_, f32[32,16,512]{2,1,0:T(8,128)S(1)} %collective-permute-done.18.refs_2_, f32[64,16,512]{2,1,0:T(8,128)} %bitcast.34, ...), custom_call_target="tpu_custom_call", output_to_operand_aliasing={{0}: (4, {})} | custom-call | flops 10000000000 | bytes 1000 | tf_op jit(solution)/shard_map/place/pallas_call | solution.py:80
  153.7 3.2 %collective-permute-done.19.refs_2_ = f32[24,16,512]{2,1,0:T(8,128)S(1)} collective-permute-done((f32[24,16,512]{2,1,0:T(8,128)S(1)}, f32[24,16,512]{2,1,0:T(8,128)S(1)}, u32[]{:S(2)}, u32[]{:S(2)}) %collective-permute-start.19) | collective-permute-done | bytes 786464 | tf_op jit(solution)/shard_map/ppermute | solution.py:385
  (121 shorter events, 43.4 us)
Async XLA Ops:
  0.6 9.9 %collective-permute-start = (f32[64,16,512]{2,1,0:T(8,128)}, f32[64,16,512]{2,1,0:T(8,128)}, u32[]{:S(2)}, u32[]{:S(2)}) collective-permute-start(f32[64,16,512]{2,1,0:T(8,128)} %bitcast.30), channel_id=1, source_target_pairs={{0,1},{1,0},{2,3},{3,2},{4,5},{5,4},{6,7},{7,6},{8,9},{9,8},{10,11... | collective-permute-start | bytes 6291464 | tf_op jit(solution)/shard_map/ppermute | solution.py:382
  1.2 9.4 %collective-permute-start.1 = (f32[64,16,512]{2,1,0:T(8,128)}, f32[64,16,512]{2,1,0:T(8,128)S(1)}, u32[]{:S(2)}, u32[]{:S(2)}) collective-permute-start(f32[64,16,512]{2,1,0:T(8,128)} %bitcast.35), channel_id=1, source_target_pairs={{0,1},{1,0},{2,3},{3,2},{4,5},{5,4},{6,7},{7,6},{8,9},{9,8},{10,11... | collective-permute-start | bytes 6291464 | tf_op jit(solution)/shard_map/ppermute | solution.py:382
  4.6 27.1 %collective-permute-start.2 = (f32[16,64,256]{2,1,0:T(8,128)}, f32[16,64,256]{2,1,0:T(8,128)}, u32[]{:S(2)}, u32[]{:S(2)}) collective-permute-start(f32[16,64,256]{2,1,0:T(8,128)} %get-tuple-element.85.refs_1_), channel_id=1, source_target_pairs={{0,2},{1,3},{2,0},{3,1},{4,6},{5,7},{6,4},{7,5},{8,10},{9,11},{10,... | collective-permute-start | bytes 3145736 | tf_op jit(solution)/shard_map/ppermute | solution.py:382
  7.5 26.4 %collective-permute-start.3 = (f32[16,64,256]{2,1,0:T(8,128)}, f32[16,64,256]{2,1,0:T(8,128)}, u32[]{:S(2)}, u32[]{:S(2)}) collective-permute-start(f32[16,64,256]{2,1,0:T(8,128)} %get-tuple-element.87.refs_1_), channel_id=1, source_target_pairs={{0,4},{1,5},{2,6},{3,7},{4,0},{5,1},{6,2},{7,3},{8,12},{9,13},{10,... | collective-permute-start | bytes 3145736 | tf_op jit(solution)/shard_map/ppermute | solution.py:382
  14.8 29.9 %copy-start.18 = (bf16[256,256]{1,0:T(8,128)(2,1)}, bf16[256,256]{1,0:T(8,128)(2,1)S(1)}, u32[]{:S(2)}) copy-start(bf16[256,256]{1,0:T(8,128)(2,1)S(1)} %get-tuple-element.97.refs_7_) | copy-start | bytes 393220
  21.1 32.8 %collective-permute-start.6 = (f32[16,64,256]{2,1,0:T(8,128)}, f32[16,64,256]{2,1,0:T(8,128)}, u32[]{:S(2)}, u32[]{:S(2)}) collective-permute-start(f32[16,64,256]{2,1,0:T(8,128)} %get-tuple-element.99.refs_1_), channel_id=1, source_target_pairs={{0,2},{1,3},{2,0},{3,1},{4,6},{5,7},{6,4},{7,5},{8,10},{9,11},{10,... | collective-permute-start | bytes 3145736 | tf_op jit(solution)/shard_map/ppermute | solution.py:382
  21.6 36.6 %collective-permute-start.7 = (f32[16,64,256]{2,1,0:T(8,128)}, f32[16,64,256]{2,1,0:T(8,128)}, u32[]{:S(2)}, u32[]{:S(2)}) collective-permute-start(f32[16,64,256]{2,1,0:T(8,128)} %get-tuple-element.106.refs_1_), channel_id=1, source_target_pairs={{0,4},{1,5},{2,6},{3,7},{4,0},{5,1},{6,2},{7,3},{8,12},{9,13},{10,... | collective-permute-start | bytes 3145736 | tf_op jit(solution)/shard_map/ppermute | solution.py:382
  25.1 29.0 %copy-start.8 = (bf16[4,512,512]{2,1,0:T(8,128)(2,1)}, bf16[4,512,512]{2,1,0:T(8,128)(2,1)S(1)}, u32[]{:S(2)}) copy-start(bf16[4,512,512]{2,1,0:T(8,128)(2,1)S(1)} %get-tuple-element.103.refs_3_.refs_5_) | copy-start | bytes 6291460
  25.1 29.0 %copy-start.11 = (bf16[4,512,512]{2,1,0:T(8,128)(2,1)}, bf16[4,512,512]{2,1,0:T(8,128)(2,1)S(1)}, u32[]{:S(2)}) copy-start(bf16[4,512,512]{2,1,0:T(8,128)(2,1)S(1)} %get-tuple-element.104.refs_4_.refs_6_) | copy-start | bytes 6291460
  27.3 31.4 %copy-start.4 = (bf16[4,512,512]{2,1,0:T(8,128)(2,1)}, bf16[4,512,512]{2,1,0:T(8,128)(2,1)S(1)}, u32[]{:S(2)}) copy-start(bf16[4,512,512]{2,1,0:T(8,128)(2,1)S(1)} %get-tuple-element.110.refs_3_.refs_5_) | copy-start | bytes 6291460
  31.7 2.9 %collective-permute-start.4 = (f32[16,64,256]{2,1,0:T(8,128)}, f32[16,64,256]{2,1,0:T(8,128)S(1)}, u32[]{:S(2)}, u32[]{:S(2)}) collective-permute-start(f32[16,64,256]{2,1,0:T(8,128)} %get-tuple-element.89.refs_3_), channel_id=1, source_target_pairs={{0,1},{1,0},{2,3},{3,2},{4,5},{5,4},{6,7},{7,6},{8,9},{9,8},{10,11... | collective-permute-start | bytes 3145736 | tf_op jit(solution)/shard_map/ppermute | solution.py:382
  33.8 10.9 %collective-permute-start.5 = (f32[16,64,256]{2,1,0:T(8,128)}, f32[16,64,256]{2,1,0:T(8,128)}, u32[]{:S(2)}, u32[]{:S(2)}) collective-permute-start(f32[16,64,256]{2,1,0:T(8,128)} %get-tuple-element.94.refs_3_), channel_id=1, source_target_pairs={{0,1},{1,0},{2,3},{3,2},{4,5},{5,4},{6,7},{7,6},{8,9},{9,8},{10,11... | collective-permute-start | bytes 3145736 | tf_op jit(solution)/shard_map/ppermute | solution.py:382
  53.9 5.7 %collective-permute-start.8 = (f32[16,64,256]{2,1,0:T(8,128)}, f32[16,64,256]{2,1,0:T(8,128)S(1)}, u32[]{:S(2)}, u32[]{:S(2)}) collective-permute-start(f32[16,64,256]{2,1,0:T(8,128)} %get-tuple-element.113.refs_3_), channel_id=1, source_target_pairs={{0,1},{1,0},{2,3},{3,2},{4,5},{5,4},{6,7},{7,6},{8,9},{9,8},{10,11... | collective-permute-start | bytes 3145736 | tf_op jit(solution)/shard_map/ppermute | solution.py:382
  58.2 16.0 %collective-permute-start.9 = (f32[16,64,256]{2,1,0:T(8,128)}, f32[16,64,256]{2,1,0:T(8,128)}, u32[]{:S(2)}, u32[]{:S(2)}) collective-permute-start(f32[16,64,256]{2,1,0:T(8,128)} %get-tuple-element.119.refs_3_), channel_id=1, source_target_pairs={{0,1},{1,0},{2,3},{3,2},{4,5},{5,4},{6,7},{7,6},{8,9},{9,8},{10,11... | collective-permute-start | bytes 3145736 | tf_op jit(solution)/shard_map/ppermute | solution.py:382
  72.1 25.9 %collective-permute-start.10 = (f32[32,16,512]{2,1,0:T(8,128)}, f32[32,16,512]{2,1,0:T(8,128)}, u32[]{:S(2)}, u32[]{:S(2)}) collective-permute-start(f32[32,16,512]{2,1,0:T(8,128)} %get-tuple-element.127), channel_id=1, source_target_pairs={{0,4},{1,5},{2,6},{3,7},{4,0},{5,1},{6,2},{7,3},{8,12},{9,13},{10,... | collective-permute-start | bytes 3145736 | tf_op jit(solution)/shard_map/ppermute | solution.py:382
  84.4 22.3 %collective-permute-start.11 = (f32[16,16,512]{2,1,0:T(8,128)S(1)}, f32[16,16,512]{2,1,0:T(8,128)S(1)}, u32[]{:S(2)}, u32[]{:S(2)}) collective-permute-start(f32[16,16,512]{2,1,0:T(8,128)S(1)} %get-tuple-element.129), channel_id=1, source_target_pairs={{0,2},{1,3},{2,0},{3,1},{4,6},{5,7},{6,4},{7,5},{8,10},{9,11},{10,... | collective-permute-start | bytes 1572872 | tf_op jit(solution)/shard_map/ppermute | solution.py:382
  95.1 20.2 %collective-permute-start.12 = (f32[24,16,512]{2,1,0:T(8,128)S(1)}, f32[24,16,512]{2,1,0:T(8,128)S(1)}, u32[]{:S(2)}, u32[]{:S(2)}) collective-permute-start(f32[24,16,512]{2,1,0:T(8,128)S(1)} %get-tuple-element.132), channel_id=1, source_target_pairs={{0,2},{1,3},{2,0},{3,1},{4,6},{5,7},{6,4},{7,5},{8,10},{9,11},{10,... | collective-permute-start | bytes 2359304 | tf_op jit(solution)/shard_map/ppermute | solution.py:382
  96.6 24.6 %collective-permute-start.13 = (f32[32,16,512]{2,1,0:T(8,128)S(1)}, f32[32,16,512]{2,1,0:T(8,128)S(1)}, u32[]{:S(2)}, u32[]{:S(2)}) collective-permute-start(f32[32,16,512]{2,1,0:T(8,128)S(1)} %get-tuple-element.134), channel_id=1, source_target_pairs={{0,4},{1,5},{2,6},{3,7},{4,0},{5,1},{6,2},{7,3},{8,12},{9,13},{10,... | collective-permute-start | bytes 3145736 | tf_op jit(solution)/shard_map/ppermute | solution.py:382
  103.0 26.7 %collective-permute-start.14 = (f32[32,16,512]{2,1,0:T(8,128)S(1)}, f32[32,16,512]{2,1,0:T(8,128)S(1)}, u32[]{:S(2)}, u32[]{:S(2)}) collective-permute-start(f32[32,16,512]{2,1,0:T(8,128)S(1)} %get-tuple-element.136), channel_id=1, source_target_pairs={{0,8},{8,16},{16,24},{1,9},{9,17},{17,25},{2,10},{10,18},{18,26},{... | collective-permute-start | bytes 3145736 | tf_op jit(solution)/shard_map/ppermute | solution.py:385
  108.5 23.9 %collective-permute-start.15 = (f32[16,16,512]{2,1,0:T(8,128)S(1)}, f32[16,16,512]{2,1,0:T(8,128)S(1)}, u32[]{:S(2)}, u32[]{:S(2)}) collective-permute-start(f32[16,16,512]{2,1,0:T(8,128)S(1)} %get-tuple-element.138), channel_id=1, source_target_pairs={{8,0},{16,8},{24,16},{9,1},{17,9},{25,17},{10,2},{18,10},{26,18},{... | collective-permute-start | bytes 1572872 | tf_op jit(solution)/shard_map/ppermute | solution.py:385
  113.1 20.8 %collective-permute-start.16 = (f32[24,16,512]{2,1,0:T(8,128)S(1)}, f32[24,16,512]{2,1,0:T(8,128)S(1)}, u32[]{:S(2)}, u32[]{:S(2)}) collective-permute-start(f32[24,16,512]{2,1,0:T(8,128)S(1)} %get-tuple-element.140), channel_id=1, source_target_pairs={{0,2},{1,3},{2,0},{3,1},{4,6},{5,7},{6,4},{7,5},{8,10},{9,11},{10,... | collective-permute-start | bytes 2359304 | tf_op jit(solution)/shard_map/ppermute | solution.py:382
  118.5 21.8 %collective-permute-start.17 = (f32[24,16,512]{2,1,0:T(8,128)S(1)}, f32[24,16,512]{2,1,0:T(8,128)S(1)}, u32[]{:S(2)}, u32[]{:S(2)}) collective-permute-start(f32[24,16,512]{2,1,0:T(8,128)S(1)} %get-tuple-element.142), channel_id=1, source_target_pairs={{8,0},{16,8},{24,16},{9,1},{17,9},{25,17},{10,2},{18,10},{26,18},{... | collective-permute-start | bytes 2359304 | tf_op jit(solution)/shard_map/ppermute | solution.py:385
  126.1 24.9 %collective-permute-start.18 = (f32[32,16,512]{2,1,0:T(8,128)S(1)}, f32[32,16,512]{2,1,0:T(8,128)S(1)}, u32[]{:S(2)}, u32[]{:S(2)}) collective-permute-start(f32[32,16,512]{2,1,0:T(8,128)S(1)} %get-tuple-element.145), channel_id=1, source_target_pairs={{0,8},{8,16},{16,24},{1,9},{9,17},{17,25},{2,10},{10,18},{18,26},{... | collective-permute-start | bytes 3145736 | tf_op jit(solution)/shard_map/ppermute | solution.py:385
  137.1 19.9 %collective-permute-start.19 = (f32[24,16,512]{2,1,0:T(8,128)S(1)}, f32[24,16,512]{2,1,0:T(8,128)S(1)}, u32[]{:S(2)}, u32[]{:S(2)}) collective-permute-start(f32[24,16,512]{2,1,0:T(8,128)S(1)} %get-tuple-element.149), channel_id=1, source_target_pairs={{8,0},{16,8},{24,16},{9,1},{17,9},{25,17},{10,2},{18,10},{26,18},{... | collective-permute-start | bytes 2359304 | tf_op jit(solution)/shard_map/ppermute | solution.py:385
  (29 other events, 234.8 us)

commit v5 on v4

--- a/solution.py
+++ b/solution.py
@@ -315,7 +315,7 @@
     bra_spec = pl.BlockSpec((states, depth, columns), lambda i: (0, only or 0, 0))
     yhs = [h for h, _, _ in pieces]
     yls = [l for _, l, _ in pieces]
-    block = next(b for b in range(min(count, 24), 0, -1) if start % b == 0 and count % b == 0)
+    block = next(b for b in range(min(count, 16), 0, -1) if start % b == 0 and count % b == 0)
 
     def y_spec(y, base):
         return pl.BlockSpec((states, block * width, y.shape[2]), lambda i: (0, (start - base) // block + i, 0))
@@ -409,6 +409,7 @@
             self.ranks = {"o": outer, "i": inner}[gather]
             self.others = {"o": outer, "i": inner}[reduce]
             self.pieces = shares(rows, (1, 1) if distance > 0 else (2, 3, 3), group)
+            self.starts = [rows - self.pieces[0]] + [sum(self.pieces[1:j]) for j in range(1, len(self.pieces))]
             self.own, self.done, self.sent, self.handed, self.out = [], [], [], [], []
 
         def gather_near(self):
@@ -435,27 +436,27 @@
             self.done.append(first_part(turns, *args, b_at, b_count, j > 0 or self.distance < 0))
 
         def begin(self):
-            starts = [(k - 1) * rows for k in range(1, self.others)]
+            starts = [(k - 1) * rows + self.starts[0] for k in range(1, self.others)]
             args = self.done, self.bra
             self.begun = [second_part(turns, *args, at, self.pieces[0], width, [], 0) for at in starts]
 
         def send(self, j):
             got = []
             for k in range(1, self.others):
-                start = (k - 1) * rows + sum(self.pieces[:j])
+                start = (k - 1) * rows + self.starts[j]
                 more, only = ([], None) if j else ([self.begun[k - 1]], 1)
                 x = second_part(turns, self.done, self.bra, start, self.pieces[j], width, more, only)
                 got.append(moved(x, **{self.reduce: k}))
             self.sent.append(got)
 
         def keep(self, j):
-            start = (self.others - 1) * rows + sum(self.pieces[:j])
+            start = (self.others - 1) * rows + self.starts[j]
             x = second_part(turns, self.done, self.bra, start, self.pieces[j], width, self.sent[j])
             self.handed.append(handed(x, self.distance))
 
         def place(self, j):
             edge = 0 if self.distance > 0 else chain - 1
-            self.out = place(turns, self.handed[j], self.env, sum(self.pieces[:j]), self.out, scalars, edge)
+            self.out = place(turns, self.handed[j], self.env, self.starts[j], self.out, scalars, edge)
 
     turns = Turns()
     left_op = jnp.transpose(left_mpo[0], (3, 1, 0, 2)).reshape(states * width, -1)

time: 160 us -> 160 us (level)
  transfers between devices with their start and end apart: 20 -> 20, of which waited for: 9 -> 8; matrix products, arithmetic and copies ran while one was open for 1% -> 1% of each run, Pallas kernels for 64% -> 64%
where the time goes in v5:
time: 160 us; the launch traced here: 159 us
  Pallas kernels  104 us (65%)
  starting transfers between devices  26.7 us (17%)
  waiting for transfers between devices  23.6 us (15%)
  local copies, waits for them, and re-layouts  3.73 us (2%)
    pallas_call x33, Pallas kernels, call(): pl.pallas_call(inner, name=name, grid_spec=pltpu.PrefetchScalarGridSpec(n...  104 us
    ppermute x15, starting transfers between devices, moved(): return lax.ppermute(x, 'bond', route)  15.5 us
    ppermute x5, waiting for transfers between devices, handed(): lax.ppermute(x, 'site', [(k, k + distance) for k in range(chain) if 0 <=...  14.2 us
    ppermute x5, starting transfers between devices, handed(): lax.ppermute(x, 'site', [(k, k + distance) for k in range(chain) if 0 <=...  11.2 us
    ppermute x15, waiting for transfers between devices, moved(): return lax.ppermute(x, 'bond', route)  9.41 us
  transfers between devices with their start and end apart: 20, of which 8 were waited for; matrix products, arithmetic and copies ran while one was open for 1% of the time, Pallas kernels for 64%

profile of v5, /device:TPU:0, one launch (start us, length us, event | category | flops | bytes accessed | tf_op | source)
XLA Modules:
  0.0 159.2 jit_solution(13300178530814134721)
XLA Ops:
  1.2 3.3 %cut_columns.2 = (f32[16,64,256]{2,1,0:T(8,128)}, f32[16,64,256]{2,1,0:T(8,128)}, f32[8,128]{1,0:T(8,128)S(1)}) custom-call(f32[64,16,512]{2,1,0:T(8,128)} %bitcast.31, f32[64,16,512]{2,1,0:T(8,128)} %bitcast.36), custom_call_target="tpu_custom_call" | custom-call | flops 30000001024 | bytes 1000 | tf_op jit(solution)/shard_map/cut_columns/pallas_call | solution.py:80
  4.6 2.9 %collective-permute-start.2 = (f32[16,64,256]{2,1,0:T(8,128)}, f32[16,64,256]{2,1,0:T(8,128)}, u32[]{:S(2)}, u32[]{:S(2)}) collective-permute-start(f32[16,64,256]{2,1,0:T(8,128)} %get-tuple-element.85.refs_1_), channel_id=1, source_target_pairs={{0,2},{1,3},{2,0},{3,1},{4,6},{5,7},{6,4},{7,5},{8,10},{9,11},{10,... | collective-permute-start | bytes 3145736 | tf_op jit(solution)/shard_map/ppermute | solution.py:382
  14.9 2.6 %ket.3 = (bf16[512,256]{1,0:T(8,128)(2,1)S(1)}, bf16[512,256]{1,0:T(8,128)(2,1)S(1)}, f32[8,128]{1,0:T(8,128)S(1)}) custom-call(s32[14]{0:T(128)S(1)} %dynamic-slice_bitcast_fusion.refs_0_, f32[8,128]{1,0:T(8,128)S(1)} %get-tuple-element.80.refs_1_, f32[512,4,512]{2,1,0:T(4,128)} %bitcast.23, f32[512,4,512]{2,1,0:T(4,128)} %bitcast.24, ...), custom_call_target="tpu_custom_call" | custom-call | flops 269999996928 | bytes 1000 | tf_op jit(solution)/shard_map/ket/pallas_call | solution.py:80
  17.5 3.5 %cut_columns.3 = (f32[16,64,256]{2,1,0:T(8,128)}, f32[16,64,256]{2,1,0:T(8,128)}, f32[8,128]{1,0:T(8,128)S(1)}) custom-call(f32[8,128]{1,0:T(8,128)S(1)} %get-tuple-element.81.refs_0_, f32[64,16,512]{2,1,0:T(8,128)} %bitcast.32, f32[64,16,512]{2,1,0:T(8,128)} %bitcast.37), custom_call_target="tpu_custom_call" | custom-call | flops 30000001024 | bytes 1000 | tf_op jit(solution)/shard_map/cut_columns/pallas_call | solution.py:80
  27.3 4.4 %collective-permute-done.2.refs_1_ = f32[16,64,256]{2,1,0:T(8,128)} collective-permute-done((f32[16,64,256]{2,1,0:T(8,128)}, f32[16,64,256]{2,1,0:T(8,128)}, u32[]{:S(2)}, u32[]{:S(2)}) %collective-permute-start.2) | collective-permute-done | bytes 1048608 | tf_op jit(solution)/shard_map/ppermute | solution.py:382
  34.6 10.2 %first_part.4 = (bf16[4,2048,256]{2,1,0:T(8,128)(2,1)}, bf16[4,2048,256]{2,1,0:T(8,128)(2,1)}, f32[8,128]{1,0:T(8,128)S(1)}) custom-call(f32[8,128]{1,0:T(8,128)S(1)} %get-tuple-element.88.refs_0_, f32[16,64,256]{2,1,0:T(8,128)} %get-tuple-element.85.refs_1_, f32[64,16,512]{2,1,0:T(8,128)} %collective-permute-done.refs_2_, ...), custom_call_target="tpu_custom_call" | custom-call | flops 1068000018432 | bytes 1000 | tf_op jit(solution)/shard_map/first_part/pallas_call | solution.py:80
  44.8 9.1 %first_part.5 = (bf16[4,2048,256]{2,1,0:T(8,128)(2,1)S(1)}, bf16[4,2048,256]{2,1,0:T(8,128)(2,1)S(1)}, f32[8,128]{1,0:T(8,128)S(1)}) custom-call(f32[8,128]{1,0:T(8,128)S(1)} %get-tuple-element.93.refs_0_, f32[16,64,256]{2,1,0:T(8,128)} %get-tuple-element.87.refs_1_, f32[64,16,512]{2,1,0:T(8,128)} %copy-done.32, f32[16,64,256]{2,1,0:T(8,128)} %get-tuple-element.94.refs_3_, ...), custom_call_target="tpu_custom_call" | custom-call | flops 1068000018432 | bytes 1000 | tf_op jit(solution)/shard_map/first_part/pallas_call | solution.py:80
  54.1 4.1 %second_part.12 = (f32[32,16,512]{2,1,0:T(8,128)S(1)}, f32[8,128]{1,0:T(8,128)S(1)}) custom-call(f32[8,128]{1,0:T(8,128)S(1)} %get-tuple-element.100.refs_0_, bf16[4,2048,256]{2,1,0:T(8,128)(2,1)} %get-tuple-element.101.refs_1_, bf16[4,2048,256]{2,1,0:T(8,128)(2,1)} %get-tuple-element.102.refs_2_.refs_3_, ...), custom_call_target="tpu_custom_call" | custom-call | flops 3000000000 | bytes 1000 | tf_op jit(solution)/shard_map/second_part/pallas_call | solution.py:80
  59.8 9.0 %first_part.6 = (bf16[4,2048,256]{2,1,0:T(8,128)(2,1)S(1)}, bf16[4,2048,256]{2,1,0:T(8,128)(2,1)S(1)}, f32[8,128]{1,0:T(8,128)S(1)}) custom-call(f32[8,128]{1,0:T(8,128)S(1)} %get-tuple-element.112.refs_0_, f32[16,64,256]{2,1,0:T(8,128)} %get-tuple-element.99.refs_1_, f32[64,16,512]{2,1,0:T(8,128)} %collective-permute-done.refs_2_, ...), custom_call_target="tpu_custom_call" | custom-call | flops 1068000018432 | bytes 1000 | tf_op jit(solution)/shard_map/first_part/pallas_call | solution.py:80
  68.8 3.3 %second_part.14 = (f32[32,16,512]{2,1,0:T(8,128)}, f32[8,128]{1,0:T(8,128)S(1)}) custom-call(f32[8,128]{1,0:T(8,128)S(1)} %get-tuple-element.114.refs_0_, bf16[4,2048,256]{2,1,0:T(8,128)(2,1)S(1)} %get-tuple-element.115.refs_1_.refs_2_, bf16[4,2048,256]{2,1,0:T(8,128)(2,1)S(1)} %get-tuple-element.116.refs_2_.refs_4_, bf16[4,512,512]{2,1,0:T(8,128)(2,1)S(1)} %copy-done.9, ...), custom_call_target="tpu_custom_call" | custom-call | flops 3000000000 | bytes 1000 | tf_op jit(solution)/shard_map/second_part/pallas_call | solution.py:80
  74.3 9.1 %first_part.7 = (bf16[4,2048,256]{2,1,0:T(8,128)(2,1)S(1)}, bf16[4,2048,256]{2,1,0:T(8,128)(2,1)S(1)}, f32[8,128]{1,0:T(8,128)S(1)}) custom-call(f32[8,128]{1,0:T(8,128)S(1)} %get-tuple-element.118.refs_0_, f32[16,64,256]{2,1,0:T(8,128)} %get-tuple-element.106.refs_1_, f32[64,16,512]{2,1,0:T(8,128)} %copy-done.32, ...), custom_call_target="tpu_custom_call" | custom-call | flops 1068000018432 | bytes 1000 | tf_op jit(solution)/shard_map/first_part/pallas_call | solution.py:80
  86.9 4.9 %second_part.16 = (f32[32,16,512]{2,1,0:T(8,128)S(1)}, f32[8,128]{1,0:T(8,128)S(1)}) custom-call(f32[8,128]{1,0:T(8,128)S(1)} %get-tuple-element.124.refs_0_, bf16[4,2048,256]{2,1,0:T(8,128)(2,1)} %get-tuple-element.101.refs_1_, bf16[4,2048,256]{2,1,0:T(8,128)(2,1)S(1)} %copy-done.7, bf16[4,2048,256]{2,1,0:T(8,128)(2,1)} %get-tuple-element.102.refs_2_.refs_3_, ...), custom_call_target="tpu_custom_call" | custom-call | flops 3000000000 | bytes 1000 | tf_op jit(solution)/shard_map/second_part/pallas_call | solution.py:80
  91.9 3.4 %second_part.17 = (f32[24,16,512]{2,1,0:T(8,128)S(1)}, f32[8,128]{1,0:T(8,128)S(1)}) custom-call(f32[8,128]{1,0:T(8,128)S(1)} %get-tuple-element.125.refs_0_, bf16[4,2048,256]{2,1,0:T(8,128)(2,1)S(1)} %copy-done.1, bf16[4,2048,256]{2,1,0:T(8,128)(2,1)S(1)} %get-tuple-element.121.refs_1_.refs_2_, bf16[4,2048,256]{2,1,0:T(8,128)(2,1)S(1)} %copy-done.3, ...), custom_call_target="tpu_custom_call" | custom-call | flops 3000000000 | bytes 1000 | tf_op jit(solution)/shard_map/second_part/pallas_call | solution.py:80
  98.0 5.0 %second_part.18 = (f32[32,16,512]{2,1,0:T(8,128)S(1)}, f32[8,128]{1,0:T(8,128)S(1)}) custom-call(f32[8,128]{1,0:T(8,128)S(1)} %get-tuple-element.126.refs_0_, bf16[4,2048,256]{2,1,0:T(8,128)(2,1)} %get-tuple-element.101.refs_1_, bf16[4,2048,256]{2,1,0:T(8,128)(2,1)S(1)} %copy-done.7, bf16[4,2048,256]{2,1,0:T(8,128)(2,1)} %get-tuple-element.102.refs_2_.refs_3_, ...), custom_call_target="tpu_custom_call" | custom-call | flops 3000000000 | bytes 1000 | tf_op jit(solution)/shard_map/second_part/pallas_call | solution.py:80
  103.0 3.8 %collective-permute-start.14 = (f32[32,16,512]{2,1,0:T(8,128)S(1)}, f32[32,16,512]{2,1,0:T(8,128)S(1)}, u32[]{:S(2)}, u32[]{:S(2)}) collective-permute-start(f32[32,16,512]{2,1,0:T(8,128)S(1)} %get-tuple-element.136), channel_id=1, source_target_pairs={{0,8},{8,16},{16,24},{1,9},{9,17},{17,25},{2,10},{10,18},{18,26},{... | collective-permute-start | bytes 3145736 | tf_op jit(solution)/shard_map/ppermute | solution.py:385
  109.9 3.4 %second_part.20 = (f32[24,16,512]{2,1,0:T(8,128)S(1)}, f32[8,128]{1,0:T(8,128)S(1)}) custom-call(f32[8,128]{1,0:T(8,128)S(1)} %get-tuple-element.130.refs_0_, bf16[4,2048,256]{2,1,0:T(8,128)(2,1)S(1)} %copy-done.1, bf16[4,2048,256]{2,1,0:T(8,128)(2,1)S(1)} %get-tuple-element.121.refs_1_.refs_2_, bf16[4,2048,256]{2,1,0:T(8,128)(2,1)S(1)} %copy-done.3, ...), custom_call_target="tpu_custom_call" | custom-call | flops 3000000000 | bytes 1000 | tf_op jit(solution)/shard_map/second_part/pallas_call | solution.py:80
  115.1 3.2 %second_part.21 = (f32[24,16,512]{2,1,0:T(8,128)S(1)}, f32[8,128]{1,0:T(8,128)S(1)}) custom-call(f32[8,128]{1,0:T(8,128)S(1)} %get-tuple-element.131.refs_0_, bf16[4,2048,256]{2,1,0:T(8,128)(2,1)S(1)} %copy-done.1, bf16[4,2048,256]{2,1,0:T(8,128)(2,1)S(1)} %get-tuple-element.121.refs_1_.refs_2_, bf16[4,2048,256]{2,1,0:T(8,128)(2,1)S(1)} %copy-done.3, ...), custom_call_target="tpu_custom_call" | custom-call | flops 3000000000 | bytes 1000 | tf_op jit(solution)/shard_map/second_part/pallas_call | solution.py:80
  121.5 4.8 %second_part.22 = (f32[32,16,512]{2,1,0:T(8,128)S(1)}, f32[8,128]{1,0:T(8,128)S(1)}) custom-call(f32[8,128]{1,0:T(8,128)S(1)} %get-tuple-element.133.refs_0_, bf16[4,2048,256]{2,1,0:T(8,128)(2,1)} %get-tuple-element.101.refs_1_, bf16[4,2048,256]{2,1,0:T(8,128)(2,1)S(1)} %copy-done.7, bf16[4,2048,256]{2,1,0:T(8,128)(2,1)} %get-tuple-element.102.refs_2_.refs_3_, ...), custom_call_target="tpu_custom_call" | custom-call | flops 3000000000 | bytes 1000 | tf_op jit(solution)/shard_map/second_part/pallas_call | solution.py:80
  126.3 3.5 %collective-permute-start.18 = (f32[32,16,512]{2,1,0:T(8,128)S(1)}, f32[32,16,512]{2,1,0:T(8,128)S(1)}, u32[]{:S(2)}, u32[]{:S(2)}) collective-permute-start(f32[32,16,512]{2,1,0:T(8,128)S(1)} %get-tuple-element.145), channel_id=1, source_target_pairs={{0,8},{8,16},{16,24},{1,9},{9,17},{17,25},{2,10},{10,18},{18,26},{... | collective-permute-start | bytes 3145736 | tf_op jit(solution)/shard_map/ppermute | solution.py:385
  129.8 2.7 %place.5 = (f32[64,16,512]{2,1,0:T(8,128)}, f32[8,128]{1,0:T(8,128)S(1)}) custom-call(s32[14]{0:T(128)S(1)} %copy-done.17, f32[8,128]{1,0:T(8,128)S(1)} %get-tuple-element.135.refs_1_, f32[32,16,512]{2,1,0:T(8,128)S(1)} %collective-permute-done.14.refs_2_, f32[64,16,512]{2,1,0:T(8,128)} %bitcast.33), custom_call_target="tpu_custom_call" | custom-call | flops 10000000000 | bytes 1000 | tf_op jit(solution)/shard_map/place/pallas_call | solution.py:80
  134.0 3.2 %second_part.23 = (f32[24,16,512]{2,1,0:T(8,128)S(1)}, f32[8,128]{1,0:T(8,128)S(1)}) custom-call(f32[8,128]{1,0:T(8,128)S(1)} %get-tuple-element.139.refs_0_, bf16[4,2048,256]{2,1,0:T(8,128)(2,1)S(1)} %copy-done.1, bf16[4,2048,256]{2,1,0:T(8,128)(2,1)S(1)} %get-tuple-element.121.refs_1_.refs_2_, bf16[4,2048,256]{2,1,0:T(8,128)(2,1)S(1)} %copy-done.3, ...), custom_call_target="tpu_custom_call" | custom-call | flops 3000000000 | bytes 1000 | tf_op jit(solution)/shard_map/second_part/pallas_call | solution.py:80
  141.6 9.4 %collective-permute-done.18.refs_2_ = f32[32,16,512]{2,1,0:T(8,128)S(1)} collective-permute-done((f32[32,16,512]{2,1,0:T(8,128)S(1)}, f32[32,16,512]{2,1,0:T(8,128)S(1)}, u32[]{:S(2)}, u32[]{:S(2)}) %collective-permute-start.18) | collective-permute-done | bytes 1048608 | tf_op jit(solution)/shard_map/ppermute | solution.py:385
  151.0 2.7 %place.8 = (f32[64,16,512]{2,1,0:T(8,128)}, f32[8,128]{1,0:T(8,128)S(1)}) custom-call(s32[14]{0:T(128)S(1)} %copy-done.17, f32[8,128]{1,0:T(8,128)S(1)} %get-tuple-element.144.refs_1_, f32[32,16,512]{2,1,0:T(8,128)S(1)} %collective-permute-done.18.refs_2_, f32[64,16,512]{2,1,0:T(8,128)} %bitcast.34, ...), custom_call_target="tpu_custom_call", output_to_operand_aliasing={{0}: (4, {})} | custom-call | flops 10000000000 | bytes 1000 | tf_op jit(solution)/shard_map/place/pallas_call | solution.py:80
  153.8 3.2 %collective-permute-done.19.refs_2_ = f32[24,16,512]{2,1,0:T(8,128)S(1)} collective-permute-done((f32[24,16,512]{2,1,0:T(8,128)S(1)}, f32[24,16,512]{2,1,0:T(8,128)S(1)}, u32[]{:S(2)}, u32[]{:S(2)}) %collective-permute-start.19) | collective-permute-done | bytes 786464 | tf_op jit(solution)/shard_map/ppermute | solution.py:385
  (121 shorter events, 42.9 us)
Async XLA Ops:
  0.6 9.9 %collective-permute-start = (f32[64,16,512]{2,1,0:T(8,128)}, f32[64,16,512]{2,1,0:T(8,128)}, u32[]{:S(2)}, u32[]{:S(2)}) collective-permute-start(f32[64,16,512]{2,1,0:T(8,128)} %bitcast.30), channel_id=1, source_target_pairs={{0,1},{1,0},{2,3},{3,2},{4,5},{5,4},{6,7},{7,6},{8,9},{9,8},{10,11... | collective-permute-start | bytes 6291464 | tf_op jit(solution)/shard_map/ppermute | solution.py:382
  1.2 9.4 %collective-permute-start.1 = (f32[64,16,512]{2,1,0:T(8,128)}, f32[64,16,512]{2,1,0:T(8,128)S(1)}, u32[]{:S(2)}, u32[]{:S(2)}) collective-permute-start(f32[64,16,512]{2,1,0:T(8,128)} %bitcast.35), channel_id=1, source_target_pairs={{0,1},{1,0},{2,3},{3,2},{4,5},{5,4},{6,7},{7,6},{8,9},{9,8},{10,11... | collective-permute-start | bytes 6291464 | tf_op jit(solution)/shard_map/ppermute | solution.py:382
  4.6 27.1 %collective-permute-start.2 = (f32[16,64,256]{2,1,0:T(8,128)}, f32[16,64,256]{2,1,0:T(8,128)}, u32[]{:S(2)}, u32[]{:S(2)}) collective-permute-start(f32[16,64,256]{2,1,0:T(8,128)} %get-tuple-element.85.refs_1_), channel_id=1, source_target_pairs={{0,2},{1,3},{2,0},{3,1},{4,6},{5,7},{6,4},{7,5},{8,10},{9,11},{10,... | collective-permute-start | bytes 3145736 | tf_op jit(solution)/shard_map/ppermute | solution.py:382
  7.5 26.4 %collective-permute-start.3 = (f32[16,64,256]{2,1,0:T(8,128)}, f32[16,64,256]{2,1,0:T(8,128)}, u32[]{:S(2)}, u32[]{:S(2)}) collective-permute-start(f32[16,64,256]{2,1,0:T(8,128)} %get-tuple-element.87.refs_1_), channel_id=1, source_target_pairs={{0,4},{1,5},{2,6},{3,7},{4,0},{5,1},{6,2},{7,3},{8,12},{9,13},{10,... | collective-permute-start | bytes 3145736 | tf_op jit(solution)/shard_map/ppermute | solution.py:382
  14.8 29.9 %copy-start.18 = (bf16[256,256]{1,0:T(8,128)(2,1)}, bf16[256,256]{1,0:T(8,128)(2,1)S(1)}, u32[]{:S(2)}) copy-start(bf16[256,256]{1,0:T(8,128)(2,1)S(1)} %get-tuple-element.97.refs_7_) | copy-start | bytes 393220
  21.1 32.8 %collective-permute-start.6 = (f32[16,64,256]{2,1,0:T(8,128)}, f32[16,64,256]{2,1,0:T(8,128)}, u32[]{:S(2)}, u32[]{:S(2)}) collective-permute-start(f32[16,64,256]{2,1,0:T(8,128)} %get-tuple-element.99.refs_1_), channel_id=1, source_target_pairs={{0,2},{1,3},{2,0},{3,1},{4,6},{5,7},{6,4},{7,5},{8,10},{9,11},{10,... | collective-permute-start | bytes 3145736 | tf_op jit(solution)/shard_map/ppermute | solution.py:382
  21.6 36.6 %collective-permute-start.7 = (f32[16,64,256]{2,1,0:T(8,128)}, f32[16,64,256]{2,1,0:T(8,128)}, u32[]{:S(2)}, u32[]{:S(2)}) collective-permute-start(f32[16,64,256]{2,1,0:T(8,128)} %get-tuple-element.106.refs_1_), channel_id=1, source_target_pairs={{0,4},{1,5},{2,6},{3,7},{4,0},{5,1},{6,2},{7,3},{8,12},{9,13},{10,... | collective-permute-start | bytes 3145736 | tf_op jit(solution)/shard_map/ppermute | solution.py:382
  25.1 29.0 %copy-start.8 = (bf16[4,512,512]{2,1,0:T(8,128)(2,1)}, bf16[4,512,512]{2,1,0:T(8,128)(2,1)S(1)}, u32[]{:S(2)}) copy-start(bf16[4,512,512]{2,1,0:T(8,128)(2,1)S(1)} %get-tuple-element.103.refs_3_.refs_5_) | copy-start | bytes 6291460
  25.1 29.0 %copy-start.11 = (bf16[4,512,512]{2,1,0:T(8,128)(2,1)}, bf16[4,512,512]{2,1,0:T(8,128)(2,1)S(1)}, u32[]{:S(2)}) copy-start(bf16[4,512,512]{2,1,0:T(8,128)(2,1)S(1)} %get-tuple-element.104.refs_4_.refs_6_) | copy-start | bytes 6291460
  27.3 31.4 %copy-start.4 = (bf16[4,512,512]{2,1,0:T(8,128)(2,1)}, bf16[4,512,512]{2,1,0:T(8,128)(2,1)S(1)}, u32[]{:S(2)}) copy-start(bf16[4,512,512]{2,1,0:T(8,128)(2,1)S(1)} %get-tuple-element.110.refs_3_.refs_5_) | copy-start | bytes 6291460
  31.7 2.9 %collective-permute-start.4 = (f32[16,64,256]{2,1,0:T(8,128)}, f32[16,64,256]{2,1,0:T(8,128)S(1)}, u32[]{:S(2)}, u32[]{:S(2)}) collective-permute-start(f32[16,64,256]{2,1,0:T(8,128)} %get-tuple-element.89.refs_3_), channel_id=1, source_target_pairs={{0,1},{1,0},{2,3},{3,2},{4,5},{5,4},{6,7},{7,6},{8,9},{9,8},{10,11... | collective-permute-start | bytes 3145736 | tf_op jit(solution)/shard_map/ppermute | solution.py:382
  33.8 10.9 %collective-permute-start.5 = (f32[16,64,256]{2,1,0:T(8,128)}, f32[16,64,256]{2,1,0:T(8,128)}, u32[]{:S(2)}, u32[]{:S(2)}) collective-permute-start(f32[16,64,256]{2,1,0:T(8,128)} %get-tuple-element.94.refs_3_), channel_id=1, source_target_pairs={{0,1},{1,0},{2,3},{3,2},{4,5},{5,4},{6,7},{7,6},{8,9},{9,8},{10,11... | collective-permute-start | bytes 3145736 | tf_op jit(solution)/shard_map/ppermute | solution.py:382
  53.9 5.7 %collective-permute-start.8 = (f32[16,64,256]{2,1,0:T(8,128)}, f32[16,64,256]{2,1,0:T(8,128)S(1)}, u32[]{:S(2)}, u32[]{:S(2)}) collective-permute-start(f32[16,64,256]{2,1,0:T(8,128)} %get-tuple-element.113.refs_3_), channel_id=1, source_target_pairs={{0,1},{1,0},{2,3},{3,2},{4,5},{5,4},{6,7},{7,6},{8,9},{9,8},{10,11... | collective-permute-start | bytes 3145736 | tf_op jit(solution)/shard_map/ppermute | solution.py:382
  58.2 16.0 %collective-permute-start.9 = (f32[16,64,256]{2,1,0:T(8,128)}, f32[16,64,256]{2,1,0:T(8,128)}, u32[]{:S(2)}, u32[]{:S(2)}) collective-permute-start(f32[16,64,256]{2,1,0:T(8,128)} %get-tuple-element.119.refs_3_), channel_id=1, source_target_pairs={{0,1},{1,0},{2,3},{3,2},{4,5},{5,4},{6,7},{7,6},{8,9},{9,8},{10,11... | collective-permute-start | bytes 3145736 | tf_op jit(solution)/shard_map/ppermute | solution.py:382
  72.1 25.9 %collective-permute-start.10 = (f32[32,16,512]{2,1,0:T(8,128)}, f32[32,16,512]{2,1,0:T(8,128)}, u32[]{:S(2)}, u32[]{:S(2)}) collective-permute-start(f32[32,16,512]{2,1,0:T(8,128)} %get-tuple-element.127), channel_id=1, source_target_pairs={{0,4},{1,5},{2,6},{3,7},{4,0},{5,1},{6,2},{7,3},{8,12},{9,13},{10,... | collective-permute-start | bytes 3145736 | tf_op jit(solution)/shard_map/ppermute | solution.py:382
  84.4 22.3 %collective-permute-start.11 = (f32[16,16,512]{2,1,0:T(8,128)S(1)}, f32[16,16,512]{2,1,0:T(8,128)S(1)}, u32[]{:S(2)}, u32[]{:S(2)}) collective-permute-start(f32[16,16,512]{2,1,0:T(8,128)S(1)} %get-tuple-element.129), channel_id=1, source_target_pairs={{0,2},{1,3},{2,0},{3,1},{4,6},{5,7},{6,4},{7,5},{8,10},{9,11},{10,... | collective-permute-start | bytes 1572872 | tf_op jit(solution)/shard_map/ppermute | solution.py:382
  95.3 19.8 %collective-permute-start.12 = (f32[24,16,512]{2,1,0:T(8,128)S(1)}, f32[24,16,512]{2,1,0:T(8,128)S(1)}, u32[]{:S(2)}, u32[]{:S(2)}) collective-permute-start(f32[24,16,512]{2,1,0:T(8,128)S(1)} %get-tuple-element.132), channel_id=1, source_target_pairs={{0,2},{1,3},{2,0},{3,1},{4,6},{5,7},{6,4},{7,5},{8,10},{9,11},{10,... | collective-permute-start | bytes 2359304 | tf_op jit(solution)/shard_map/ppermute | solution.py:382
  96.8 24.6 %collective-permute-start.13 = (f32[32,16,512]{2,1,0:T(8,128)S(1)}, f32[32,16,512]{2,1,0:T(8,128)S(1)}, u32[]{:S(2)}, u32[]{:S(2)}) collective-permute-start(f32[32,16,512]{2,1,0:T(8,128)S(1)} %get-tuple-element.134), channel_id=1, source_target_pairs={{0,4},{1,5},{2,6},{3,7},{4,0},{5,1},{6,2},{7,3},{8,12},{9,13},{10,... | collective-permute-start | bytes 3145736 | tf_op jit(solution)/shard_map/ppermute | solution.py:382
  103.0 26.8 %collective-permute-start.14 = (f32[32,16,512]{2,1,0:T(8,128)S(1)}, f32[32,16,512]{2,1,0:T(8,128)S(1)}, u32[]{:S(2)}, u32[]{:S(2)}) collective-permute-start(f32[32,16,512]{2,1,0:T(8,128)S(1)} %get-tuple-element.136), channel_id=1, source_target_pairs={{0,8},{8,16},{16,24},{1,9},{9,17},{17,25},{2,10},{10,18},{18,26},{... | collective-permute-start | bytes 3145736 | tf_op jit(solution)/shard_map/ppermute | solution.py:385
  108.6 24.0 %collective-permute-start.15 = (f32[16,16,512]{2,1,0:T(8,128)S(1)}, f32[16,16,512]{2,1,0:T(8,128)S(1)}, u32[]{:S(2)}, u32[]{:S(2)}) collective-permute-start(f32[16,16,512]{2,1,0:T(8,128)S(1)} %get-tuple-element.138), channel_id=1, source_target_pairs={{8,0},{16,8},{24,16},{9,1},{17,9},{25,17},{10,2},{18,10},{26,18},{... | collective-permute-start | bytes 1572872 | tf_op jit(solution)/shard_map/ppermute | solution.py:385
  113.3 20.7 %collective-permute-start.16 = (f32[24,16,512]{2,1,0:T(8,128)S(1)}, f32[24,16,512]{2,1,0:T(8,128)S(1)}, u32[]{:S(2)}, u32[]{:S(2)}) collective-permute-start(f32[24,16,512]{2,1,0:T(8,128)S(1)} %get-tuple-element.140), channel_id=1, source_target_pairs={{0,2},{1,3},{2,0},{3,1},{4,6},{5,7},{6,4},{7,5},{8,10},{9,11},{10,... | collective-permute-start | bytes 2359304 | tf_op jit(solution)/shard_map/ppermute | solution.py:382
  118.3 21.8 %collective-permute-start.17 = (f32[24,16,512]{2,1,0:T(8,128)S(1)}, f32[24,16,512]{2,1,0:T(8,128)S(1)}, u32[]{:S(2)}, u32[]{:S(2)}) collective-permute-start(f32[24,16,512]{2,1,0:T(8,128)S(1)} %get-tuple-element.142), channel_id=1, source_target_pairs={{8,0},{16,8},{24,16},{9,1},{17,9},{25,17},{10,2},{18,10},{26,18},{... | collective-permute-start | bytes 2359304 | tf_op jit(solution)/shard_map/ppermute | solution.py:385
  126.3 24.7 %collective-permute-start.18 = (f32[32,16,512]{2,1,0:T(8,128)S(1)}, f32[32,16,512]{2,1,0:T(8,128)S(1)}, u32[]{:S(2)}, u32[]{:S(2)}) collective-permute-start(f32[32,16,512]{2,1,0:T(8,128)S(1)} %get-tuple-element.145), channel_id=1, source_target_pairs={{0,8},{8,16},{16,24},{1,9},{9,17},{17,25},{2,10},{10,18},{18,26},{... | collective-permute-start | bytes 3145736 | tf_op jit(solution)/shard_map/ppermute | solution.py:385
  137.2 19.8 %collective-permute-start.19 = (f32[24,16,512]{2,1,0:T(8,128)S(1)}, f32[24,16,512]{2,1,0:T(8,128)S(1)}, u32[]{:S(2)}, u32[]{:S(2)}) collective-permute-start(f32[24,16,512]{2,1,0:T(8,128)S(1)} %get-tuple-element.149), channel_id=1, source_target_pairs={{8,0},{16,8},{24,16},{9,1},{17,9},{25,17},{10,2},{18,10},{26,18},{... | collective-permute-start | bytes 2359304 | tf_op jit(solution)/shard_map/ppermute | solution.py:385
  (29 other events, 234.9 us)
